TPU v7x, 128 devices: a whole 4x4x4 slice. The times are simulated.
128 devices in a mesh: rep: 4 (over z_lo, core), fsdp: 32 (over z_hi, x, y).
Axes of the slice: x: 4, y: 4, z: 4 (z_hi: 2, z_lo: 2; z = z_hi * 2 + z_lo), core: 2. Of those that a mesh axis runs over, the one named last changes fastest.
Arguments:
- tokens: bfloat16 [8192, 8192], P('fsdp'), as said below
- query_ckpt: float32 [4, 8192, 1024], P('rep', 'fsdp'), as said below
- key_value_ckpt: float32 [4, 8192, 256], P('rep', 'fsdp'), as said below
- numerators: int32 [4], replicated, may hold values from 1 to 8
Outputs:
- context: bfloat16 [8192, 1024], P('fsdp')
Inputs may be any that keep to these rules, and one draw needn't show every extreme that they name: `tokens`: hidden states of mixed scales. `query_ckpt`: checkpoint weights. `key_value_ckpt`: checkpoint weights.
All inputs are finite; a program needn't handle non-finite values.
Results may differ from a plain program's by a relative error of at most 0.0081.
Values may be sent and summed in bfloat16 or wider, within the bound.
No kernel may reach another device: no remote copies, remote signals or barrier semaphores. Data moves between devices by JAX's collectives and lax.ppermute only.
A program may use at most 128 MiB of HBM per device.

v0:
```python
import math

import jax
import jax.numpy as jnp
from jax import lax
from jax.sharding import PartitionSpec as P

theta_base = 500000.0
eps_norm = 1e-05
masked_score = -1e30


def rms_normed(hidden):
    wide_copy = hidden.astype(jnp.float32)
    return (
        wide_copy * lax.rsqrt(jnp.mean(wide_copy * wide_copy, axis=-1, keepdims=True) + eps_norm)
    ).astype(jnp.bfloat16)


def rotary(values, positions):
    half_size = values.shape[-1] // 2
    inverse_freq = jnp.exp(
        -(jnp.arange(half_size, dtype=jnp.float32) * (2.0 / values.shape[-1]))
        * math.log(theta_base)
    )
    angles = positions.astype(jnp.float32)[:, None] * inverse_freq[None, :]
    cosine_table = jnp.cos(angles)[:, None, :]
    sine_table = jnp.sin(angles)[:, None, :]
    first_half = values[..., :half_size]
    second_half = values[..., half_size:]
    return jnp.concatenate(
        [
            first_half * cosine_table - second_half * sine_table,
            second_half * cosine_table + first_half * sine_table,
        ],
        axis=-1,
    )


def attend_heads(queries, pair_rows, query_pos, key_pos):
    head_size = queries.shape[-1]
    key_rows = pair_rows[:, :head_size]
    value_rows = pair_rows[:, head_size:]
    score_scale = 1.0 / math.sqrt(head_size)
    allowed = key_pos[None, :] <= query_pos[:, None]

    def one_head(query_head):
        scores = jnp.dot(query_head, key_rows.T, preferred_element_type=jnp.float32) * score_scale
        scores = jnp.where(allowed, scores, masked_score)
        row_top = jnp.max(scores, axis=1, keepdims=True)
        weights_exp = jnp.exp(scores - row_top)
        norm_sum = jnp.sum(weights_exp, axis=1, keepdims=True)
        mixed_out = (
            jnp.dot(
                weights_exp.astype(jnp.bfloat16), value_rows, preferred_element_type=jnp.float32
            )
            / norm_sum
        )
        return mixed_out.astype(jnp.bfloat16)

    head_outs = lax.map(one_head, jnp.transpose(queries, (1, 0, 2)))
    return jnp.transpose(head_outs, (1, 0, 2)).reshape(queries.shape[0], -1)


def local(tokens, query_ckpt, key_value_ckpt, numerators):
    fsdp_count = lax.axis_size("fsdp")
    rep_idx = lax.axis_index("rep")
    fsdp_idx = lax.axis_index("fsdp")
    slot_ids = jnp.arange(numerators.shape[0], dtype=jnp.int32)
    weight_sum = jnp.sum(numerators).astype(jnp.float32)
    my_share = (
        jnp.sum(jnp.where(slot_ids == rep_idx, numerators, 0)).astype(jnp.float32) / weight_sum
    )
    query_term = my_share * query_ckpt[0]
    pair_term = my_share * key_value_ckpt[0]
    tok_dev = tokens.shape[0]
    seq_length = tok_dev * fsdp_count
    offset = fsdp_idx * tok_dev
    normed = rms_normed(tokens)
    query_width = query_ckpt.shape[2]
    pair_width = key_value_ckpt.shape[2]
    query_sum, pair_sum = lax.psum((query_term, pair_term), "rep")
    query_rows = query_sum.astype(jnp.bfloat16)
    pair_rows = pair_sum.astype(jnp.bfloat16)
    queries = jnp.dot(
        normed,
        lax.all_gather(query_rows, "fsdp", axis=0, tiled=True),
        preferred_element_type=jnp.float32,
    )
    pair_proj = jnp.dot(
        normed,
        lax.all_gather(pair_rows, "fsdp", axis=0, tiled=True),
        preferred_element_type=jnp.float32,
    )
    positions = (offset + jnp.arange(tok_dev, dtype=jnp.int32)) % seq_length
    head_size = pair_width // 2
    query_rot = rotary(
        queries.reshape(tok_dev, query_width // head_size, head_size), positions
    ).astype(jnp.bfloat16)
    key_rot = rotary(pair_proj[:, None, :head_size], positions)[:, 0, :].astype(jnp.bfloat16)
    pair_local = jnp.concatenate([key_rot, pair_proj[:, head_size:].astype(jnp.bfloat16)], axis=1)
    pair_all = lax.all_gather(pair_local, "fsdp", axis=0, tiled=True)
    key_pos = jnp.arange(seq_length, dtype=jnp.int32)
    context = attend_heads(query_rot, pair_all, positions, key_pos)
    return context


def solution(mesh):
    in_specs = (P("fsdp", None), P("rep", "fsdp", None), P("rep", "fsdp", None), P())
    out_specs = P("fsdp", None)
    return jax.shard_map(local, mesh=mesh, in_specs=in_specs, out_specs=out_specs, check_vma=False)
```

profile of v0, /device:TPU:1, one launch (start us, length us, event | category | flops | bytes accessed | tf_op | source)
XLA Modules:
  0.0 448.5 jit_solution(5793324266639311685)
XLA Ops:
  6.5 0.0 all-gather.6.cloned.1.call-start
  6.5 1.3 fusion.43
  9.1 1.3 multiply_bitcast_fusion
  10.4 1.0 multiply_bitcast_fusion.1
  11.4 30.6 %all-reduce.2 = (bf16[256,1024]{1,0:T(8,128)(2,1)}, bf16[256,256]{1,0:T(8,128)(2,1)}) all-reduce(f32[256,1024]{1,0:T(8,128)S(1)} %multiply_bitcast_fusion, f32[256,256]{1,0:T(8,128)S(1)} %multiply_bitcast_fusion.1), channel_id=1, replica_groups=mesh['rep'=4,'fsdp'=32] {'rep'}, use_global_device_ids=true, to_apply=%region_3.4 | all-reduce | flops 327680 | bytes 1966080 | tf_op jit(solution)/shard_map/psum | solution.py:82
  41.9 0.0 all-gather.6.cloned.1.call-update
  42.0 0.0 all-gather.8.cloned.1.call-start
  42.0 3.1 fusion.23
  45.2 79.4 %all-gather.6.cloned.1.call-done = bf16[8192,256]{1,0:T(8,128)(2,1)} async-done(((bf16[256,256]{1,0:T(8,128)(2,1)}), bf16[8192,256]{1,0:T(8,128)(2,1)}) %all-gather.6.cloned.1.call-update) | async-done | bytes 4194320 | tf_op jit(solution)/shard_map/all_gather | solution.py:92
  124.6 5.4 %fusion.25 = f32[256,256]{0,1:T(8,128)S(1)} fusion(bf16[8192,256]{1,0:T(8,128)(2,1)} %all-gather.6.cloned.1.call-done, bf16[256,8192]{1,0:T(8,128)(2,1)} %param.6, f32[256]{0:T(256)S(1)} %add_rsqrt_fusion), kind=kOutput, calls=%fused_computation.20 | convolution fusion | flops 1080033280 | bytes 8651776 | tf_op jit(solution)/shard_map/dot_general | solution.py:90
  130.0 0.3 fusion.37
  130.3 0.7 pad_maximum_fusion
  131.0 0.0 all-gather.8.cloned.1.call-update
  131.0 0.2 all-gather.4.cloned.1.call-start
  131.3 0.5 all-gather.4.cloned.1.call-update
  131.8 0.5 multiply_cosine_fusion
  132.3 91.1 %all-gather.8.cloned.1.call-done = bf16[8192,256]{0,1:T(8,128)(2,1)} async-done(((bf16[256,256]{0,1:T(8,128)(2,1)}), bf16[8192,256]{0,1:T(8,128)(2,1)}) %all-gather.8.cloned.1.call-update) | async-done | bytes 4194320 | tf_op jit(solution)/shard_map/all_gather | solution.py:102
  223.4 3.9 fusion.45
  227.3 2.5 copy.7
  229.8 3.2 copy.8
  233.0 147.3 %all-gather.4.cloned.1.call-done = bf16[8192,1024]{1,0:T(8,128)(2,1)} async-done(((bf16[256,1024]{1,0:T(8,128)(2,1)}), bf16[8192,1024]{1,0:T(8,128)(2,1)}) %all-gather.4.cloned.1.call-update) | async-done | bytes 16777232 | tf_op jit(solution)/shard_map/all_gather | solution.py:87
  380.3 9.4 %fusion.29 = f32[32,8,8,128]{3,1,2,0:T(8,128)S(1)} fusion(bf16[8192,1024]{1,0:T(8,128)(2,1)} %all-gather.4.cloned.1.call-done, bf16[256,8192]{1,0:T(8,128)(2,1)} %param.6, f32[256]{0:T(256)S(1)} %add_rsqrt_fusion), kind=kOutput, calls=%fused_computation.22 | convolution fusion | flops 4301258752 | bytes 22021120 | tf_op jit(solution)/shard_map/dot_general | solution.py:85
  389.7 0.2 copy.13
  389.9 0.3 fusion.46
  390.3 0.4 subtract_convert_fusion
  390.7 0.3 maximum_bitcast_fusion
  391.0 50.1 %while.11 = (s32[]{:T(128)}, bf16[8,256,128]{2,1,0:T(8,128)(2,1)S(1)}, bf16[8,256,128]{2,1,0:T(8,128)(2,1)S(1)}, bf16[8192,128]{1,0:T(8,128)(2,1)}, bf16[8192,12...) while((s32[]{:T(128)}, bf16[8,256,128]{2,1,0:T(8,128)(2,1)S(1)}, ...), condition=%wide.region_8.9_spmd.clone, body=%wide.region_5.8_spmd.clone.sunk | while | flops 1090584064 | bytes 29497428 | solution.py:61
  391.0 3.3 fusion.61
  394.3 1.4 fusion.62
  395.7 1.6 fusion.63
  397.3 3.3 fusion.61
  400.6 1.4 fusion.62
  401.9 1.6 fusion.63
  403.5 3.3 fusion.61
  406.8 1.4 fusion.62
  408.2 1.6 fusion.63
  409.8 3.3 fusion.61
  413.1 1.4 fusion.62
  414.5 1.6 fusion.63
  416.1 3.3 fusion.61
  419.4 1.4 fusion.62
  420.7 1.6 fusion.63
  422.3 3.3 fusion.61
  425.6 1.4 fusion.62
  427.0 1.6 fusion.63
  428.6 3.3 fusion.61
  431.9 1.4 fusion.62
  433.3 1.6 fusion.63
  434.9 3.3 fusion.61
  438.2 1.4 fusion.62
  439.5 1.6 fusion.63
  441.1 0.9 copy_bitcast_fusion
  (8 shorter events, 0.1 us)
Async XLA Ops:
  6.5 118.0 %all-gather.6.cloned.1.call-start = ((), (), s32[]{:S(2)}) async-start(), calls=%async_computation.1 | async-start | bytes 4325376 | tf_op jit(solution)/shard_map/all_gather | solution.py:92
  42.0 181.5 %all-gather.8.cloned.1.call-start = ((), (), s32[]{:S(2)}) async-start(), calls=%async_computation.2 | async-start | bytes 4325376 | tf_op jit(solution)/shard_map/all_gather | solution.py:102
  131.0 249.3 %all-gather.4.cloned.1.call-start = ((), (), s32[]{:S(2)}) async-start(), calls=%async_computation | async-start | bytes 17301504 | tf_op jit(solution)/shard_map/all_gather | solution.py:87
Sparse Core Ops, SparseCore 0:
  42.1 82.4 all-gather.5
  131.2 92.2 all-gather.7
  226.5 153.7 all-gather.3
where the time goes:
time: 449 us
  waiting for transfers between devices  318 us (71%)
  matrix products  53.9 us (12%)
  blocking collectives  30.6 us (7%)
  other arithmetic  19.8 us (4%)
  between operations  14.5 us (3%)
  local copies, waits for them, and re-layouts  11 us (2%)
    all_gather x1, waiting for transfers between devices, local(): lax.all_gather(query_rows, 'fsdp', axis=0, tiled=True)  147 us
    all_gather x1, waiting for transfers between devices, local(): pair_all = lax.all_gather(pair_local, 'fsdp', axis=0, tiled=True)  91.1 us
    all_gather x1, waiting for transfers between devices, local(): lax.all_gather(pair_rows, 'fsdp', axis=0, tiled=True)  79.4 us
    psum x1, blocking collectives, local(): query_sum, pair_sum = lax.psum((query_term, pair_term), 'rep')  30.6 us
    dot_general x8, matrix products, one_head(): jnp.dot(query_head, key_rows.T, preferred_element_type=jnp.float32)  26.4 us
    dot_general x8, matrix products, one_head(): jnp.dot(weights_exp.astype(jnp.bfloat16), value_rows, preferred_element_t...  12.7 us
    reduce_sum x8, other arithmetic, one_head(): norm_sum = jnp.sum(weights_exp, axis=1, keepdims=True)  10.9 us
    dot_general x1, matrix products, local(): jnp.dot(normed, lax.all_gather(query_rows, 'fsdp', axis=0, tiled=True), p...  9.4 us
  transfers between devices with their start and end apart: 3, of which 3 were waited for; matrix products, arithmetic and copies ran while one was open for 3% of the time, Pallas kernels for 0%

commit v1 on v0

v1 whole, which is shorter than its diff:
```python
import functools
import math

import jax
import jax.numpy as jnp
import numpy as np
from jax import lax
from jax.experimental import pallas as pl
from jax.experimental.pallas import tpu as pltpu
from jax.sharding import Mesh, PartitionSpec as P

theta_base = 500000.0
eps_norm = 1e-05
masked_score = -1e30
HEAD = 128
F32 = jnp.float32
BF16 = jnp.bfloat16
VMEM = pltpu.VMEM
SMEM = pltpu.SMEM
NT = (((1,), (1,)), ((), ()))
SWAP = [(0, 1), (1, 0)]


def params(mib=56):
    return pltpu.CompilerParams(vmem_limit_bytes=mib * 1024 * 1024)


def cost(flops, nbytes, trans=0):
    return pl.CostEstimate(flops=flops, bytes_accessed=nbytes, transcendentals=trans)


def vspec():
    return pl.BlockSpec(memory_space=VMEM)


def sspec():
    return pl.BlockSpec(memory_space=SMEM)


def pair_order():
    order = []
    for r in range(4):
        order += list(range(16 * r, 16 * r + 16))
        order += list(range(64 + 16 * r, 64 + 16 * r + 16))
        order += list(range(128 + 32 * r, 128 + 32 * r + 32))
    return order


def norm_kernel(idx, x_ref, own_ref, send_ref):
    zh, c = idx[0], idx[1]
    x = x_ref[...].astype(F32)
    scale = lax.rsqrt(jnp.mean(x * x, axis=-1, keepdims=True) + eps_norm)
    half = own_ref.shape[1]
    quarter = send_ref.shape[1]
    own = x_ref[:, pl.ds(pl.multiple_of(zh * half, half), half)].astype(F32)
    own_ref[...] = (own * scale).astype(BF16)
    start = pl.multiple_of((1 - zh) * half + c * quarter, quarter)
    send = x_ref[:, pl.ds(start, quarter)].astype(F32)
    send_ref[...] = (send * scale).astype(BF16)


def normalise(idx, tokens):
    rows, width = tokens.shape
    step = 32
    return pl.pallas_call(
        norm_kernel,
        grid=(rows // step,),
        in_specs=[sspec(), pl.BlockSpec((step, width), lambda i: (i, 0))],
        out_specs=[
            pl.BlockSpec((step, width // 2), lambda i: (i, 0)),
            pl.BlockSpec((step, width // 4), lambda i: (i, 0)),
        ],
        out_shape=[
            jax.ShapeDtypeStruct((rows, width // 2), BF16),
            jax.ShapeDtypeStruct((rows, width // 4), BF16),
        ],
        compiler_params=params(),
        cost_estimate=cost(rows * width * 4, rows * width * 4),
        name="normalise",
    )(idx, tokens)


def prep_kernel(idx, share, q_ref, kv_ref, perm_ref, send_ref, keep_ref):
    c = idx[1]
    s = share[0]
    kvt = lax.dot_general(
        perm_ref[...], kv_ref[...] * s, NT, precision=lax.Precision.HIGHEST,
        preferred_element_type=F32,
    )
    for zl in range(2):
        for cc in range(2):
            col = (zl * 2 + cc) * 256
            row = (zl * 2 + cc) * 64

            @pl.when(cc == c)
            def _():
                keep_ref[zl, 0:256] = q_ref[:, col:col + 256] * s
                keep_ref[zl, 256:320] = kvt[row:row + 64]

            @pl.when(cc != c)
            def _():
                send_ref[zl, 0:256] = q_ref[:, col:col + 256] * s
                send_ref[zl, 256:320] = kvt[row:row + 64]


def prepare(idx, share, q, kv, perm):
    shape = jax.ShapeDtypeStruct((2, 320, 256), F32)
    return pl.pallas_call(
        prep_kernel,
        in_specs=[sspec(), sspec(), vspec(), vspec(), vspec()],
        out_specs=[vspec(), vspec()],
        out_shape=[shape, shape],
        compiler_params=params(),
        cost_estimate=cost(256 * 256 * 256 * 12, 3 << 20),
        name="prepare",
    )(idx, share, q, kv, perm)


def kv_kernel(w_ref, *refs):
    xs, out_ref = refs[:-1], refs[-1]
    blocks = w_ref.shape[0]
    per = blocks // len(xs)
    acc = jnp.zeros(out_ref.shape, F32)
    for i, x_ref in enumerate(xs):
        for j in range(per):
            acc += lax.dot_general(
                w_ref[i * per + j], x_ref[:, j * 256:(j + 1) * 256], NT,
                preferred_element_type=F32,
            )
    out_ref[...] = acc.astype(out_ref.dtype)


def q_kernel(w_ref, *refs):
    xs, out_ref = refs[:-1], refs[-1]
    blocks = w_ref.shape[0]
    per = blocks // len(xs)
    acc = jnp.zeros(out_ref.shape, F32)
    for i, x_ref in enumerate(xs):
        for j in range(per):
            acc += jnp.dot(
                x_ref[:, j * 256:(j + 1) * 256], w_ref[i * per + j],
                preferred_element_type=F32,
            )
    out_ref[...] = acc.astype(out_ref.dtype)


def project(kernel, w, xs, shape, dtype, name):
    return pl.pallas_call(
        kernel,
        in_specs=[vspec()] * (1 + len(xs)),
        out_specs=vspec(),
        out_shape=jax.ShapeDtypeStruct(shape, dtype),
        compiler_params=params(),
        cost_estimate=cost(2 * shape[0] * shape[1] * 4096, 4 << 20),
        name=name,
    )(w, *xs)


def kv_finish_kernel(own_ref, got_ref, cos_ref, sin_ref, out_ref):
    t = own_ref[...] + got_ref[...]
    u, w = t[0:16], t[16:32]
    cos, sin = cos_ref[...], sin_ref[...]
    lo = (u * cos - w * sin).astype(BF16)
    hi = (w * cos + u * sin).astype(BF16)
    v = t[32:64].astype(BF16)
    for h in range(2):
        cols = slice(h * 128, (h + 1) * 128)
        out_ref[h, 0:16] = lo[:, cols]
        out_ref[h, 16:32] = hi[:, cols]
        out_ref[h, 32:64] = v[:, cols]


def q_finish_kernel(own_ref, got_ref, cos_ref, sin_ref, out_ref):
    t = own_ref[...] + got_ref[...].astype(F32)
    cos, sin = cos_ref[...], sin_ref[...]
    for h in range(2):
        u = t[:, h * 128:h * 128 + 64]
        w = t[:, h * 128 + 64:h * 128 + 128]
        out_ref[h] = jnp.concatenate([u * cos - w * sin, w * cos + u * sin], axis=1).astype(BF16)


def finish(kernel, args, shape, name):
    return pl.pallas_call(
        kernel,
        in_specs=[vspec()] * len(args),
        out_specs=vspec(),
        out_shape=jax.ShapeDtypeStruct(shape, BF16),
        compiler_params=params(),
        cost_estimate=cost(1 << 18, 1 << 19),
        name=name,
    )(*args)


CHUNK = 4
EXP_SCALE = math.log2(math.e) / math.sqrt(HEAD)


def attend_kernel(idx, qa_ref, qb_ref, kv_ref, oa_ref, ob_ref):
    f, c = idx[2], idx[1]
    last = f // CHUNK

    def load(j):
        kt, vt = [], []
        for b in range(CHUNK):
            blk = kv_ref.at[j * CHUNK + b]
            kt.append(jnp.concatenate(
                [blk[r, 0:16] for r in range(4)] + [blk[r, 16:32] for r in range(4)], axis=0))
            vt.append(jnp.concatenate([blk[r, 32:64] for r in range(4)], axis=0))
        return jnp.concatenate(kt, axis=1), jnp.concatenate(vt, axis=1)

    def step(q, j, carry, masked):
        m, l, acc = carry
        kt, vt = load(j)
        s = jnp.dot(q, kt, preferred_element_type=F32)
        if masked:
            row = lax.broadcasted_iota(jnp.int32, s.shape, 0) + f * 256
            col = lax.broadcasted_iota(jnp.int32, s.shape, 1)
            pos = (j * CHUNK + col // 128) * 256 + c * 128 + col % 128
            s = jnp.where(pos <= row, s, masked_score)
        top = jnp.maximum(m, jnp.max(s, axis=1, keepdims=True))
        p = jnp.exp2((s - top) * EXP_SCALE)
        fix = jnp.exp2((m - top) * EXP_SCALE)
        psum = p[:, 0:128]
        for b in range(1, CHUNK):
            psum = psum + p[:, b * 128:(b + 1) * 128]
        l = l * fix + psum
        acc = acc * fix + lax.dot_general(p.astype(BF16), vt, NT, preferred_element_type=F32)
        return top, l, acc

    for q_ref, o_ref in ((qa_ref, oa_ref), (qb_ref, ob_ref)):
        for h in range(2):
            q = q_ref[h]
            carry = (
                jnp.full((256, 1), masked_score, F32),
                jnp.zeros((256, 128), F32),
                jnp.zeros((256, 128), F32),
            )
            carry = lax.fori_loop(0, last, lambda j, s: step(q, j, s, False), carry)
            m, l, acc = step(q, last, carry, True)
            o_ref[0, h * 256:(h + 1) * 256] = acc
            o_ref[1, h * 256:(h + 1) * 256] = jnp.broadcast_to(m, (256, 128))
            o_ref[2, h * 256:(h + 1) * 256] = l


def attend(idx, qa, qb, kv):
    shape = jax.ShapeDtypeStruct((3, 512, 128), F32)
    return pl.pallas_call(
        attend_kernel,
        in_specs=[sspec(), vspec(), vspec(), vspec()],
        out_specs=[vspec(), vspec()],
        out_shape=[shape, shape],
        compiler_params=params(),
        cost_estimate=cost(4 * 1024 * 4096 * 128, 4 << 20, 1024 * 4096),
        name="attend",
    )(idx, qa, qb, kv)


def combine_kernel(a_ref, b_ref, out_ref):
    ma, mb = a_ref[1], b_ref[1]
    top = jnp.maximum(ma, mb)
    fa = jnp.exp2((ma - top) * EXP_SCALE)
    fb = jnp.exp2((mb - top) * EXP_SCALE)
    total = jnp.sum(a_ref[2] * fa + b_ref[2] * fb, axis=1, keepdims=True)
    o = ((a_ref[0] * fa + b_ref[0] * fb) / total).astype(BF16)
    for h in range(2):
        out_ref[:, h * 128:(h + 1) * 128] = o[h * 256:(h + 1) * 256]


def combine(a, b):
    return pl.pallas_call(
        combine_kernel,
        in_specs=[vspec(), vspec()],
        out_specs=vspec(),
        out_shape=jax.ShapeDtypeStruct((256, 256), BF16),
        compiler_params=params(),
        cost_estimate=cost(1 << 19, 2 << 20),
        name="combine",
    )(a, b)


def local(tokens, query_ckpt, key_value_ckpt, numerators):
    zl, c, zh = lax.axis_index("zl"), lax.axis_index("c"), lax.axis_index("zh")
    f = lax.axis_index(("zh", "x", "y"))
    r = zl * 2 + c
    idx = jnp.stack([zh, c, f]).astype(jnp.int32)
    share = (numerators[r].astype(F32) / jnp.sum(numerators).astype(F32)).reshape(1)

    perm = np.zeros((256, 256), np.float32)
    perm[np.arange(256), pair_order()] = 1.0
    send, keep = prepare(idx, share, query_ckpt[0], key_value_ckpt[0], jnp.asarray(perm))
    half = keep + lax.ppermute(send, "c", SWAP)
    mine = jnp.where(zl == 0, half[0], half[1])
    theirs = jnp.where(zl == 0, half[1], half[0]).astype(BF16)
    w = (mine + lax.ppermute(theirs, "zl", SWAP).astype(F32)).astype(BF16)
    wq, wkv = w[0:256], w[256:320]

    own, out = normalise(idx, tokens)
    got = lax.ppermute(out, "zh", SWAP)
    other = lax.ppermute(got, "c", SWAP)
    first = jnp.where(c == 0, got, other)
    second = jnp.where(c == 0, other, got)

    plane = ("x", "y")
    wkv_all = lax.all_to_all(jnp.broadcast_to(wkv[None], (16, 64, 256)), plane, 0, 0)
    wq_all = lax.all_to_all(jnp.broadcast_to(wq[None], (16, 256, 256)), plane, 0, 0)

    inverse_freq = jnp.exp(
        -(jnp.arange(64, dtype=F32) * (2.0 / HEAD)) * math.log(theta_base)
    )
    positions = (f * 256 + jnp.arange(256, dtype=jnp.int32)).astype(F32)
    angles = positions[:, None] * inverse_freq[None, :]
    cos, sin = jnp.cos(angles), jnp.sin(angles)
    my_freq = lax.dynamic_slice_in_dim(inverse_freq, r * 16, 16)
    angles_t = positions[None, :] * my_freq[:, None]
    cos_t, sin_t = jnp.cos(angles_t), jnp.sin(angles_t)

    kv_theirs = project(kv_kernel, wkv_all, (first, second), (64, 256), F32, "kv_theirs")
    kv_got = lax.ppermute(kv_theirs, "zh", SWAP)
    kv_own = project(kv_kernel, wkv_all, (own,), (64, 256), F32, "kv_own")
    pair = finish(kv_finish_kernel, (kv_own, kv_got, cos_t, sin_t), (2, 64, 128), "kv_finish")
    kv_all = lax.all_to_all(
        jnp.broadcast_to(pair[None], (64, 2, 64, 128)).reshape(128, 64, 128),
        ("zh", "x", "y", "zl", "c"), 0, 0,
    )

    q_theirs = project(q_kernel, wq_all, (first, second), (256, 256), BF16, "q_theirs")
    q_got = lax.ppermute(q_theirs, "zh", SWAP)
    q_own = project(q_kernel, wq_all, (own,), (256, 256), F32, "q_own")
    qa = finish(q_finish_kernel, (q_own, q_got, cos, sin), (2, 256, 128), "q_finish")
    qb = lax.ppermute(qa, "c", SWAP)

    oa, ob = attend(idx, qa, qb, kv_all.reshape(32, 4, 64, 128))
    mixed = combine(oa, lax.ppermute(ob, "c", SWAP))
    return lax.all_gather(mixed, ("zl", "c"), axis=1, tiled=True)


def solution(mesh):
    grid = Mesh(mesh.devices.reshape(2, 2, 2, 4, 4), ("zl", "c", "zh", "x", "y"))
    rep, fsdp = ("zl", "c"), ("zh", "x", "y")
    in_specs = (P(fsdp, None), P(rep, fsdp, None), P(rep, fsdp, None), P())
    return jax.shard_map(
        local, mesh=grid, in_specs=in_specs, out_specs=P(fsdp, None), check_vma=False
    )
```

time: 449 us -> 173 us (0.39)
  the two profiles are of different devices: /device:TPU:1 before, /device:TPU:71 now
where the time goes in v1:
time: 173 us; the launch traced here: 172 us
  waiting for transfers between devices  64.6 us (37%)
  Pallas kernels  47.1 us (27%)
  starting transfers between devices  33.1 us (19%)
  local copies, waits for them, and re-layouts  9.99 us (6%)
  blocking collectives  8.47 us (5%)
  other arithmetic  6.85 us (4%)
    ppermute x1, waiting for transfers between devices, local(): w = (mine + lax.ppermute(theirs, 'zl', SWAP).astype(F32)).astype(BF16)  26.7 us
    ppermute x1, waiting for transfers between devices, local(): q_got = lax.ppermute(q_theirs, 'zh', SWAP)  18.2 us
    pallas_call x1, Pallas kernels, attend(): pl.pallas_call(attend_kernel, in_specs=[sspec(), vspec(), vspec(), vspec(...  17.9 us
    pallas_call x4, Pallas kernels, project(): pl.pallas_call(kernel, in_specs=[vspec()] * (1 + len(xs)), out_specs=vspe...  13.4 us
    all_to_all x1, starting transfers between devices, local(): lax.all_to_all(jnp.broadcast_to(pair[None], (64, 2, 64, 128)).reshape(128...  13.1 us
    all_to_all x1, waiting for transfers between devices, local(): lax.all_to_all(jnp.broadcast_to(wkv[None], (16, 64, 256)), plane, 0, 0)  8.56 us
    all_gather x1, blocking collectives, local(): return lax.all_gather(mixed, ('zl', 'c'), axis=1, tiled=True)  8.47 us
    pallas_call x1, Pallas kernels, normalise(): pl.pallas_call(norm_kernel, grid=(rows // step,), in_specs=[sspec(), pl.B...  7.12 us
  transfers between devices with their start and end apart: 11, of which 7 were waited for; matrix products, arithmetic and copies ran while one was open for 4% of the time, Pallas kernels for 14%

profile of v1, /device:TPU:71, one launch (start us, length us, event | category | flops | bytes accessed | tf_op | source)
XLA Modules:
  0.0 171.6 jit_solution(11813508479992117126)
XLA Ops:
  0.0 1.3 reduce_sum.9
  1.9 1.3 dynamic_slice.6
  3.9 0.6 pad_add_fusion.idx
  4.5 2.9 %prepare.1 = (f32[2,320,256]{2,1,0:T(8,128)}, f32[2,320,256]{2,1,0:T(8,128)}) custom-call(s32[3]{0:T(128)} %pad_add_fusion.idx, f32[1]{0:T(128)} %bitcast.4.share, f32[256,1024]{1,0:T(8,128)} %bitcast.16, f32[256,256]{1,0:T(8,128)} %bitcast.17, f32[256,256]{1,0:T(8,128)} %constant.39.clone.perm_ref), custom_call_target="tpu_custom_call" | custom-call | flops 201326592 | bytes 3145728 | tf_op jit(solution)/shard_map/prepare/pallas_call | solution.py:108
  7.4 0.0 copy-start.3
  7.4 0.7 collective-permute-start
  8.1 7.1 %normalise.1 = (bf16[256,4096]{1,0:T(8,128)(2,1)}, bf16[256,2048]{1,0:T(8,128)(2,1)}) custom-call(s32[3]{0:T(128)} %pad_add_fusion.idx, bf16[256,8192]{1,0:T(8,128)(2,1)} %x_ref.1), custom_call_target="tpu_custom_call" | custom-call | flops 8388608 | bytes 8388608 | tf_op jit(solution)/shard_map/normalise/pallas_call | solution.py:65
  15.2 0.0 collective-permute-start.2
  15.2 0.0 collective-permute-done
  15.2 0.0 copy-done.3
  15.2 0.1 add.39
  15.3 1.7 collective-permute-start.1
  17.0 26.7 %collective-permute-done.1 = bf16[320,256]{1,0:T(8,128)(2,1)S(1)} collective-permute-done((bf16[320,256]{1,0:T(8,128)(2,1)S(1)}, bf16[320,256]{1,0:T(8,128)(2,1)S(1)}, u32[]{:S(2)}, u32[]{:S(2)}) %collective-permute-start.1) | collective-permute-done | bytes 163872 | tf_op jit(solution)/shard_map/ppermute | solution.py:294
  43.8 0.1 fusion
  43.8 0.8 broadcast_in_dim.7
  44.7 6.9 %all-to-all-start.1 = ((bf16[16,64,256]{2,1,0:T(8,128)(2,1)}), bf16[16,64,256]{2,1,0:T(8,128)(2,1)S(1)}, u32[]{:S(2)}, u32[]{:S(2)}) async-start(bf16[16,64,256]{2,1,0:T(8,128)(2,1)} %broadcast_in_dim.7), calls=%async_computation.1 | async-start | bytes 1048576 | tf_op jit(solution)/shard_map/all_to_all | solution.py:304
  51.6 8.6 %all-to-all-done.1.w_ref = bf16[16,64,256]{2,1,0:T(8,128)(2,1)S(1)} async-done(((bf16[16,64,256]{2,1,0:T(8,128)(2,1)}), bf16[16,64,256]{2,1,0:T(8,128)(2,1)S(1)}, u32[]{:S(2)}, u32[]{:S(2)}) %all-to-all-start.1) | async-done | bytes 524320 | tf_op jit(solution)/shard_map/all_to_all | solution.py:304
  60.1 0.0 copy-start.1
  60.1 1.5 broadcast_in_dim.6
  61.6 0.0 copy-done.1
  61.7 5.3 %all-to-all-start = ((bf16[16,256,256]{2,1,0:T(8,128)(2,1)}), bf16[16,256,256]{2,1,0:T(8,128)(2,1)S(1)}, u32[]{:S(2)}, u32[]{:S(2)}) async-start(bf16[16,256,256]{2,1,0:T(8,128)(2,1)} %broadcast_in_dim.6), calls=%async_computation | async-start | bytes 4194304 | tf_op jit(solution)/shard_map/all_to_all | solution.py:305
  66.9 0.0 collective-permute-done.2
  66.9 2.6 %collective-permute-start.3 = (bf16[256,2048]{1,0:T(8,128)(2,1)}, bf16[256,2048]{1,0:T(8,128)(2,1)S(1)}, u32[]{:S(2)}, u32[]{:S(2)}) collective-permute-start(bf16[256,2048]{1,0:T(8,128)(2,1)} %collective-permute-done.2), channel_id=1, source_target_pairs={{0,32},{32,0},{1,33},{33,1},{2,34},{34,2},{3,35},{35,3},{4,36},{36... | collective-permute-start | bytes 3145736 | tf_op jit(solution)/shard_map/ppermute | solution.py:299
  69.6 0.1 dynamic_slice.7
  69.7 2.4 %collective-permute-done.3 = bf16[256,2048]{1,0:T(8,128)(2,1)S(1)} collective-permute-done((bf16[256,2048]{1,0:T(8,128)(2,1)}, bf16[256,2048]{1,0:T(8,128)(2,1)S(1)}, u32[]{:S(2)}, u32[]{:S(2)}) %collective-permute-start.3) | collective-permute-done | bytes 1048608 | tf_op jit(solution)/shard_map/ppermute | solution.py:299
  72.1 2.8 %broadcast_select_fusion = (bf16[256,2048]{1,0:T(8,128)(2,1)}, bf16[256,2048]{1,0:T(8,128)(2,1)}) fusion(bf16[256,2048]{1,0:T(8,128)(2,1)S(1)} %collective-permute-done.3, bf16[256,2048]{1,0:T(8,128)(2,1)} %collective-permute-done.2, pred[]{:T(512)S(6)} %eq.9), kind=kLoop, calls=%fused_computation | loop fusion | flops 1048576 | bytes 4194305 | tf_op jit(solution)/shard_map/jit(_where)/select_n | solution.py:301
  74.8 3.1 %kv_theirs.1 = f32[64,256]{1,0:T(8,128)} custom-call(bf16[16,64,256]{2,1,0:T(8,128)(2,1)} %copy-done.1, bf16[256,2048]{1,0:T(8,128)(2,1)} %get-tuple-element.18.refs_0_, bf16[256,2048]{1,0:T(8,128)(2,1)} %get-tuple-element.17.refs_1_), custom_call_target="tpu_custom_call" | custom-call | flops 134217728 | bytes 4194304 | tf_op jit(solution)/shard_map/kv_theirs/pallas_call | solution.py:148
  77.9 2.1 %collective-permute-start.6 = (f32[64,256]{1,0:T(8,128)}, f32[64,256]{1,0:T(8,128)S(1)}, u32[]{:S(2)}, u32[]{:S(2)}) collective-permute-start(f32[64,256]{1,0:T(8,128)} %kv_theirs.1), channel_id=1, source_target_pairs={{0,16},{16,0},{1,17},{17,1},{2,18},{18,2},{3,19},{19,3},{4,20},{20... | collective-permute-start | bytes 196616 | tf_op jit(solution)/shard_map/ppermute | solution.py:318
  80.0 0.8 multiply_sine_fusion.1
  80.8 3.1 %kv_own.1.own_ref = f32[64,256]{1,0:T(8,128)} custom-call(bf16[16,64,256]{2,1,0:T(8,128)(2,1)} %copy-done.1, bf16[256,4096]{1,0:T(8,128)(2,1)} %get-tuple-element.13.refs_0_), custom_call_target="tpu_custom_call" | custom-call | flops 134217728 | bytes 4194304 | tf_op jit(solution)/shard_map/kv_own/pallas_call | solution.py:148
  83.9 0.0 collective-permute-done.6.got_ref
  83.9 0.0 copy-start.5
  83.9 0.6 copy-done.5
  84.5 1.5 kv_finish.1
  86.0 5.4 %all-to-all-done.w_ref = bf16[16,256,256]{2,1,0:T(8,128)(2,1)S(1)} async-done(((bf16[16,256,256]{2,1,0:T(8,128)(2,1)}), bf16[16,256,256]{2,1,0:T(8,128)(2,1)S(1)}, u32[]{:S(2)}, u32[]{:S(2)}) %all-to-all-start) | async-done | bytes 2097184 | tf_op jit(solution)/shard_map/all_to_all | solution.py:305
  91.4 0.0 copy-start
  91.4 2.6 %broadcast_in_dim.8 = bf16[64,2,64,128]{3,2,1,0:T(8,128)(2,1)} broadcast(bf16[2,64,128]{2,1,0:T(8,128)(2,1)} %kv_finish.1), dimensions={1,2,3} | broadcast | bytes 2129920 | tf_op jit(solution)/shard_map/broadcast_in_dim | solution.py:322
  94.1 0.0 copy-done
  94.1 13.1 %all-to-all-start.2 = ((bf16[128,64,128]{2,1,0:T(8,128)(2,1)}), bf16[128,64,128]{2,1,0:T(8,128)(2,1)}, u32[]{:S(2)}, u32[]{:S(2)}) async-start(bf16[128,64,128]{2,1,0:T(8,128)(2,1)} %bitcast.15), calls=%async_computation.2 | async-start | bytes 4194304 | tf_op jit(solution)/shard_map/all_to_all | solution.py:321
  107.2 3.6 %q_theirs.1 = bf16[256,256]{1,0:T(8,128)(2,1)} custom-call(bf16[16,256,256]{2,1,0:T(8,128)(2,1)} %copy-done, bf16[256,2048]{1,0:T(8,128)(2,1)} %get-tuple-element.18.refs_0_, bf16[256,2048]{1,0:T(8,128)(2,1)} %get-tuple-element.17.refs_1_), custom_call_target="tpu_custom_call" | custom-call | flops 536870912 | bytes 4194304 | tf_op jit(solution)/shard_map/q_theirs/pallas_call | solution.py:148
  110.7 0.0 collective-permute-start.4
  110.7 1.2 multiply_sine_fusion
  112.0 3.6 %q_own.1.own_ref = f32[256,256]{1,0:T(8,128)} custom-call(bf16[16,256,256]{2,1,0:T(8,128)(2,1)} %copy-done, bf16[256,4096]{1,0:T(8,128)(2,1)} %get-tuple-element.13.refs_0_), custom_call_target="tpu_custom_call" | custom-call | flops 536870912 | bytes 4194304 | tf_op jit(solution)/shard_map/q_own/pallas_call | solution.py:148
  115.6 18.2 %collective-permute-done.4.got_ref = bf16[256,256]{1,0:T(8,128)(2,1)S(1)} collective-permute-done((bf16[256,256]{1,0:T(8,128)(2,1)}, bf16[256,256]{1,0:T(8,128)(2,1)S(1)}, u32[]{:S(2)}, u32[]{:S(2)}) %collective-permute-start.4) | collective-permute-done | bytes 131104 | tf_op jit(solution)/shard_map/ppermute | solution.py:327
  133.8 0.0 copy-start.4
  133.8 0.7 copy-done.4
  134.5 2.1 %q_finish.1.qa_ref = bf16[2,256,128]{2,1,0:T(8,128)(2,1)} custom-call(f32[256,256]{1,0:T(8,128)} %q_own.1.own_ref, bf16[256,256]{1,0:T(8,128)(2,1)} %copy-done.4, f32[256,64]{1,0:T(8,128)} %get-tuple-element.22.cos_ref, f32[256,64]{1,0:T(8,128)} %get-tuple-element.21.sin_ref), custom_call_target="tpu_custom_call" | custom-call | flops 262144 | bytes 524288 | tf_op jit(solution)/shard_map/q_finish/pallas_call | solution.py:183
  136.5 0.4 collective-permute-start.5
  137.0 1.2 collective-permute-done.5.qb_ref
  138.2 0.0 copy-start.6
  138.2 0.0 all-to-all-done.2
  138.2 0.6 copy-done.6
  138.8 17.9 %attend.1 = (f32[3,512,128]{2,1,0:T(8,128)}, f32[3,512,128]{2,1,0:T(8,128)}) custom-call(s32[3]{0:T(128)} %pad_add_fusion.idx, bf16[2,256,128]{2,1,0:T(8,128)(2,1)} %q_finish.1.qa_ref, bf16[2,256,128]{2,1,0:T(8,128)(2,1)} %copy-done.6, bf16[32,4,64,128]{3,2,1,0:T(8,128)(2,1)} %bitcast.10.kv_ref), custom_call_target="tpu_custom_call" | custom-call | flops 2147483648 | bytes 4194304 | tf_op jit(solution)/shard_map/attend/pallas_call | solution.py:247
  156.7 0.4 collective-permute-start.7
  157.1 2.1 %collective-permute-done.7.b_ref = f32[3,512,128]{2,1,0:T(8,128)S(1)} collective-permute-done((f32[3,512,128]{2,1,0:T(8,128)}, f32[3,512,128]{2,1,0:T(8,128)S(1)}, u32[]{:S(2)}, u32[]{:S(2)}) %collective-permute-start.7) | collective-permute-done | bytes 786464 | tf_op jit(solution)/shard_map/ppermute | solution.py:333
  159.2 0.0 copy-start.2
  159.2 0.9 copy-done.2
  160.2 2.2 %combine.1 = bf16[256,256]{1,0:T(8,128)(2,1)} custom-call(f32[3,512,128]{2,1,0:T(8,128)} %get-tuple-element.15.a_ref, f32[3,512,128]{2,1,0:T(8,128)} %copy-done.2), custom_call_target="tpu_custom_call" | custom-call | flops 524288 | bytes 2097152 | tf_op jit(solution)/shard_map/combine/pallas_call | solution.py:270
  162.4 8.5 %all_gather.3 = bf16[256,1024]{1,0:T(8,128)(2,1)S(1)} all-gather(bf16[256,256]{1,0:T(8,128)(2,1)} %combine.1), channel_id=1, replica_groups=mesh['zl'=2,'c'=2,'zh'=2,'x'=4,'y'=4] {'zl','c'}, dimensions={1}, use_global_device_ids=true | all-gather | bytes 655360 | tf_op jit(solution)/shard_map/all_gather | solution.py:334
  170.8 0.8 copy.7
  (5 shorter events, 0.1 us)
Async XLA Ops:
  7.4 7.8 %copy-start.3 = (f32[2,320,256]{2,1,0:T(8,128)S(1)}, f32[2,320,256]{2,1,0:T(8,128)}, u32[]{:S(2)}) copy-start(f32[2,320,256]{2,1,0:T(8,128)} %get-tuple-element.11) | copy-start | bytes 1966084
  7.4 7.8 %collective-permute-start = (f32[2,320,256]{2,1,0:T(8,128)}, f32[2,320,256]{2,1,0:T(8,128)S(1)}, u32[]{:S(2)}, u32[]{:S(2)}) collective-permute-start(f32[2,320,256]{2,1,0:T(8,128)} %get-tuple-element.12), channel_id=1, source_target_pairs={{0,32},{32,0},{1,33},{33,1},{2,34},{34,2},{3,35},{35,3},{4,36},{36... | collective-permute-start | bytes 1966088 | tf_op jit(solution)/shard_map/ppermute | solution.py:291
  15.2 51.7 %collective-permute-start.2 = (bf16[256,2048]{1,0:T(8,128)(2,1)}, bf16[256,2048]{1,0:T(8,128)(2,1)}, u32[]{:S(2)}, u32[]{:S(2)}) collective-permute-start(bf16[256,2048]{1,0:T(8,128)(2,1)} %get-tuple-element.14), channel_id=1, source_target_pairs={{0,16},{16,0},{1,17},{17,1},{2,18},{18,2},{3,19},{19,3},{4,20},{20... | collective-permute-start | bytes 3145736 | tf_op jit(solution)/shard_map/ppermute | solution.py:298
  15.3 28.4 %collective-permute-start.1 = (bf16[320,256]{1,0:T(8,128)(2,1)S(1)}, bf16[320,256]{1,0:T(8,128)(2,1)S(1)}, u32[]{:S(2)}, u32[]{:S(2)}) collective-permute-start(bf16[320,256]{1,0:T(8,128)(2,1)S(1)} %fusion.1), channel_id=1, source_target_pairs={{0,64},{64,0},{1,65},{65,1},{2,66},{66,2},{3,67},{67,3},{4,68},{68... | collective-permute-start | bytes 491528 | tf_op jit(solution)/shard_map/ppermute | solution.py:294
  44.7 15.4 %all-to-all-start.1 = ((bf16[16,64,256]{2,1,0:T(8,128)(2,1)}), bf16[16,64,256]{2,1,0:T(8,128)(2,1)S(1)}, u32[]{:S(2)}, u32[]{:S(2)}) async-start(bf16[16,64,256]{2,1,0:T(8,128)(2,1)} %broadcast_in_dim.7), calls=%async_computation.1 | async-start | bytes 1048576 | tf_op jit(solution)/shard_map/all_to_all | solution.py:304
  60.1 1.5 copy-start.1
  61.7 29.8 %all-to-all-start = ((bf16[16,256,256]{2,1,0:T(8,128)(2,1)}), bf16[16,256,256]{2,1,0:T(8,128)(2,1)S(1)}, u32[]{:S(2)}, u32[]{:S(2)}) async-start(bf16[16,256,256]{2,1,0:T(8,128)(2,1)} %broadcast_in_dim.6), calls=%async_computation | async-start | bytes 4194304 | tf_op jit(solution)/shard_map/all_to_all | solution.py:305
  66.9 5.1 %collective-permute-start.3 = (bf16[256,2048]{1,0:T(8,128)(2,1)}, bf16[256,2048]{1,0:T(8,128)(2,1)S(1)}, u32[]{:S(2)}, u32[]{:S(2)}) collective-permute-start(bf16[256,2048]{1,0:T(8,128)(2,1)} %collective-permute-done.2), channel_id=1, source_target_pairs={{0,32},{32,0},{1,33},{33,1},{2,34},{34,2},{3,35},{35,3},{4,36},{36... | collective-permute-start | bytes 3145736 | tf_op jit(solution)/shard_map/ppermute | solution.py:299
  77.9 6.0 %collective-permute-start.6 = (f32[64,256]{1,0:T(8,128)}, f32[64,256]{1,0:T(8,128)S(1)}, u32[]{:S(2)}, u32[]{:S(2)}) collective-permute-start(f32[64,256]{1,0:T(8,128)} %kv_theirs.1), channel_id=1, source_target_pairs={{0,16},{16,0},{1,17},{17,1},{2,18},{18,2},{3,19},{19,3},{4,20},{20... | collective-permute-start | bytes 196616 | tf_op jit(solution)/shard_map/ppermute | solution.py:318
  83.9 0.6 copy-start.5
  91.4 2.6 %copy-start = (bf16[16,256,256]{2,1,0:T(8,128)(2,1)}, bf16[16,256,256]{2,1,0:T(8,128)(2,1)S(1)}, u32[]{:S(2)}) copy-start(bf16[16,256,256]{2,1,0:T(8,128)(2,1)S(1)} %all-to-all-done.w_ref) | copy-start | bytes 6291460
  94.1 44.1 %all-to-all-start.2 = ((bf16[128,64,128]{2,1,0:T(8,128)(2,1)}), bf16[128,64,128]{2,1,0:T(8,128)(2,1)}, u32[]{:S(2)}, u32[]{:S(2)}) async-start(bf16[128,64,128]{2,1,0:T(8,128)(2,1)} %bitcast.15), calls=%async_computation.2 | async-start | bytes 4194304 | tf_op jit(solution)/shard_map/all_to_all | solution.py:321
  110.7 23.1 %collective-permute-start.4 = (bf16[256,256]{1,0:T(8,128)(2,1)}, bf16[256,256]{1,0:T(8,128)(2,1)S(1)}, u32[]{:S(2)}, u32[]{:S(2)}) collective-permute-start(bf16[256,256]{1,0:T(8,128)(2,1)} %q_theirs.1), channel_id=1, source_target_pairs={{0,16},{16,0},{1,17},{17,1},{2,18},{18,2},{3,19},{19,3},{4,20},{20... | collective-permute-start | bytes 393224 | tf_op jit(solution)/shard_map/ppermute | solution.py:327
  133.8 0.7 copy-start.4
  136.5 1.6 collective-permute-start.5
  138.2 0.7 copy-start.6
  156.7 2.5 %collective-permute-start.7 = (f32[3,512,128]{2,1,0:T(8,128)}, f32[3,512,128]{2,1,0:T(8,128)S(1)}, u32[]{:S(2)}, u32[]{:S(2)}) collective-permute-start(f32[3,512,128]{2,1,0:T(8,128)} %get-tuple-element.16), channel_id=1, source_target_pairs={{0,32},{32,0},{1,33},{33,1},{2,34},{34,2},{3,35},{35,3},{4,36},{36... | collective-permute-start | bytes 2359304 | tf_op jit(solution)/shard_map/ppermute | solution.py:333
  159.2 0.9 copy-start.2

commit v2 on v0

v2 whole, which is shorter than its diff:
```python
import functools
import math

import jax
import jax.numpy as jnp
from jax import lax
from jax.experimental import pallas as pl
from jax.experimental.pallas import tpu as pltpu
from jax.sharding import Mesh, PartitionSpec as P

theta_base = 500000.0
eps_norm = 1e-05
masked_score = -1e30
HEAD = 128
F32 = jnp.float32
BF16 = jnp.bfloat16
VMEM = pltpu.VMEM
SMEM = pltpu.SMEM
NT = (((1,), (1,)), ((), ()))
SWAP = [(0, 1), (1, 0)]


def params(mib=20):
    return pltpu.CompilerParams(vmem_limit_bytes=mib * 1024 * 1024)


def cost(flops, nbytes, trans=0):
    return pl.CostEstimate(flops=flops, bytes_accessed=nbytes, transcendentals=trans)


def vspec():
    return pl.BlockSpec(memory_space=VMEM)


def sspec():
    return pl.BlockSpec(memory_space=SMEM)


def pair_order():
    row = lax.broadcasted_iota(jnp.int32, (256, 256), 0)
    col = lax.broadcasted_iota(jnp.int32, (256, 256), 1)
    r, t = row // 64, row % 64
    key = r * 16 + t + jnp.where(t < 16, 0, 48)
    return jnp.where(col == jnp.where(t < 32, key, r * 32 + t + 96), 1.0, 0.0)


def norm_kernel(idx, x_ref, scale_ref, send_ref):
    zh, c = idx[0], idx[1]
    x = x_ref[...].astype(F32)
    scale = lax.rsqrt(jnp.mean(x * x, axis=-1, keepdims=True) + eps_norm)
    scale_ref[...] = jnp.broadcast_to(scale, scale_ref.shape)
    quarter = send_ref.shape[1]
    start = pl.multiple_of(((1 - zh) * 2 + c) * quarter, quarter)
    send_ref[...] = normed(x_ref, start, quarter, scale)


def normed(x_ref, start, width, scale):
    return (x_ref[:, pl.ds(start, width)].astype(F32) * scale).astype(BF16)


def normalise(idx, tokens):
    rows, width = tokens.shape
    step = 128
    return pl.pallas_call(
        norm_kernel,
        grid=(rows // step,),
        in_specs=[sspec(), pl.BlockSpec((step, width), lambda i: (i, 0))],
        out_specs=[
            pl.BlockSpec((step, 128), lambda i: (i, 0)),
            pl.BlockSpec((step, width // 4), lambda i: (i, 0)),
        ],
        out_shape=[
            jax.ShapeDtypeStruct((rows, 128), F32),
            jax.ShapeDtypeStruct((rows, width // 4), BF16),
        ],
        compiler_params=params(),
        cost_estimate=cost(rows * width * 4, rows * width * 3),
        name="normalise",
    )(idx, tokens)


def share_of(idx, num, shape):
    r = idx[3]
    total = num[0] + num[1] + num[2] + num[3]
    mine = jnp.full(shape, num[r], jnp.int32).astype(F32)
    return mine / jnp.full(shape, total, jnp.int32).astype(F32)


def prep_kernel(idx, num, q_ref, kv_ref, send_ref, keep_ref):
    c = idx[1]
    s = share_of(idx, num, (1, 256))
    kvt = lax.dot_general(
        pair_order(), kv_ref[0] * s, NT, precision=lax.Precision.HIGHEST,
        preferred_element_type=F32,
    )
    for zl in range(2):
        keep = pl.multiple_of((zl * 2 + c) * 256, 256)
        send = pl.multiple_of((zl * 2 + 1 - c) * 256, 256)
        first, second = kvt[zl * 128:zl * 128 + 64], kvt[zl * 128 + 64:zl * 128 + 128]
        for ref, col, pair in (
            (keep_ref, keep, jnp.where(c == 0, first, second)),
            (send_ref, send, jnp.where(c == 0, second, first)),
        ):
            for half in range(2):
                at = half * 160
                ref[zl, at:at + 128] = q_ref[0, half * 128:half * 128 + 128, pl.ds(col, 256)] * s
                ref[zl, at + 128:at + 160] = pair[half * 32:half * 32 + 32]


def prepare(idx, num, q, kv):
    shape = jax.ShapeDtypeStruct((2, 320, 256), F32)
    return pl.pallas_call(
        prep_kernel,
        in_specs=[sspec(), sspec()] + [vspec()] * 2,
        out_specs=[vspec(), vspec()],
        out_shape=[shape, shape],
        compiler_params=params(),
        cost_estimate=cost(1 << 20, 3 << 20),
        name="prepare",
    )(idx, num, q, kv)


def ring(step):
    return [(i, (i + step) % 4) for i in range(4)]


def gather_plane(w):
    lower, upper = w[0:160], w[160:320]
    lower = jnp.stack([lower] + [lax.ppermute(lower, "y", ring(d)) for d in (1, 3, 2)])
    upper = jnp.stack([upper] + [lax.ppermute(upper, "x", ring(d)) for d in (1, 3, 2)])
    lower, upper = lax.optimization_barrier((lower, upper))
    lowers = [lower] + [lax.ppermute(lower, "x", ring(d)) for d in (1, 3, 2)]
    uppers = [upper] + [lax.ppermute(upper, "y", ring(d)) for d in (1, 3, 2)]
    return lowers + uppers


def plane_block(idx, w_refs, j):
    back = (0, 1, 3, 2)
    dx, dy = j // 4, j % 4
    low, up = w_refs[dx], w_refs[4 + dy]
    q = jnp.concatenate([low[dy, 0:128], up[dx, 0:128]], axis=0)
    pair = jnp.concatenate([low[dy, 128:160], up[dx, 128:160]], axis=0)
    return q, pair, ((idx[4] + 4 - back[dx]) % 4) * 4 + (idx[5] + 4 - back[dy]) % 4


def accumulate(idx, w_refs, block):
    acc, pair_acc = None, None
    for j in range(16):
        w, pair, at = plane_block(idx, w_refs, j)
        x = block(at)
        part = jnp.dot(x, w, preferred_element_type=F32)
        pair_part = lax.dot_general(x, pair, NT, preferred_element_type=F32)
        acc = part if acc is None else acc + part
        pair_acc = pair_part if pair_acc is None else pair_acc + pair_part
    row = lax.broadcasted_iota(jnp.int32, (64, 64), 0)
    col = lax.broadcasted_iota(jnp.int32, (64, 64), 1)
    pair_acc = lax.dot_general(
        jnp.where(row == col, 1.0, 0.0), pair_acc, NT, precision=lax.Precision.HIGHEST,
        preferred_element_type=F32,
    )
    return acc, pair_acc


def own_kernel(idx, *refs):
    w_refs, (x_ref, scale_ref, q_ref, pair_ref) = refs[:-4], refs[-4:]
    scale = scale_ref[:, 0:1]

    def block(at):
        return normed(x_ref, pl.multiple_of((idx[0] * 16 + at) * 256, 256), 256, scale)

    q_ref[...], pair_ref[...] = accumulate(idx, w_refs, block)


def theirs_kernel(idx, *refs):
    w_refs, (xa_ref, xb_ref, out_ref) = refs[:-3], refs[-3:]

    def block(at):
        cols = pl.ds(pl.multiple_of((at % 8) * 256, 256), 256)
        return jnp.where(at // 8 == idx[1], xa_ref[:, cols], xb_ref[:, cols])

    q, pair = accumulate(idx, w_refs, block)
    high = pair.astype(BF16)
    out_ref[0:256] = q.astype(BF16)
    out_ref[256:320] = high
    out_ref[320:384] = (pair - high.astype(F32)).astype(BF16)


def project(kernel, args, outs, name):
    return pl.pallas_call(
        kernel,
        in_specs=[sspec()] + [vspec()] * (len(args) - 1),
        out_specs=[vspec()] * len(outs),
        out_shape=outs,
        compiler_params=params(),
        cost_estimate=cost(2 * 256 * 320 * 4096, 5 << 20),
        name=name,
    )(*args)


def pair_finish_kernel(own_ref, got_ref, cos_ref, sin_ref, out_ref):
    t = own_ref[...] + (got_ref[256:320].astype(F32) + got_ref[320:384].astype(F32))
    u, w = t[0:16], t[16:32]
    cos, sin = cos_ref[...], sin_ref[...]
    key = jnp.concatenate([u * cos - w * sin, w * cos + u * sin], axis=0)
    val = t[32:64]
    for r in range(4):
        cols = slice(r * 64, (r + 1) * 64)
        piece = jnp.concatenate([key[:, cols], val[:, cols]], axis=1).astype(BF16)
        for f in range(out_ref.shape[0]):
            out_ref[f, r] = piece


def q_finish_kernel(own_ref, got_ref, cos_ref, sin_ref, out_ref):
    t = own_ref[...] + got_ref[0:256].astype(F32)
    cos, sin = cos_ref[...], sin_ref[...]
    for h in range(2):
        u = t[:, h * 128:h * 128 + 64]
        w = t[:, h * 128 + 64:h * 128 + 128]
        rotated = jnp.concatenate([u * cos - w * sin, w * cos + u * sin], axis=1)
        out_ref[h] = rotated.T.astype(BF16)


def finish(kernel, args, shape, name):
    return pl.pallas_call(
        kernel,
        in_specs=[vspec()] * 4,
        out_specs=vspec(),
        out_shape=jax.ShapeDtypeStruct(shape, BF16),
        compiler_params=params(),
        cost_estimate=cost(1 << 18, 1 << 20),
        name=name,
    )(*args)


CHUNK = 512
KEYS = 2048
EXP_SCALE = math.log2(math.e) / math.sqrt(HEAD)
STAT = 144


def attend_kernel(idx, *refs):
    q_refs, kv_ref = refs[0:4], refs[4]
    o_refs = refs[5:9]
    k_s, v_s, qx, s0, s1 = refs[9:]
    scores = (s0, s1)
    f, r = idx[2], idx[3]
    lane = lax.broadcasted_iota(jnp.int32, (32, 128), 1)
    col = lax.broadcasted_iota(jnp.int32, (128, 128), 1)
    row = lax.broadcasted_iota(jnp.int32, (128, 128), 0)
    for p in range(KEYS // 128):
        ks, vs = [], []
        for rr in range(4):
            a = kv_ref[2 * p, rr].astype(F32)
            b = kv_ref[2 * p + 1, rr].astype(F32)
            ks.append(jnp.where(lane < 64, a, pltpu.roll(b, 64, 1)).astype(BF16))
            vs.append(jnp.where(lane < 64, pltpu.roll(a, 64, 1), b).astype(BF16))
        key = jnp.concatenate([x[0:16] for x in ks] + [x[16:32] for x in ks], axis=0)
        k_s[p * 128:(p + 1) * 128, 0:128] = key.T
        blk = 2 * p + row // 64
        extra = jnp.where((blk == f) & (col == row % 64), 1.0, 0.0)
        extra = jnp.where((blk > f) & (col == 64), 1.0, extra)
        k_s[p * 128:(p + 1) * 128, 128:256] = extra.astype(BF16)
        v_s[:, p * 128:(p + 1) * 128] = jnp.concatenate(vs, axis=0)
    t = lax.broadcasted_iota(jnp.int32, (128, 256), 0)
    i = lax.broadcasted_iota(jnp.int32, (128, 256), 1)
    hidden = ((t < 64) & (64 * r + t > i)) | (t == 64)
    qx[...] = jnp.where(hidden, masked_score, 0.0).astype(BF16)

    def queries(h):
        return jnp.concatenate([q_refs[h // 2][h % 2], qx[...]], axis=0)

    def score(h, j, q, top):
        s = jnp.dot(k_s[j * CHUNK:(j + 1) * CHUNK], q, preferred_element_type=F32)
        scores[h % 2][j * CHUNK:(j + 1) * CHUNK] = s
        part = jnp.max(s.reshape(CHUNK // 8, 8, 256), axis=0)
        return part if top is None else jnp.maximum(top, part)

    chunks = KEYS // CHUNK
    tops, q = None, queries(0)
    for j in range(chunks):
        tops = score(0, j, q, tops)
    for h in range(8):
        top = jnp.max(tops, axis=0, keepdims=True)
        tops, acc, total = None, None, None
        if h < 7:
            q = queries(h + 1)
        for j in range(chunks):
            if h < 7:
                tops = score(h + 1, j, q, tops)
            p = jnp.exp2((scores[h % 2][j * CHUNK:(j + 1) * CHUNK] - top) * EXP_SCALE)
            part = jnp.sum(p.reshape(CHUNK // 8, 8, 256), axis=0)
            mix = jnp.dot(
                v_s[:, j * CHUNK:(j + 1) * CHUNK], p.astype(BF16), preferred_element_type=F32
            )
            acc = mix if acc is None else acc + mix
            total = part if total is None else total + part
        total = jnp.sum(total, axis=0, keepdims=True)
        o_ref, at = o_refs[h // 2], (h % 2) * STAT
        o_ref[at:at + 128] = (acc / total).astype(BF16)
        put_log(o_ref, at, top * EXP_SCALE + jnp.log2(total))


def attend(idx, qs, kv):
    shape = jax.ShapeDtypeStruct((2 * STAT, 256), BF16)
    return pl.pallas_call(
        attend_kernel,
        in_specs=[sspec()] + [vspec()] * 5,
        out_specs=[vspec()] * 4,
        out_shape=[shape] * 4,
        scratch_shapes=[
            VMEM((KEYS, 256), BF16), VMEM((128, KEYS), BF16), VMEM((128, 256), BF16),
            VMEM((KEYS, 256), F32), VMEM((KEYS, 256), F32),
        ],
        compiler_params=params(),
        cost_estimate=cost(4 * 2048 * 2048 * 128, 4 << 20, 2048 * 2048),
        name="attend",
    )(idx, *qs, kv)


def log_sum(ref, at):
    t = ref[at + 128:at + STAT].astype(F32)
    return t[0:1] + t[1:2] + t[2:3]


def put_log(ref, at, log):
    w = lax.broadcasted_iota(jnp.int32, (16, 256), 0)
    hi = log.astype(BF16).astype(F32)
    mid = (log - hi).astype(BF16).astype(F32)
    terms = jnp.where(w == 0, hi, jnp.where(w == 1, mid, jnp.where(w == 2, log - hi - mid, 0.0)))
    ref[at + 128:at + STAT] = terms.astype(BF16)


def merged(a_ref, b_ref, at):
    a, b = log_sum(a_ref, at), log_sum(b_ref, at)
    top = jnp.maximum(a, b)
    fa, fb = jnp.exp2(a - top), jnp.exp2(b - top)
    total = fa + fb
    mixed = a_ref[at:at + 128].astype(F32) * (fa / total)
    mixed = mixed + b_ref[at:at + 128].astype(F32) * (fb / total)
    return mixed, top + jnp.log2(total)


def merge_kernel(a0, a1, b0, b1, o0, o1):
    for a_ref, b_ref, o_ref in ((a0, b0, o0), (a1, b1, o1)):
        for h in range(2):
            at = h * STAT
            mixed, log = merged(a_ref, b_ref, at)
            o_ref[at:at + 128] = mixed.astype(BF16)
            put_log(o_ref, at, log)


def last_kernel(a0, a1, b0, b1, out_ref):
    for i, (a_ref, b_ref) in enumerate(((a0, b0), (a1, b1))):
        for h in range(2):
            mixed, _ = merged(a_ref, b_ref, h * STAT)
            col = (i * 2 + h) * 128
            out_ref[:, col:col + 128] = mixed.T.astype(BF16)


def place_kernel(idx, mine_ref, other_ref, out_ref):
    r = idx[3]
    for i in range(2):
        for mask, ref in ((0, mine_ref), (1, other_ref)):
            col = pl.multiple_of(((r ^ mask) ^ (i * 2)) * 256, 256)
            out_ref[:, pl.ds(col, 256)] = ref[:, i * 256:(i + 1) * 256]


def small(kernel, args, shapes, name, scalars=0):
    return pl.pallas_call(
        kernel,
        in_specs=[sspec()] * scalars + [vspec()] * (len(args) - scalars),
        out_specs=[vspec()] * len(shapes),
        out_shape=[jax.ShapeDtypeStruct(shape, BF16) for shape in shapes],
        compiler_params=params(),
        cost_estimate=cost(1 << 19, 1 << 20),
        name=name,
    )(*args)


REP = ("zl", "c")


def to_rep(x, mask):
    if mask == 1:
        return lax.ppermute(x, "c", SWAP)
    if mask == 2:
        return lax.ppermute(x, "zl", SWAP)
    return lax.ppermute(x, REP, [(i, i ^ mask) for i in range(4)])


def average(send, keep, zl, dtype):
    half = keep + lax.ppermute(send, "c", SWAP)
    mine = jnp.where(zl == 0, half[0], half[1])
    theirs = jnp.where(zl == 0, half[1], half[0]).astype(dtype)
    return mine, lax.ppermute(theirs, "zl", SWAP)


def local(tokens, query_ckpt, key_value_ckpt, numerators):
    zl, c, zh = lax.axis_index("zl"), lax.axis_index("c"), lax.axis_index("zh")
    f = lax.axis_index(("zh", "x", "y"))
    r = zl * 2 + c
    idx = jnp.stack([zh, c, f, r, lax.axis_index("x"), lax.axis_index("y")]).astype(jnp.int32)

    send, keep = prepare(idx, numerators, query_ckpt, key_value_ckpt)
    w_mine, w_got = average(send, keep, zl, BF16)

    scale, out = normalise(idx, tokens)
    out, w_got = lax.optimization_barrier((out, w_got))
    w = (w_mine + w_got.astype(F32)).astype(BF16)
    w_all = gather_plane(w)
    got = lax.ppermute(out, "zh", SWAP)
    got, *w_all = lax.optimization_barrier((got, *w_all))
    other = lax.ppermute(got, "c", SWAP)

    inverse_freq = jnp.exp(
        -(jnp.arange(64, dtype=F32) * (2.0 / HEAD)) * math.log(theta_base)
    )
    positions = (f * 256 + jnp.arange(256, dtype=jnp.int32)).astype(F32)
    angles = positions[:, None] * inverse_freq[None, :]
    cos, sin = jnp.cos(angles), jnp.sin(angles)
    my_freq = lax.dynamic_slice_in_dim(inverse_freq, r * 16, 16)
    angles_t = positions[None, :] * my_freq[:, None]
    cos_t, sin_t = jnp.cos(angles_t), jnp.sin(angles_t)

    (theirs,) = project(
        theirs_kernel, (idx, *w_all, got, other), [jax.ShapeDtypeStruct((384, 256), BF16)],
        "theirs")
    back = lax.ppermute(theirs, "zh", SWAP)
    q_own, pair_own = project(
        own_kernel, (idx, *w_all, tokens, scale),
        [jax.ShapeDtypeStruct((256, 256), F32), jax.ShapeDtypeStruct((64, 256), F32)], "own")
    pair = finish(
        pair_finish_kernel, (pair_own, back, cos_t, sin_t), (32, 4, 32, 128), "pair_finish")
    pair_all = lax.all_to_all(
        pair.reshape(128, 32, 128), ("zh", "x", "y", "zl", "c"), 0, 0)
    q0 = finish(q_finish_kernel, (q_own, back, cos, sin), (2, 128, 256), "q_finish")
    qs = [q0] + [to_rep(q0, m) for m in (1, 2, 3)]

    parts = attend(idx, qs, pair_all.reshape(32, 4, 32, 128))
    stat = (2 * STAT, 256)
    b0, b1 = to_rep(parts[1], 1), to_rep(parts[3], 1)
    a0, a1 = small(merge_kernel, (parts[0], parts[2], b0, b1), [stat, stat], "merge")
    c0, c1 = to_rep(a1, 2), to_rep(a0, 2)
    (mine,) = small(last_kernel, (a0, a1, c0, c1), [(256, 512)], "last")
    (out,) = small(place_kernel, (idx, mine, to_rep(mine, 1)), [(256, 1024)], "place", 1)
    return out


def solution(mesh):
    grid = Mesh(mesh.devices.reshape(2, 2, 2, 4, 4), ("zl", "c", "zh", "x", "y"))
    fsdp = ("zh", "x", "y")
    in_specs = (P(fsdp, None), P(REP, fsdp, None), P(REP, fsdp, None), P())
    return jax.shard_map(
        local, mesh=grid, in_specs=in_specs, out_specs=P(fsdp, None), check_vma=False
    )
```

time: 449 us -> 118 us (0.26)
  waiting for transfers between devices: 318 us -> 49.5 us
  matrix products: 53.9 us -> 0 us
  starting transfers between devices: 0.27 us -> 44.3 us
  blocking collectives: 30.6 us -> 0 us
  other arithmetic: 19.8 us -> 0.94 us
  Pallas kernels: 0 us -> 17.8 us
  between operations: 14.5 us -> 0.15 us
  local copies, waits for them, and re-layouts: 11 us -> 5.21 us
    all_gather x3 -> x0, waiting for transfers between devices: 318 us -> none  [the longest x1 147 us: local(): lax.all_gather(query_rows, 'fsdp', axis=0, tiled=True)]
    dot_general x18 -> x0, matrix products: 53.9 us -> none  [the longest x8 26.4 us: one_head(): jnp.dot(query_head, key_rows.T, preferred_element_type=jnp.float32)]
    ppermute x0 -> x25, waiting for transfers between devices: none -> 49.5 us  [the longest x3 20.4 us: to_rep(): return lax.ppermute(x, 'zl', SWAP)]
    ppermute x0 -> x25, starting transfers between devices: none -> 38.1 us  [the longest x3 7.08 us: gather_plane(): lowers = [lower] + [lax.ppermute(lower, 'x', ring(d)) for d in (1, 3, 2)]]
    psum x1 -> x0, blocking collectives: 30.6 us -> none  [local(): query_sum, pair_sum = lax.psum((query_term, pair_term), 'rep')]
    pallas_call x0 -> x10, Pallas kernels: none -> 17.8 us  [the longest x1 6.21 us: attend(): pl.pallas_call(attend_kernel, in_specs=[sspec()] + [vspec()] * 5, out_spe...]
    reduce_sum x10 -> x0, other arithmetic: 15.3 us -> none  [the longest x8 10.9 us: one_head(): norm_sum = jnp.sum(weights_exp, axis=1, keepdims=True)]
    all_to_all x0 -> x1, starting transfers between devices: none -> 6.21 us  [local(): lax.all_to_all(pair.reshape(128, 32, 128), ('zh', 'x', 'y', 'zl', 'c'), 0...]
  transfers between devices with their start and end apart: 3 -> 26, of which waited for: 3 -> 18; matrix products, arithmetic and copies ran while one was open for 3% -> 1% of each run, Pallas kernels for 0% -> 4%
where the time goes in v2:
time: 118 us
  waiting for transfers between devices  49.5 us (42%)
  starting transfers between devices  44.3 us (38%)
  Pallas kernels  17.8 us (15%)
  local copies, waits for them, and re-layouts  5.21 us (4%)
    ppermute x3, waiting for transfers between devices, to_rep(): return lax.ppermute(x, 'zl', SWAP)  20.4 us
    ppermute x3, starting transfers between devices, gather_plane(): lowers = [lower] + [lax.ppermute(lower, 'x', ring(d)) for d in (1, 3, 2)]  7.08 us
    ppermute x3, waiting for transfers between devices, gather_plane(): lowers = [lower] + [lax.ppermute(lower, 'x', ring(d)) for d in (1, 3, 2)]  6.87 us
    ppermute x1, starting transfers between devices, local(): other = lax.ppermute(got, 'c', SWAP)  6.53 us
    pallas_call x1, Pallas kernels, attend(): pl.pallas_call(attend_kernel, in_specs=[sspec()] + [vspec()] * 5, out_spe...  6.21 us
    all_to_all x1, starting transfers between devices, local(): lax.all_to_all(pair.reshape(128, 32, 128), ('zh', 'x', 'y', 'zl', 'c'), 0...  6.21 us
    pallas_call x2, Pallas kernels, project(): pl.pallas_call(kernel, in_specs=[sspec()] + [vspec()] * (len(args) - 1),...  5.5 us
    ppermute x1, waiting for transfers between devices, local(): back = lax.ppermute(theirs, 'zh', SWAP)  5.18 us
  transfers between devices with their start and end apart: 26, of which 18 were waited for; matrix products, arithmetic and copies ran while one was open for 1% of the time, Pallas kernels for 4%

profile of v2, /device:TPU:1, one launch (start us, length us, event | category | flops | bytes accessed | tf_op | source)
XLA Modules:
  0.0 118.0 jit_solution(13404171806375796345)
XLA Ops:
  0.0 0.1 stack.57.idx
  0.1 1.2 %copy-done.2 = f32[1,256,1024]{2,1,0:T(8,128)S(1)} copy-done((f32[1,256,1024]{2,1,0:T(8,128)S(1)}, f32[1,256,1024]{2,1,0:T(8,128)}, u32[]{:S(2)}) %copy-start.2) | copy-done | bytes 1048600
  1.3 0.9 copy-done.3
  2.3 0.7 copy-done.4
  2.9 1.0 prepare.1
  3.9 1.5 %collective-permute-start = (f32[2,320,256]{2,1,0:T(8,128)S(1)}, f32[2,320,256]{2,1,0:T(8,128)S(1)}, u32[]{:S(2)}, u32[]{:S(2)}) collective-permute-start(f32[2,320,256]{2,1,0:T(8,128)S(1)} %get-tuple-element.32), channel_id=1, source_target_pairs={{0,32},{32,0},{1,33},{33,1},{2,34},{34,2},{3,35},{35,3},{4,36},{36... | collective-permute-start | bytes 1966088 | tf_op jit(solution)/shard_map/ppermute | solution.py:392
  5.4 1.7 %collective-permute-done = f32[2,320,256]{2,1,0:T(8,128)S(1)} collective-permute-done((f32[2,320,256]{2,1,0:T(8,128)S(1)}, f32[2,320,256]{2,1,0:T(8,128)S(1)}, u32[]{:S(2)}, u32[]{:S(2)}) %collective-permute-start) | collective-permute-done | bytes 655392 | tf_op jit(solution)/shard_map/ppermute | solution.py:392
  7.1 0.1 add.35
  7.3 1.8 %collective-permute-start.1 = (bf16[320,256]{1,0:T(8,128)(2,1)S(1)}, bf16[320,256]{1,0:T(8,128)(2,1)S(1)}, u32[]{:S(2)}, u32[]{:S(2)}) collective-permute-start(bf16[320,256]{1,0:T(8,128)(2,1)S(1)} %fusion.1), channel_id=1, source_target_pairs={{0,64},{64,0},{1,65},{65,1},{2,66},{66,2},{3,67},{67,3},{4,68},{68... | collective-permute-start | bytes 491528 | tf_op jit(solution)/shard_map/ppermute | solution.py:395
  9.1 2.2 %copy-done = bf16[256,8192]{1,0:T(8,128)(2,1)S(1)} copy-done((bf16[256,8192]{1,0:T(8,128)(2,1)S(1)}, bf16[256,8192]{1,0:T(8,128)(2,1)}, u32[]{:S(2)}) %copy-start) | copy-done | bytes 4194328
  11.3 1.8 %normalise.1 = (f32[256,128]{1,0:T(8,128)S(1)}, bf16[256,2048]{1,0:T(8,128)(2,1)S(1)}) custom-call(s32[6]{0:T(128)S(1)} %stack.57.idx, bf16[256,8192]{1,0:T(8,128)(2,1)S(1)} %copy-done), custom_call_target="tpu_custom_call" | custom-call | flops 8388608 | bytes 6291456 | tf_op jit(solution)/shard_map/normalise/pallas_call | solution.py:64
  13.0 0.3 collective-permute-done.1
  13.3 0.1 fusion
  13.4 3.2 %collective-permute-start.2 = (bf16[256,2048]{1,0:T(8,128)(2,1)S(1)}, bf16[256,2048]{1,0:T(8,128)(2,1)}, u32[]{:S(2)}, u32[]{:S(2)}) collective-permute-start(bf16[256,2048]{1,0:T(8,128)(2,1)S(1)} %get-tuple-element.33), channel_id=1, source_target_pairs={{0,16},{16,0},{1,17},{17,1},{2,18},{18,2},{3,19},{19,3},{4,20},{20... | collective-permute-start | bytes 3145736 | tf_op jit(solution)/shard_map/ppermute | solution.py:411
  16.6 1.3 %collective-permute-start.6 = (bf16[160,256]{1,0:T(8,128)(2,1)S(1)}, bf16[160,256]{1,0:T(8,128)(2,1)S(1)}, u32[]{:S(2)}, u32[]{:S(2)}) collective-permute-start(bf16[160,256]{1,0:T(8,128)(2,1)S(1)} %get-tuple-element.57), channel_id=1, source_target_pairs={{0,4},{4,8},{8,12},{12,0},{1,5},{5,9},{9,13},{13,1},{2,6},{6,10},{... | collective-permute-start | bytes 245768 | tf_op jit(solution)/shard_map/ppermute | solution.py:130
  17.9 1.5 %collective-permute-start.7 = (bf16[160,256]{1,0:T(8,128)(2,1)S(1)}, bf16[160,256]{1,0:T(8,128)(2,1)S(1)}, u32[]{:S(2)}, u32[]{:S(2)}) collective-permute-start(bf16[160,256]{1,0:T(8,128)(2,1)S(1)} %get-tuple-element.57), channel_id=1, source_target_pairs={{0,12},{4,0},{8,4},{12,8},{1,13},{5,1},{9,5},{13,9},{2,14},{6,2},{... | collective-permute-start | bytes 245768 | tf_op jit(solution)/shard_map/ppermute | solution.py:130
  19.3 1.5 %collective-permute-start.8 = (bf16[160,256]{1,0:T(8,128)(2,1)S(1)}, bf16[160,256]{1,0:T(8,128)(2,1)S(1)}, u32[]{:S(2)}, u32[]{:S(2)}) collective-permute-start(bf16[160,256]{1,0:T(8,128)(2,1)S(1)} %get-tuple-element.57), channel_id=1, source_target_pairs={{0,8},{4,12},{8,0},{12,4},{1,9},{5,13},{9,1},{13,5},{2,10},{6,14},... | collective-permute-start | bytes 245768 | tf_op jit(solution)/shard_map/ppermute | solution.py:130
  20.9 2.7 %collective-permute-start.4 = (bf16[160,256]{1,0:T(8,128)(2,1)S(1)}, bf16[160,256]{1,0:T(8,128)(2,1)S(1)}, u32[]{:S(2)}, u32[]{:S(2)}) collective-permute-start(bf16[160,256]{1,0:T(8,128)(2,1)S(1)} %get-tuple-element.58), channel_id=1, source_target_pairs={{0,3},{1,0},{2,1},{3,2},{4,7},{5,4},{6,5},{7,6},{8,11},{9,8},{10,9... | collective-permute-start | bytes 245768 | tf_op jit(solution)/shard_map/ppermute | solution.py:129
  23.6 0.9 collective-permute-start.5
  24.5 0.0 collective-permute-done.7
  24.5 0.4 collective-permute-start.3
  24.9 0.5 collective-permute-done.8
  25.4 3.4 %collective-permute-done.5 = bf16[160,256]{1,0:T(8,128)(2,1)S(1)} collective-permute-done((bf16[160,256]{1,0:T(8,128)(2,1)S(1)}, bf16[160,256]{1,0:T(8,128)(2,1)S(1)}, u32[]{:S(2)}, u32[]{:S(2)}) %collective-permute-start.5) | collective-permute-done | bytes 81952 | tf_op jit(solution)/shard_map/ppermute | solution.py:129
  28.8 0.9 collective-permute-done.3
  29.7 1.0 collective-permute-start.10
  30.8 1.1 collective-permute-start.11
  31.9 2.7 %collective-permute-start.13 = (bf16[4,160,256]{2,1,0:T(8,128)(2,1)S(1)}, bf16[4,160,256]{2,1,0:T(8,128)(2,1)S(1)}, u32[]{:S(2)}, u32[]{:S(2)}) collective-permute-start(bf16[4,160,256]{2,1,0:T(8,128)(2,1)S(1)} %pad_maximum_fusion.1.refs_4_), channel_id=1, source_target_pairs={{0,3},{1,0},{2,1},{3,2},{4,7},{5,4},{6,5},{7,6},{8,11},{9,8},{10,9... | collective-permute-start | bytes 983048 | tf_op jit(solution)/shard_map/ppermute | solution.py:133
  34.6 1.5 %collective-permute-done.10.refs_2_ = bf16[4,160,256]{2,1,0:T(8,128)(2,1)S(1)} collective-permute-done((bf16[4,160,256]{2,1,0:T(8,128)(2,1)S(1)}, bf16[4,160,256]{2,1,0:T(8,128)(2,1)S(1)}, u32[]{:S(2)}, u32[]{:S(2)}) %collective-permute-start.10) | collective-permute-done | bytes 327712 | tf_op jit(solution)/shard_map/ppermute | solution.py:132
  36.1 0.9 collective-permute-start.14
  37.0 1.6 %collective-permute-done.11.refs_3_ = bf16[4,160,256]{2,1,0:T(8,128)(2,1)S(1)} collective-permute-done((bf16[4,160,256]{2,1,0:T(8,128)(2,1)S(1)}, bf16[4,160,256]{2,1,0:T(8,128)(2,1)S(1)}, u32[]{:S(2)}, u32[]{:S(2)}) %collective-permute-start.11) | collective-permute-done | bytes 327712 | tf_op jit(solution)/shard_map/ppermute | solution.py:132
  38.6 4.9 %collective-permute-start.9 = (bf16[4,160,256]{2,1,0:T(8,128)(2,1)S(1)}, bf16[4,160,256]{2,1,0:T(8,128)(2,1)S(1)}, u32[]{:S(2)}, u32[]{:S(2)}) collective-permute-start(bf16[4,160,256]{2,1,0:T(8,128)(2,1)S(1)} %pad_maximum_fusion.refs_0_), channel_id=1, source_target_pairs={{0,4},{4,8},{8,12},{12,0},{1,5},{5,9},{9,13},{13,1},{2,6},{6,10},{... | collective-permute-start | bytes 983048 | tf_op jit(solution)/shard_map/ppermute | solution.py:132
  43.5 2.3 %collective-permute-done.14.refs_7_ = bf16[4,160,256]{2,1,0:T(8,128)(2,1)S(1)} collective-permute-done((bf16[4,160,256]{2,1,0:T(8,128)(2,1)S(1)}, bf16[4,160,256]{2,1,0:T(8,128)(2,1)S(1)}, u32[]{:S(2)}, u32[]{:S(2)}) %collective-permute-start.14) | collective-permute-done | bytes 327712 | tf_op jit(solution)/shard_map/ppermute | solution.py:133
  45.8 3.7 %collective-permute-done.9.refs_1_ = bf16[4,160,256]{2,1,0:T(8,128)(2,1)S(1)} collective-permute-done((bf16[4,160,256]{2,1,0:T(8,128)(2,1)S(1)}, bf16[4,160,256]{2,1,0:T(8,128)(2,1)S(1)}, u32[]{:S(2)}, u32[]{:S(2)}) %collective-permute-start.9) | collective-permute-done | bytes 327712 | tf_op jit(solution)/shard_map/ppermute | solution.py:132
  49.5 6.5 %collective-permute-start.15 = (bf16[256,2048]{1,0:T(8,128)(2,1)}, bf16[256,2048]{1,0:T(8,128)(2,1)}, u32[]{:S(2)}, u32[]{:S(2)}) collective-permute-start(bf16[256,2048]{1,0:T(8,128)(2,1)} %collective-permute-done.2.refs_8_), channel_id=1, source_target_pairs={{0,32},{32,0},{1,33},{33,1},{2,34},{34,2},{3,35},{35,3},{4,36},{36... | collective-permute-start | bytes 3145736 | tf_op jit(solution)/shard_map/ppermute | solution.py:413
  56.1 0.1 dynamic_slice.3
  56.2 2.5 %collective-permute-done.15.refs_9_ = bf16[256,2048]{1,0:T(8,128)(2,1)} collective-permute-done((bf16[256,2048]{1,0:T(8,128)(2,1)}, bf16[256,2048]{1,0:T(8,128)(2,1)}, u32[]{:S(2)}, u32[]{:S(2)}) %collective-permute-start.15) | collective-permute-done | bytes 1048608 | tf_op jit(solution)/shard_map/ppermute | solution.py:413
  58.7 3.2 %theirs.1 = bf16[384,256]{1,0:T(8,128)(2,1)S(1)} custom-call(s32[6]{0:T(128)S(1)} %stack.57.idx, bf16[4,160,256]{2,1,0:T(8,128)(2,1)S(1)} %pad_maximum_fusion.refs_0_, bf16[4,160,256]{2,1,0:T(8,128)(2,1)S(1)} %collective-permute-done.9.refs_1_, bf16[4,160,256]{2,1,0:T(8,128)(2,1)S(1)} %collective-permute-done.10.refs_2_, ...), custom_call_target="tpu_custom_call" | custom-call | flops 671088640 | bytes 5242880 | tf_op jit(solution)/shard_map/theirs/pallas_call | solution.py:189
  62.0 0.1 collective-permute-start.16
  62.1 0.1 multiply_sine_fusion.1
  62.2 2.3 %own.1 = (f32[256,256]{1,0:T(8,128)S(1)}, f32[64,256]{1,0:T(8,128)S(1)}) custom-call(s32[6]{0:T(128)S(1)} %stack.57.idx, bf16[4,160,256]{2,1,0:T(8,128)(2,1)S(1)} %pad_maximum_fusion.refs_0_, bf16[4,160,256]{2,1,0:T(8,128)(2,1)S(1)} %collective-permute-done.9.refs_1_, bf16[4,160,256]{2,1,0:T(8,128)(2,1)S(1)} %collective-permute-done.10.refs_2_, ...), custom_call_target="tpu_custom_call" | custom-call | flops 671088640 | bytes 5242880 | tf_op jit(solution)/shard_map/own/pallas_call | solution.py:189
  64.5 5.2 %collective-permute-done.16.got_ref = bf16[384,256]{1,0:T(8,128)(2,1)S(1)} collective-permute-done((bf16[384,256]{1,0:T(8,128)(2,1)S(1)}, bf16[384,256]{1,0:T(8,128)(2,1)S(1)}, u32[]{:S(2)}, u32[]{:S(2)}) %collective-permute-start.16) | collective-permute-done | bytes 196640 | tf_op jit(solution)/shard_map/ppermute | solution.py:428
  69.7 1.2 pair_finish.1
  70.8 6.2 %all-to-all-start = ((bf16[128,32,128]{2,1,0:T(8,128)(2,1)}), bf16[128,32,128]{2,1,0:T(8,128)(2,1)S(1)}, u32[]{:S(2)}, u32[]{:S(2)}) async-start(bf16[128,32,128]{2,1,0:T(8,128)(2,1)} %bitcast.16), calls=%async_computation | async-start | bytes 2097152 | tf_op jit(solution)/shard_map/all_to_all | solution.py:434
  77.0 0.5 multiply_sine_fusion
  77.6 0.4 q_finish.1.refs_0_
  78.0 1.1 collective-permute-start.17
  79.1 0.8 collective-permute-start.18
  79.9 0.9 collective-permute-start.19
  80.9 13.5 %collective-permute-done.18.refs_2_ = bf16[2,128,256]{2,1,0:T(8,128)(2,1)S(1)} collective-permute-done((bf16[2,128,256]{2,1,0:T(8,128)(2,1)S(1)}, bf16[2,128,256]{2,1,0:T(8,128)(2,1)S(1)}, u32[]{:S(2)}, u32[]{:S(2)}) %collective-permute-start.18) | collective-permute-done | bytes 131104 | tf_op jit(solution)/shard_map/ppermute | solution.py:387
  94.4 3.0 %collective-permute-done.19.refs_3_ = bf16[2,128,256]{2,1,0:T(8,128)(2,1)S(1)} collective-permute-done((bf16[2,128,256]{2,1,0:T(8,128)(2,1)S(1)}, bf16[2,128,256]{2,1,0:T(8,128)(2,1)S(1)}, u32[]{:S(2)}, u32[]{:S(2)}) %collective-permute-start.19) | collective-permute-done | bytes 131104 | tf_op jit(solution)/shard_map/ppermute | solution.py:388
  97.4 6.2 %attend.1 = (bf16[288,256]{1,0:T(8,128)(2,1)S(1)}, bf16[288,256]{1,0:T(8,128)(2,1)S(1)}, bf16[288,256]{1,0:T(8,128)(2,1)S(1)}, bf16[288,256]{1,0:T(8,128)(2,1)S(1)}) custom-call(s32[6]{0:T(128)S(1)} %stack.57.idx, bf16[2,128,256]{2,1,0:T(8,128)(2,1)S(1)} %q_finish.1.refs_0_, bf16[2,128,256]{2,1,0:T(8,128)(2,1)S(1)} %collective-permute-done.17.refs_1_, ...), custom_call_target="tpu_custom_call" | custom-call | flops 2147483648 | bytes 4194304 | tf_op jit(solution)/shard_map/attend/pallas_call | solution.py:305
  103.6 0.5 collective-permute-start.20
  104.1 0.1 collective-permute-start.21
  104.2 0.9 collective-permute-done.20.b0
  105.1 0.4 collective-permute-done.21.b1
  105.4 0.2 merge.1
  105.6 0.4 collective-permute-start.22
  106.0 1.2 collective-permute-start.23
  107.1 3.8 %collective-permute-done.22.b0 = bf16[288,256]{1,0:T(8,128)(2,1)S(1)} collective-permute-done((bf16[288,256]{1,0:T(8,128)(2,1)S(1)}, bf16[288,256]{1,0:T(8,128)(2,1)S(1)}, u32[]{:S(2)}, u32[]{:S(2)}) %collective-permute-start.22) | collective-permute-done | bytes 147488 | tf_op jit(solution)/shard_map/ppermute | solution.py:387
  110.9 3.2 %collective-permute-done.23.b1 = bf16[288,256]{1,0:T(8,128)(2,1)S(1)} collective-permute-done((bf16[288,256]{1,0:T(8,128)(2,1)S(1)}, bf16[288,256]{1,0:T(8,128)(2,1)S(1)}, u32[]{:S(2)}, u32[]{:S(2)}) %collective-permute-start.23) | collective-permute-done | bytes 147488 | tf_op jit(solution)/shard_map/ppermute | solution.py:387
  114.1 0.2 last.1.mine_ref
  114.3 1.1 collective-permute-start.24
  115.4 1.2 collective-permute-done.24.other_ref
  116.6 1.4 %place.1 = bf16[256,1024]{1,0:T(8,128)(2,1)} custom-call(s32[6]{0:T(128)S(1)} %stack.57.idx, bf16[256,512]{1,0:T(8,128)(2,1)S(1)} %last.1.mine_ref, bf16[256,512]{1,0:T(8,128)(2,1)S(1)} %collective-permute-done.24.other_ref), custom_call_target="tpu_custom_call" | custom-call | flops 524288 | bytes 1048576 | tf_op jit(solution)/shard_map/place/pallas_call | solution.py:369
  (20 shorter events, 0.2 us)
Async XLA Ops:
  0.1 1.2 %copy-start.2 = (f32[1,256,1024]{2,1,0:T(8,128)S(1)}, f32[1,256,1024]{2,1,0:T(8,128)}, u32[]{:S(2)}) copy-start(f32[1,256,1024]{2,1,0:T(8,128)} %q_ref.1) | copy-start | bytes 3145732
  1.3 0.9 copy-start.3
  2.3 0.7 copy-start.4
  3.9 3.2 %collective-permute-start = (f32[2,320,256]{2,1,0:T(8,128)S(1)}, f32[2,320,256]{2,1,0:T(8,128)S(1)}, u32[]{:S(2)}, u32[]{:S(2)}) collective-permute-start(f32[2,320,256]{2,1,0:T(8,128)S(1)} %get-tuple-element.32), channel_id=1, source_target_pairs={{0,32},{32,0},{1,33},{33,1},{2,34},{34,2},{3,35},{35,3},{4,36},{36... | collective-permute-start | bytes 1966088 | tf_op jit(solution)/shard_map/ppermute | solution.py:392
  7.3 6.0 %collective-permute-start.1 = (bf16[320,256]{1,0:T(8,128)(2,1)S(1)}, bf16[320,256]{1,0:T(8,128)(2,1)S(1)}, u32[]{:S(2)}, u32[]{:S(2)}) collective-permute-start(bf16[320,256]{1,0:T(8,128)(2,1)S(1)} %fusion.1), channel_id=1, source_target_pairs={{0,64},{64,0},{1,65},{65,1},{2,66},{66,2},{3,67},{67,3},{4,68},{68... | collective-permute-start | bytes 491528 | tf_op jit(solution)/shard_map/ppermute | solution.py:395
  9.1 2.2 %copy-start = (bf16[256,8192]{1,0:T(8,128)(2,1)S(1)}, bf16[256,8192]{1,0:T(8,128)(2,1)}, u32[]{:S(2)}) copy-start(bf16[256,8192]{1,0:T(8,128)(2,1)} %refs_8_.1) | copy-start | bytes 12582916
  13.4 36.2 %collective-permute-start.2 = (bf16[256,2048]{1,0:T(8,128)(2,1)S(1)}, bf16[256,2048]{1,0:T(8,128)(2,1)}, u32[]{:S(2)}, u32[]{:S(2)}) collective-permute-start(bf16[256,2048]{1,0:T(8,128)(2,1)S(1)} %get-tuple-element.33), channel_id=1, source_target_pairs={{0,16},{16,0},{1,17},{17,1},{2,18},{18,2},{3,19},{19,3},{4,20},{20... | collective-permute-start | bytes 3145736 | tf_op jit(solution)/shard_map/ppermute | solution.py:411
  16.6 7.0 %collective-permute-start.6 = (bf16[160,256]{1,0:T(8,128)(2,1)S(1)}, bf16[160,256]{1,0:T(8,128)(2,1)S(1)}, u32[]{:S(2)}, u32[]{:S(2)}) collective-permute-start(bf16[160,256]{1,0:T(8,128)(2,1)S(1)} %get-tuple-element.57), channel_id=1, source_target_pairs={{0,4},{4,8},{8,12},{12,0},{1,5},{5,9},{9,13},{13,1},{2,6},{6,10},{... | collective-permute-start | bytes 245768 | tf_op jit(solution)/shard_map/ppermute | solution.py:130
  17.9 6.6 %collective-permute-start.7 = (bf16[160,256]{1,0:T(8,128)(2,1)S(1)}, bf16[160,256]{1,0:T(8,128)(2,1)S(1)}, u32[]{:S(2)}, u32[]{:S(2)}) collective-permute-start(bf16[160,256]{1,0:T(8,128)(2,1)S(1)} %get-tuple-element.57), channel_id=1, source_target_pairs={{0,12},{4,0},{8,4},{12,8},{1,13},{5,1},{9,5},{13,9},{2,14},{6,2},{... | collective-permute-start | bytes 245768 | tf_op jit(solution)/shard_map/ppermute | solution.py:130
  19.3 6.0 %collective-permute-start.8 = (bf16[160,256]{1,0:T(8,128)(2,1)S(1)}, bf16[160,256]{1,0:T(8,128)(2,1)S(1)}, u32[]{:S(2)}, u32[]{:S(2)}) collective-permute-start(bf16[160,256]{1,0:T(8,128)(2,1)S(1)} %get-tuple-element.57), channel_id=1, source_target_pairs={{0,8},{4,12},{8,0},{12,4},{1,9},{5,13},{9,1},{13,5},{2,10},{6,14},... | collective-permute-start | bytes 245768 | tf_op jit(solution)/shard_map/ppermute | solution.py:130
  20.9 4.5 %collective-permute-start.4 = (bf16[160,256]{1,0:T(8,128)(2,1)S(1)}, bf16[160,256]{1,0:T(8,128)(2,1)S(1)}, u32[]{:S(2)}, u32[]{:S(2)}) collective-permute-start(bf16[160,256]{1,0:T(8,128)(2,1)S(1)} %get-tuple-element.58), channel_id=1, source_target_pairs={{0,3},{1,0},{2,1},{3,2},{4,7},{5,4},{6,5},{7,6},{8,11},{9,8},{10,9... | collective-permute-start | bytes 245768 | tf_op jit(solution)/shard_map/ppermute | solution.py:129
  23.6 5.2 %collective-permute-start.5 = (bf16[160,256]{1,0:T(8,128)(2,1)S(1)}, bf16[160,256]{1,0:T(8,128)(2,1)S(1)}, u32[]{:S(2)}, u32[]{:S(2)}) collective-permute-start(bf16[160,256]{1,0:T(8,128)(2,1)S(1)} %get-tuple-element.58), channel_id=1, source_target_pairs={{0,2},{1,3},{2,0},{3,1},{4,6},{5,7},{6,4},{7,5},{8,10},{9,11},{10,... | collective-permute-start | bytes 245768 | tf_op jit(solution)/shard_map/ppermute | solution.py:129
  24.5 5.2 %collective-permute-start.3 = (bf16[160,256]{1,0:T(8,128)(2,1)S(1)}, bf16[160,256]{1,0:T(8,128)(2,1)S(1)}, u32[]{:S(2)}, u32[]{:S(2)}) collective-permute-start(bf16[160,256]{1,0:T(8,128)(2,1)S(1)} %get-tuple-element.58), channel_id=1, source_target_pairs={{0,1},{1,2},{2,3},{3,0},{4,5},{5,6},{6,7},{7,4},{8,9},{9,10},{10,1... | collective-permute-start | bytes 245768 | tf_op jit(solution)/shard_map/ppermute | solution.py:129
  29.7 6.4 %collective-permute-start.10 = (bf16[4,160,256]{2,1,0:T(8,128)(2,1)S(1)}, bf16[4,160,256]{2,1,0:T(8,128)(2,1)S(1)}, u32[]{:S(2)}, u32[]{:S(2)}) collective-permute-start(bf16[4,160,256]{2,1,0:T(8,128)(2,1)S(1)} %pad_maximum_fusion.refs_0_), channel_id=1, source_target_pairs={{0,12},{4,0},{8,4},{12,8},{1,13},{5,1},{9,5},{13,9},{2,14},{6,2},{... | collective-permute-start | bytes 983048 | tf_op jit(solution)/shard_map/ppermute | solution.py:132
  30.8 7.8 %collective-permute-start.11 = (bf16[4,160,256]{2,1,0:T(8,128)(2,1)S(1)}, bf16[4,160,256]{2,1,0:T(8,128)(2,1)S(1)}, u32[]{:S(2)}, u32[]{:S(2)}) collective-permute-start(bf16[4,160,256]{2,1,0:T(8,128)(2,1)S(1)} %pad_maximum_fusion.refs_0_), channel_id=1, source_target_pairs={{0,8},{4,12},{8,0},{12,4},{1,9},{5,13},{9,1},{13,5},{2,10},{6,14},... | collective-permute-start | bytes 983048 | tf_op jit(solution)/shard_map/ppermute | solution.py:132
  31.9 11.6 %collective-permute-start.12 = (bf16[4,160,256]{2,1,0:T(8,128)(2,1)S(1)}, bf16[4,160,256]{2,1,0:T(8,128)(2,1)S(1)}, u32[]{:S(2)}, u32[]{:S(2)}) collective-permute-start(bf16[4,160,256]{2,1,0:T(8,128)(2,1)S(1)} %pad_maximum_fusion.1.refs_4_), channel_id=1, source_target_pairs={{0,1},{1,2},{2,3},{3,0},{4,5},{5,6},{6,7},{7,4},{8,9},{9,10},{10,1... | collective-permute-start | bytes 983048 | tf_op jit(solution)/shard_map/ppermute | solution.py:133
  31.9 11.6 %collective-permute-start.13 = (bf16[4,160,256]{2,1,0:T(8,128)(2,1)S(1)}, bf16[4,160,256]{2,1,0:T(8,128)(2,1)S(1)}, u32[]{:S(2)}, u32[]{:S(2)}) collective-permute-start(bf16[4,160,256]{2,1,0:T(8,128)(2,1)S(1)} %pad_maximum_fusion.1.refs_4_), channel_id=1, source_target_pairs={{0,3},{1,0},{2,1},{3,2},{4,7},{5,4},{6,5},{7,6},{8,11},{9,8},{10,9... | collective-permute-start | bytes 983048 | tf_op jit(solution)/shard_map/ppermute | solution.py:133
  36.1 9.7 %collective-permute-start.14 = (bf16[4,160,256]{2,1,0:T(8,128)(2,1)S(1)}, bf16[4,160,256]{2,1,0:T(8,128)(2,1)S(1)}, u32[]{:S(2)}, u32[]{:S(2)}) collective-permute-start(bf16[4,160,256]{2,1,0:T(8,128)(2,1)S(1)} %pad_maximum_fusion.1.refs_4_), channel_id=1, source_target_pairs={{0,2},{1,3},{2,0},{3,1},{4,6},{5,7},{6,4},{7,5},{8,10},{9,11},{10,... | collective-permute-start | bytes 983048 | tf_op jit(solution)/shard_map/ppermute | solution.py:133
  38.6 10.9 %collective-permute-start.9 = (bf16[4,160,256]{2,1,0:T(8,128)(2,1)S(1)}, bf16[4,160,256]{2,1,0:T(8,128)(2,1)S(1)}, u32[]{:S(2)}, u32[]{:S(2)}) collective-permute-start(bf16[4,160,256]{2,1,0:T(8,128)(2,1)S(1)} %pad_maximum_fusion.refs_0_), channel_id=1, source_target_pairs={{0,4},{4,8},{8,12},{12,0},{1,5},{5,9},{9,13},{13,1},{2,6},{6,10},{... | collective-permute-start | bytes 983048 | tf_op jit(solution)/shard_map/ppermute | solution.py:132
  49.5 9.2 %collective-permute-start.15 = (bf16[256,2048]{1,0:T(8,128)(2,1)}, bf16[256,2048]{1,0:T(8,128)(2,1)}, u32[]{:S(2)}, u32[]{:S(2)}) collective-permute-start(bf16[256,2048]{1,0:T(8,128)(2,1)} %collective-permute-done.2.refs_8_), channel_id=1, source_target_pairs={{0,32},{32,0},{1,33},{33,1},{2,34},{34,2},{3,35},{35,3},{4,36},{36... | collective-permute-start | bytes 3145736 | tf_op jit(solution)/shard_map/ppermute | solution.py:413
  56.1 6.1 %copy-start.1 = (bf16[256,8192]{1,0:T(8,128)(2,1)S(1)}, bf16[256,8192]{1,0:T(8,128)(2,1)}, u32[]{:S(2)}) copy-start(bf16[256,8192]{1,0:T(8,128)(2,1)} %refs_8_.1) | copy-start | bytes 12582916
  62.0 7.7 %collective-permute-start.16 = (bf16[384,256]{1,0:T(8,128)(2,1)S(1)}, bf16[384,256]{1,0:T(8,128)(2,1)S(1)}, u32[]{:S(2)}, u32[]{:S(2)}) collective-permute-start(bf16[384,256]{1,0:T(8,128)(2,1)S(1)} %theirs.1), channel_id=1, source_target_pairs={{0,16},{16,0},{1,17},{17,1},{2,18},{18,2},{3,19},{19,3},{4,20},{20... | collective-permute-start | bytes 589832 | tf_op jit(solution)/shard_map/ppermute | solution.py:428
  70.8 26.5 %all-to-all-start = ((bf16[128,32,128]{2,1,0:T(8,128)(2,1)}), bf16[128,32,128]{2,1,0:T(8,128)(2,1)S(1)}, u32[]{:S(2)}, u32[]{:S(2)}) async-start(bf16[128,32,128]{2,1,0:T(8,128)(2,1)} %bitcast.16), calls=%async_computation | async-start | bytes 2097152 | tf_op jit(solution)/shard_map/all_to_all | solution.py:434
  78.0 2.9 %collective-permute-start.17 = (bf16[2,128,256]{2,1,0:T(8,128)(2,1)S(1)}, bf16[2,128,256]{2,1,0:T(8,128)(2,1)S(1)}, u32[]{:S(2)}, u32[]{:S(2)}) collective-permute-start(bf16[2,128,256]{2,1,0:T(8,128)(2,1)S(1)} %q_finish.1.refs_0_), channel_id=1, source_target_pairs={{0,32},{32,0},{1,33},{33,1},{2,34},{34,2},{3,35},{35,3},{4,36},{36... | collective-permute-start | bytes 393224 | tf_op jit(solution)/shard_map/ppermute | solution.py:385
  79.1 15.2 %collective-permute-start.18 = (bf16[2,128,256]{2,1,0:T(8,128)(2,1)S(1)}, bf16[2,128,256]{2,1,0:T(8,128)(2,1)S(1)}, u32[]{:S(2)}, u32[]{:S(2)}) collective-permute-start(bf16[2,128,256]{2,1,0:T(8,128)(2,1)S(1)} %q_finish.1.refs_0_), channel_id=1, source_target_pairs={{0,64},{64,0},{1,65},{65,1},{2,66},{66,2},{3,67},{67,3},{4,68},{68... | collective-permute-start | bytes 393224 | tf_op jit(solution)/shard_map/ppermute | solution.py:387
  79.9 17.4 %collective-permute-start.19 = (bf16[2,128,256]{2,1,0:T(8,128)(2,1)S(1)}, bf16[2,128,256]{2,1,0:T(8,128)(2,1)S(1)}, u32[]{:S(2)}, u32[]{:S(2)}) collective-permute-start(bf16[2,128,256]{2,1,0:T(8,128)(2,1)S(1)} %q_finish.1.refs_0_), channel_id=1, source_target_pairs={{0,96},{32,64},{64,32},{96,0},{1,97},{33,65},{65,33},{97,1},{2,98}... | collective-permute-start | bytes 393224 | tf_op jit(solution)/shard_map/ppermute | solution.py:388
  103.6 1.5 %collective-permute-start.20 = (bf16[288,256]{1,0:T(8,128)(2,1)S(1)}, bf16[288,256]{1,0:T(8,128)(2,1)S(1)}, u32[]{:S(2)}, u32[]{:S(2)}) collective-permute-start(bf16[288,256]{1,0:T(8,128)(2,1)S(1)} %get-tuple-element.51), channel_id=1, source_target_pairs={{0,32},{32,0},{1,33},{33,1},{2,34},{34,2},{3,35},{35,3},{4,36},{36... | collective-permute-start | bytes 442376 | tf_op jit(solution)/shard_map/ppermute | solution.py:385
  104.1 1.4 %collective-permute-start.21 = (bf16[288,256]{1,0:T(8,128)(2,1)S(1)}, bf16[288,256]{1,0:T(8,128)(2,1)S(1)}, u32[]{:S(2)}, u32[]{:S(2)}) collective-permute-start(bf16[288,256]{1,0:T(8,128)(2,1)S(1)} %get-tuple-element.52), channel_id=1, source_target_pairs={{0,32},{32,0},{1,33},{33,1},{2,34},{34,2},{3,35},{35,3},{4,36},{36... | collective-permute-start | bytes 442376 | tf_op jit(solution)/shard_map/ppermute | solution.py:385
  105.6 5.3 %collective-permute-start.22 = (bf16[288,256]{1,0:T(8,128)(2,1)S(1)}, bf16[288,256]{1,0:T(8,128)(2,1)S(1)}, u32[]{:S(2)}, u32[]{:S(2)}) collective-permute-start(bf16[288,256]{1,0:T(8,128)(2,1)S(1)} %get-tuple-element.54.a1), channel_id=1, source_target_pairs={{0,64},{64,0},{1,65},{65,1},{2,66},{66,2},{3,67},{67,3},{4,68},{68... | collective-permute-start | bytes 442376 | tf_op jit(solution)/shard_map/ppermute | solution.py:387
  106.0 8.1 %collective-permute-start.23 = (bf16[288,256]{1,0:T(8,128)(2,1)S(1)}, bf16[288,256]{1,0:T(8,128)(2,1)S(1)}, u32[]{:S(2)}, u32[]{:S(2)}) collective-permute-start(bf16[288,256]{1,0:T(8,128)(2,1)S(1)} %get-tuple-element.53.a0), channel_id=1, source_target_pairs={{0,64},{64,0},{1,65},{65,1},{2,66},{66,2},{3,67},{67,3},{4,68},{68... | collective-permute-start | bytes 442376 | tf_op jit(solution)/shard_map/ppermute | solution.py:387
  114.3 2.3 %collective-permute-start.24 = (bf16[256,512]{1,0:T(8,128)(2,1)S(1)}, bf16[256,512]{1,0:T(8,128)(2,1)S(1)}, u32[]{:S(2)}, u32[]{:S(2)}) collective-permute-start(bf16[256,512]{1,0:T(8,128)(2,1)S(1)} %last.1.mine_ref), channel_id=1, source_target_pairs={{0,32},{32,0},{1,33},{33,1},{2,34},{34,2},{3,35},{35,3},{4,36},{36... | collective-permute-start | bytes 786440 | tf_op jit(solution)/shard_map/ppermute | solution.py:385

commit v3 on v2

--- a/solution.py
+++ b/solution.py
@@ -172,7 +172,10 @@
 
 
 def theirs_kernel(idx, *refs):
-    w_refs, (xa_ref, xb_ref, out_ref) = refs[:-3], refs[-3:]
+    w_refs, xa_ref, xb_refs, (out_ref, xb_ref) = refs[:8], refs[8], refs[9:-2], refs[-2:]
+    width = xb_refs[0].shape[1]
+    for i, ref in enumerate(xb_refs):
+        xb_ref[:, i * width:(i + 1) * width] = ref[...]
 
     def block(at):
         cols = pl.ds(pl.multiple_of((at % 8) * 256, 256), 256)
@@ -185,9 +188,10 @@
     out_ref[320:384] = (pair - high.astype(F32)).astype(BF16)
 
 
-def project(kernel, args, outs, name):
+def project(kernel, args, outs, name, scratch=()):
     return pl.pallas_call(
         kernel,
+        scratch_shapes=scratch,
         in_specs=[sspec()] + [vspec()] * (len(args) - 1),
         out_specs=[vspec()] * len(outs),
         out_shape=outs,
@@ -409,8 +413,8 @@
     w = (w_mine + w_got.astype(F32)).astype(BF16)
     w_all = gather_plane(w)
     got = lax.ppermute(out, "zh", SWAP)
-    got, *w_all = lax.optimization_barrier((got, *w_all))
-    other = lax.ppermute(got, "c", SWAP)
+    width = got.shape[1] // 4
+    other = [lax.ppermute(got[:, i * width:(i + 1) * width], "c", SWAP) for i in range(4)]
 
     inverse_freq = jnp.exp(
         -(jnp.arange(64, dtype=F32) * (2.0 / HEAD)) * math.log(theta_base)
@@ -423,8 +427,8 @@
     cos_t, sin_t = jnp.cos(angles_t), jnp.sin(angles_t)
 
     (theirs,) = project(
-        theirs_kernel, (idx, *w_all, got, other), [jax.ShapeDtypeStruct((384, 256), BF16)],
-        "theirs")
+        theirs_kernel, (idx, *w_all, got, *other), [jax.ShapeDtypeStruct((384, 256), BF16)],
+        "theirs", [VMEM((256, 2048), BF16)])
     back = lax.ppermute(theirs, "zh", SWAP)
     q_own, pair_own = project(
         own_kernel, (idx, *w_all, tokens, scale),
@@ -434,7 +438,8 @@
     pair_all = lax.all_to_all(
         pair.reshape(128, 32, 128), ("zh", "x", "y", "zl", "c"), 0, 0)
     q0 = finish(q_finish_kernel, (q_own, back, cos, sin), (2, 128, 256), "q_finish")
-    qs = [q0] + [to_rep(q0, m) for m in (1, 2, 3)]
+    q1, q2 = to_rep(q0, 1), to_rep(q0, 2)
+    qs = [q0, q1, q2, to_rep(q2, 1)]
 
     parts = attend(idx, qs, pair_all.reshape(32, 4, 32, 128))
     stat = (2 * STAT, 256)

time: 118 us -> 111 us (0.941)
  waiting for transfers between devices: 49.5 us -> 40.5 us
  local copies, waits for them, and re-layouts: 5.21 us -> 7.84 us
  starting transfers between devices: 44.3 us -> 43.1 us
    ppermute x2 -> x4, waiting for transfers between devices: 5.52 us -> 1.5 us  [local(): lax.ppermute(got[:, i * width:(i + 1) * width], 'c', SWAP)]
    ppermute x3, waiting for transfers between devices: 6.87 us -> 3.61 us  [gather_plane(): lowers = [lower] + [lax.ppermute(lower, 'x', ring(d)) for d in (1, 3, 2)]]
    ppermute x3, starting transfers between devices: 7.08 us -> 4.31 us  [gather_plane(): lowers = [lower] + [lax.ppermute(lower, 'x', ring(d)) for d in (1, 3, 2)]]
    ppermute x3, waiting for transfers between devices: 2.31 us -> 0.01 us  [gather_plane(): uppers = [upper] + [lax.ppermute(upper, 'y', ring(d)) for d in (1, 3, 2)]]
    unnamed x10 -> x18, local copies, waits for them, and re-layouts: 5.02 us -> 6.67 us
    ppermute x4 -> x5, waiting for transfers between devices: 2.42 us -> 3.43 us  [to_rep(): return lax.ppermute(x, 'c', SWAP)]
    ppermute x2 -> x4, starting transfers between devices: 7.46 us -> 8.33 us  [local(): lax.ppermute(got[:, i * width:(i + 1) * width], 'c', SWAP)]
    ppermute x4 -> x5, starting transfers between devices: 2.84 us -> 3.55 us  [to_rep(): return lax.ppermute(x, 'c', SWAP)]
  transfers between devices with their start and end apart: 26 -> 29, of which waited for: 18 -> 19; matrix products, arithmetic and copies ran while one was open for 1% -> 2% of each run, Pallas kernels for 4% -> 4%
where the time goes in v3:
time: 111 us
  starting transfers between devices  43.1 us (39%)
  waiting for transfers between devices  40.5 us (36%)
  Pallas kernels  18.1 us (16%)
  local copies, waits for them, and re-layouts  7.84 us (7%)
    ppermute x3, waiting for transfers between devices, to_rep(): return lax.ppermute(x, 'zl', SWAP)  20.1 us
    ppermute x4, starting transfers between devices, local(): lax.ppermute(got[:, i * width:(i + 1) * width], 'c', SWAP)  8.33 us
    unnamed x18, local copies, waits for them, and re-layouts  6.67 us
    all_to_all x1, starting transfers between devices, local(): lax.all_to_all(pair.reshape(128, 32, 128), ('zh', 'x', 'y', 'zl', 'c'), 0...  6.43 us
    pallas_call x1, Pallas kernels, attend(): pl.pallas_call(attend_kernel, in_specs=[sspec()] + [vspec()] * 5, out_spe...  6.21 us
    pallas_call x2, Pallas kernels, project(): pl.pallas_call(kernel, scratch_shapes=scratch, in_specs=[sspec()] + [vspe...  5.77 us
    ppermute x3, starting transfers between devices, gather_plane(): lowers = [lower] + [lax.ppermute(lower, 'x', ring(d)) for d in (1, 3, 2)]  4.31 us
    ppermute x3, starting transfers between devices, gather_plane(): lax.ppermute(upper, 'x', ring(d))  4.28 us
  transfers between devices with their start and end apart: 29, of which 19 were waited for; matrix products, arithmetic and copies ran while one was open for 2% of the time, Pallas kernels for 4%

profile of v3, /device:TPU:1, one launch (start us, length us, event | category | flops | bytes accessed | tf_op | source)
XLA Modules:
  0.0 110.7 jit_solution(14518921433621046998)
XLA Ops:
  0.1 1.2 %copy-done.2 = f32[1,256,1024]{2,1,0:T(8,128)S(1)} copy-done((f32[1,256,1024]{2,1,0:T(8,128)S(1)}, f32[1,256,1024]{2,1,0:T(8,128)}, u32[]{:S(2)}) %copy-start.2) | copy-done | bytes 1048600
  1.3 0.9 copy-done.5
  2.3 0.7 copy-done.8
  2.9 1.0 prepare.1
  3.9 1.5 %collective-permute-start = (f32[2,320,256]{2,1,0:T(8,128)S(1)}, f32[2,320,256]{2,1,0:T(8,128)S(1)}, u32[]{:S(2)}, u32[]{:S(2)}) collective-permute-start(f32[2,320,256]{2,1,0:T(8,128)S(1)} %get-tuple-element.22), channel_id=1, source_target_pairs={{0,32},{32,0},{1,33},{33,1},{2,34},{34,2},{3,35},{35,3},{4,36},{36... | collective-permute-start | bytes 1966088 | tf_op jit(solution)/shard_map/ppermute | solution.py:396
  5.4 1.7 %collective-permute-done = f32[2,320,256]{2,1,0:T(8,128)S(1)} collective-permute-done((f32[2,320,256]{2,1,0:T(8,128)S(1)}, f32[2,320,256]{2,1,0:T(8,128)S(1)}, u32[]{:S(2)}, u32[]{:S(2)}) %collective-permute-start) | collective-permute-done | bytes 655392 | tf_op jit(solution)/shard_map/ppermute | solution.py:396
  7.3 1.8 %collective-permute-start.1 = (bf16[320,256]{1,0:T(8,128)(2,1)S(1)}, bf16[320,256]{1,0:T(8,128)(2,1)S(1)}, u32[]{:S(2)}, u32[]{:S(2)}) collective-permute-start(bf16[320,256]{1,0:T(8,128)(2,1)S(1)} %fusion.1), channel_id=1, source_target_pairs={{0,64},{64,0},{1,65},{65,1},{2,66},{66,2},{3,67},{67,3},{4,68},{68... | collective-permute-start | bytes 491528 | tf_op jit(solution)/shard_map/ppermute | solution.py:399
  9.1 2.2 %copy-done = bf16[256,8192]{1,0:T(8,128)(2,1)S(1)} copy-done((bf16[256,8192]{1,0:T(8,128)(2,1)S(1)}, bf16[256,8192]{1,0:T(8,128)(2,1)}, u32[]{:S(2)}) %copy-start) | copy-done | bytes 4194328
  11.3 1.8 %normalise.1 = (f32[256,128]{1,0:T(8,128)S(1)}, bf16[256,2048]{1,0:T(8,128)(2,1)S(1)}) custom-call(s32[6]{0:T(128)S(1)} %stack.57.idx, bf16[256,8192]{1,0:T(8,128)(2,1)S(1)} %copy-done), custom_call_target="tpu_custom_call" | custom-call | flops 8388608 | bytes 6291456 | tf_op jit(solution)/shard_map/normalise/pallas_call | solution.py:64
  13.0 0.3 collective-permute-done.1
  13.3 3.1 %collective-permute-start.14 = (bf16[256,2048]{1,0:T(8,128)(2,1)S(1)}, bf16[256,2048]{1,0:T(8,128)(2,1)S(1)}, u32[]{:S(2)}, u32[]{:S(2)}) collective-permute-start(bf16[256,2048]{1,0:T(8,128)(2,1)S(1)} %get-tuple-element.29), channel_id=1, source_target_pairs={{0,16},{16,0},{1,17},{17,1},{2,18},{18,2},{3,19},{19,3},{4,20},{20... | collective-permute-start | bytes 3145736 | tf_op jit(solution)/shard_map/ppermute | solution.py:415
  16.5 1.3 %collective-permute-start.5 = (bf16[160,256]{1,0:T(8,128)(2,1)S(1)}, bf16[160,256]{1,0:T(8,128)(2,1)S(1)}, u32[]{:S(2)}, u32[]{:S(2)}) collective-permute-start(bf16[160,256]{1,0:T(8,128)(2,1)S(1)} %get-tuple-element.43), channel_id=1, source_target_pairs={{0,4},{4,8},{8,12},{12,0},{1,5},{5,9},{9,13},{13,1},{2,6},{6,10},{... | collective-permute-start | bytes 245768 | tf_op jit(solution)/shard_map/ppermute | solution.py:130
  17.8 1.5 %collective-permute-start.6 = (bf16[160,256]{1,0:T(8,128)(2,1)S(1)}, bf16[160,256]{1,0:T(8,128)(2,1)S(1)}, u32[]{:S(2)}, u32[]{:S(2)}) collective-permute-start(bf16[160,256]{1,0:T(8,128)(2,1)S(1)} %get-tuple-element.43), channel_id=1, source_target_pairs={{0,12},{4,0},{8,4},{12,8},{1,13},{5,1},{9,5},{13,9},{2,14},{6,2},{... | collective-permute-start | bytes 245768 | tf_op jit(solution)/shard_map/ppermute | solution.py:130
  19.3 1.5 %collective-permute-start.7 = (bf16[160,256]{1,0:T(8,128)(2,1)S(1)}, bf16[160,256]{1,0:T(8,128)(2,1)S(1)}, u32[]{:S(2)}, u32[]{:S(2)}) collective-permute-start(bf16[160,256]{1,0:T(8,128)(2,1)S(1)} %get-tuple-element.43), channel_id=1, source_target_pairs={{0,8},{4,12},{8,0},{12,4},{1,9},{5,13},{9,1},{13,5},{2,10},{6,14},... | collective-permute-start | bytes 245768 | tf_op jit(solution)/shard_map/ppermute | solution.py:130
  20.8 2.7 %collective-permute-start.3 = (bf16[160,256]{1,0:T(8,128)(2,1)S(1)}, bf16[160,256]{1,0:T(8,128)(2,1)S(1)}, u32[]{:S(2)}, u32[]{:S(2)}) collective-permute-start(bf16[160,256]{1,0:T(8,128)(2,1)S(1)} %get-tuple-element.44), channel_id=1, source_target_pairs={{0,3},{1,0},{2,1},{3,2},{4,7},{5,4},{6,5},{7,6},{8,11},{9,8},{10,9... | collective-permute-start | bytes 245768 | tf_op jit(solution)/shard_map/ppermute | solution.py:129
  23.5 0.8 collective-permute-start.4
  24.3 0.4 collective-permute-start.2
  24.7 0.5 collective-permute-done.7
  25.3 3.4 %collective-permute-done.4 = bf16[160,256]{1,0:T(8,128)(2,1)S(1)} collective-permute-done((bf16[160,256]{1,0:T(8,128)(2,1)S(1)}, bf16[160,256]{1,0:T(8,128)(2,1)S(1)}, u32[]{:S(2)}, u32[]{:S(2)}) %collective-permute-start.4) | collective-permute-done | bytes 81952 | tf_op jit(solution)/shard_map/ppermute | solution.py:129
  28.6 0.9 collective-permute-done.2
  29.6 1.5 %collective-permute-start.10 = (bf16[4,160,256]{2,1,0:T(8,128)(2,1)S(1)}, bf16[4,160,256]{2,1,0:T(8,128)(2,1)S(1)}, u32[]{:S(2)}, u32[]{:S(2)}) collective-permute-start(bf16[4,160,256]{2,1,0:T(8,128)(2,1)S(1)} %pad_maximum_fusion.refs_0_), channel_id=1, source_target_pairs={{0,8},{4,12},{8,0},{12,4},{1,9},{5,13},{9,1},{13,5},{2,10},{6,14},... | collective-permute-start | bytes 983048 | tf_op jit(solution)/shard_map/ppermute | solution.py:132
  31.1 2.7 %collective-permute-start.12 = (bf16[4,160,256]{2,1,0:T(8,128)(2,1)S(1)}, bf16[4,160,256]{2,1,0:T(8,128)(2,1)S(1)}, u32[]{:S(2)}, u32[]{:S(2)}) collective-permute-start(bf16[4,160,256]{2,1,0:T(8,128)(2,1)S(1)} %pad_maximum_fusion.1.refs_4_), channel_id=1, source_target_pairs={{0,3},{1,0},{2,1},{3,2},{4,7},{5,4},{6,5},{7,6},{8,11},{9,8},{10,9... | collective-permute-start | bytes 983048 | tf_op jit(solution)/shard_map/ppermute | solution.py:133
  33.8 3.6 %collective-permute-done.10.refs_3_ = bf16[4,160,256]{2,1,0:T(8,128)(2,1)S(1)} collective-permute-done((bf16[4,160,256]{2,1,0:T(8,128)(2,1)S(1)}, bf16[4,160,256]{2,1,0:T(8,128)(2,1)S(1)}, u32[]{:S(2)}, u32[]{:S(2)}) %collective-permute-start.10) | collective-permute-done | bytes 327712 | tf_op jit(solution)/shard_map/ppermute | solution.py:132
  37.4 0.3 collective-permute-start.8
  37.7 1.0 collective-permute-done.14.refs_8_
  38.7 2.5 %collective-permute-start.9 = (bf16[4,160,256]{2,1,0:T(8,128)(2,1)S(1)}, bf16[4,160,256]{2,1,0:T(8,128)(2,1)}, u32[]{:S(2)}, u32[]{:S(2)}) collective-permute-start(bf16[4,160,256]{2,1,0:T(8,128)(2,1)S(1)} %pad_maximum_fusion.refs_0_), channel_id=1, source_target_pairs={{0,12},{4,0},{8,4},{12,8},{1,13},{5,1},{9,5},{13,9},{2,14},{6,2},{... | collective-permute-start | bytes 983048 | tf_op jit(solution)/shard_map/ppermute | solution.py:132
  41.2 1.0 fusion.2
  42.2 7.3 %collective-permute-start.15 = (bf16[256,512]{1,0:T(8,128)(2,1)}, bf16[256,512]{1,0:T(8,128)(2,1)}, u32[]{:S(2)}, u32[]{:S(2)}) collective-permute-start(bf16[256,512]{1,0:T(8,128)(2,1)} %get-tuple-element.40), channel_id=1, source_target_pairs={{0,32},{32,0},{1,33},{33,1},{2,34},{34,2},{3,35},{35,3},{4,36},{36... | collective-permute-start | bytes 786440 | tf_op jit(solution)/shard_map/ppermute | solution.py:417
  49.5 0.5 collective-permute-start.17
  50.0 0.5 collective-permute-start.18
  50.6 0.4 collective-permute-done.15.refs_9_
  51.0 0.4 collective-permute-done.16.refs_10_
  51.4 0.4 collective-permute-done.17.refs_11_
  51.8 0.4 collective-permute-done.18.refs_12_
  52.1 3.1 %theirs.1 = bf16[384,256]{1,0:T(8,128)(2,1)S(1)} custom-call(s32[6]{0:T(128)S(1)} %stack.57.idx, bf16[4,160,256]{2,1,0:T(8,128)(2,1)S(1)} %pad_maximum_fusion.refs_0_, bf16[4,160,256]{2,1,0:T(8,128)(2,1)S(1)} %collective-permute-done.8.refs_1_, bf16[4,160,256]{2,1,0:T(8,128)(2,1)} %collective-permute-done.9.refs_2_, ...), custom_call_target="tpu_custom_call" | custom-call | flops 671088640 | bytes 5242880 | tf_op jit(solution)/shard_map/theirs/pallas_call | solution.py:192
  55.2 0.1 collective-permute-start.19
  55.3 0.1 multiply_sine_fusion.1
  55.5 2.7 %own.1 = (f32[256,256]{1,0:T(8,128)S(1)}, f32[64,256]{1,0:T(8,128)S(1)}) custom-call(s32[6]{0:T(128)S(1)} %stack.57.idx, bf16[4,160,256]{2,1,0:T(8,128)(2,1)S(1)} %pad_maximum_fusion.refs_0_, bf16[4,160,256]{2,1,0:T(8,128)(2,1)S(1)} %collective-permute-done.8.refs_1_, bf16[4,160,256]{2,1,0:T(8,128)(2,1)} %collective-permute-done.9.refs_2_, ...), custom_call_target="tpu_custom_call" | custom-call | flops 671088640 | bytes 5242880 | tf_op jit(solution)/shard_map/own/pallas_call | solution.py:192
  58.2 0.7 copy-done.3
  58.9 4.0 %collective-permute-done.19.got_ref = bf16[384,256]{1,0:T(8,128)(2,1)S(1)} collective-permute-done((bf16[384,256]{1,0:T(8,128)(2,1)S(1)}, bf16[384,256]{1,0:T(8,128)(2,1)S(1)}, u32[]{:S(2)}, u32[]{:S(2)}) %collective-permute-start.19) | collective-permute-done | bytes 196640 | tf_op jit(solution)/shard_map/ppermute | solution.py:432
  62.9 1.2 %pair_finish.1 = bf16[32,4,32,128]{3,2,1,0:T(8,128)(2,1)} custom-call(f32[64,256]{1,0:T(8,128)S(1)} %get-tuple-element.30.own_ref, bf16[384,256]{1,0:T(8,128)(2,1)S(1)} %collective-permute-done.19.got_ref, f32[16,256]{1,0:T(8,128)S(1)} %get-tuple-element.46.cos_ref, f32[16,256]{1,0:T(8,128)S(1)} %get-tuple-element.45.sin_ref), custom_call_target="tpu_custom_call" | custom-call | flops 262144 | bytes 1048576 | tf_op jit(solution)/shard_map/pair_finish/pallas_call | solution.py:228
  64.1 6.4 %all-to-all-start = ((bf16[128,32,128]{2,1,0:T(8,128)(2,1)}), bf16[128,32,128]{2,1,0:T(8,128)(2,1)S(1)}, u32[]{:S(2)}, u32[]{:S(2)}) async-start(bf16[128,32,128]{2,1,0:T(8,128)(2,1)} %bitcast.16), calls=%async_computation | async-start | bytes 2097152 | tf_op jit(solution)/shard_map/all_to_all | solution.py:438
  70.5 0.5 multiply_sine_fusion
  71.1 0.9 copy-done.4
  72.0 0.4 q_finish.1.refs_0_
  72.4 1.6 %collective-permute-start.21 = (bf16[2,128,256]{2,1,0:T(8,128)(2,1)S(1)}, bf16[2,128,256]{2,1,0:T(8,128)(2,1)S(1)}, u32[]{:S(2)}, u32[]{:S(2)}) collective-permute-start(bf16[2,128,256]{2,1,0:T(8,128)(2,1)S(1)} %q_finish.1.refs_0_), channel_id=1, source_target_pairs={{0,64},{64,0},{1,65},{65,1},{2,66},{66,2},{3,67},{67,3},{4,68},{68... | collective-permute-start | bytes 393224 | tf_op jit(solution)/shard_map/ppermute | solution.py:391
  74.0 0.6 collective-permute-start.20
  74.7 13.2 %collective-permute-done.21.refs_2_ = bf16[2,128,256]{2,1,0:T(8,128)(2,1)S(1)} collective-permute-done((bf16[2,128,256]{2,1,0:T(8,128)(2,1)S(1)}, bf16[2,128,256]{2,1,0:T(8,128)(2,1)S(1)}, u32[]{:S(2)}, u32[]{:S(2)}) %collective-permute-start.21) | collective-permute-done | bytes 131104 | tf_op jit(solution)/shard_map/ppermute | solution.py:391
  87.8 0.6 collective-permute-start.22
  88.5 1.0 collective-permute-done.22.refs_3_
  89.5 6.2 %attend.1 = (bf16[288,256]{1,0:T(8,128)(2,1)S(1)}, bf16[288,256]{1,0:T(8,128)(2,1)S(1)}, bf16[288,256]{1,0:T(8,128)(2,1)S(1)}, bf16[288,256]{1,0:T(8,128)(2,1)S(1)}) custom-call(s32[6]{0:T(128)S(1)} %stack.57.idx, bf16[2,128,256]{2,1,0:T(8,128)(2,1)S(1)} %q_finish.1.refs_0_, bf16[2,128,256]{2,1,0:T(8,128)(2,1)S(1)} %collective-permute-done.20.refs_1_, ...), custom_call_target="tpu_custom_call" | custom-call | flops 2147483648 | bytes 4194304 | tf_op jit(solution)/shard_map/attend/pallas_call | solution.py:309
  95.7 1.1 collective-permute-start.23
  96.8 0.1 collective-permute-start.24
  96.9 0.9 collective-permute-done.23.b0
  97.8 0.4 collective-permute-done.24.b1
  98.2 0.2 merge.1
  98.3 0.6 collective-permute-start.25
  98.9 1.0 collective-permute-start.26
  99.9 3.8 %collective-permute-done.25.b0 = bf16[288,256]{1,0:T(8,128)(2,1)S(1)} collective-permute-done((bf16[288,256]{1,0:T(8,128)(2,1)S(1)}, bf16[288,256]{1,0:T(8,128)(2,1)S(1)}, u32[]{:S(2)}, u32[]{:S(2)}) %collective-permute-start.25) | collective-permute-done | bytes 147488 | tf_op jit(solution)/shard_map/ppermute | solution.py:391
  103.7 3.2 %collective-permute-done.26.b1 = bf16[288,256]{1,0:T(8,128)(2,1)S(1)} collective-permute-done((bf16[288,256]{1,0:T(8,128)(2,1)S(1)}, bf16[288,256]{1,0:T(8,128)(2,1)S(1)}, u32[]{:S(2)}, u32[]{:S(2)}) %collective-permute-start.26) | collective-permute-done | bytes 147488 | tf_op jit(solution)/shard_map/ppermute | solution.py:391
  106.8 0.2 last.1.mine_ref
  107.0 1.1 collective-permute-start.27
  108.1 1.2 %collective-permute-done.27.other_ref = bf16[256,512]{1,0:T(8,128)(2,1)S(1)} collective-permute-done((bf16[256,512]{1,0:T(8,128)(2,1)S(1)}, bf16[256,512]{1,0:T(8,128)(2,1)S(1)}, u32[]{:S(2)}, u32[]{:S(2)}) %collective-permute-start.27) | collective-permute-done | bytes 262176 | tf_op jit(solution)/shard_map/ppermute | solution.py:389
  109.3 1.4 %place.1 = bf16[256,1024]{1,0:T(8,128)(2,1)} custom-call(s32[6]{0:T(128)S(1)} %stack.57.idx, bf16[256,512]{1,0:T(8,128)(2,1)S(1)} %last.1.mine_ref, bf16[256,512]{1,0:T(8,128)(2,1)S(1)} %collective-permute-done.27.other_ref), custom_call_target="tpu_custom_call" | custom-call | flops 524288 | bytes 1048576 | tf_op jit(solution)/shard_map/place/pallas_call | solution.py:373
  (35 shorter events, 0.5 us)
Async XLA Ops:
  0.1 1.2 %copy-start.2 = (f32[1,256,1024]{2,1,0:T(8,128)S(1)}, f32[1,256,1024]{2,1,0:T(8,128)}, u32[]{:S(2)}) copy-start(f32[1,256,1024]{2,1,0:T(8,128)} %q_ref.1) | copy-start | bytes 3145732
  1.3 0.9 copy-start.5
  2.3 0.7 copy-start.8
  3.9 3.2 %collective-permute-start = (f32[2,320,256]{2,1,0:T(8,128)S(1)}, f32[2,320,256]{2,1,0:T(8,128)S(1)}, u32[]{:S(2)}, u32[]{:S(2)}) collective-permute-start(f32[2,320,256]{2,1,0:T(8,128)S(1)} %get-tuple-element.22), channel_id=1, source_target_pairs={{0,32},{32,0},{1,33},{33,1},{2,34},{34,2},{3,35},{35,3},{4,36},{36... | collective-permute-start | bytes 1966088 | tf_op jit(solution)/shard_map/ppermute | solution.py:396
  7.3 6.0 %collective-permute-start.1 = (bf16[320,256]{1,0:T(8,128)(2,1)S(1)}, bf16[320,256]{1,0:T(8,128)(2,1)S(1)}, u32[]{:S(2)}, u32[]{:S(2)}) collective-permute-start(bf16[320,256]{1,0:T(8,128)(2,1)S(1)} %fusion.1), channel_id=1, source_target_pairs={{0,64},{64,0},{1,65},{65,1},{2,66},{66,2},{3,67},{67,3},{4,68},{68... | collective-permute-start | bytes 491528 | tf_op jit(solution)/shard_map/ppermute | solution.py:399
  9.1 2.2 %copy-start = (bf16[256,8192]{1,0:T(8,128)(2,1)S(1)}, bf16[256,8192]{1,0:T(8,128)(2,1)}, u32[]{:S(2)}) copy-start(bf16[256,8192]{1,0:T(8,128)(2,1)} %refs_8_.1) | copy-start | bytes 12582916
  13.0 37.0 %copy-start.6 = (f32[256,128]{1,0:T(8,128)}, f32[256,128]{1,0:T(8,128)S(1)}, u32[]{:S(2)}) copy-start(f32[256,128]{1,0:T(8,128)S(1)} %get-tuple-element.27.refs_9_) | copy-start | bytes 393220
  13.3 25.4 %collective-permute-start.14 = (bf16[256,2048]{1,0:T(8,128)(2,1)S(1)}, bf16[256,2048]{1,0:T(8,128)(2,1)S(1)}, u32[]{:S(2)}, u32[]{:S(2)}) collective-permute-start(bf16[256,2048]{1,0:T(8,128)(2,1)S(1)} %get-tuple-element.29), channel_id=1, source_target_pairs={{0,16},{16,0},{1,17},{17,1},{2,18},{18,2},{3,19},{19,3},{4,20},{20... | collective-permute-start | bytes 3145736 | tf_op jit(solution)/shard_map/ppermute | solution.py:415
  16.5 7.0 %collective-permute-start.5 = (bf16[160,256]{1,0:T(8,128)(2,1)S(1)}, bf16[160,256]{1,0:T(8,128)(2,1)S(1)}, u32[]{:S(2)}, u32[]{:S(2)}) collective-permute-start(bf16[160,256]{1,0:T(8,128)(2,1)S(1)} %get-tuple-element.43), channel_id=1, source_target_pairs={{0,4},{4,8},{8,12},{12,0},{1,5},{5,9},{9,13},{13,1},{2,6},{6,10},{... | collective-permute-start | bytes 245768 | tf_op jit(solution)/shard_map/ppermute | solution.py:130
  17.8 6.5 %collective-permute-start.6 = (bf16[160,256]{1,0:T(8,128)(2,1)S(1)}, bf16[160,256]{1,0:T(8,128)(2,1)S(1)}, u32[]{:S(2)}, u32[]{:S(2)}) collective-permute-start(bf16[160,256]{1,0:T(8,128)(2,1)S(1)} %get-tuple-element.43), channel_id=1, source_target_pairs={{0,12},{4,0},{8,4},{12,8},{1,13},{5,1},{9,5},{13,9},{2,14},{6,2},{... | collective-permute-start | bytes 245768 | tf_op jit(solution)/shard_map/ppermute | solution.py:130
  19.3 5.9 %collective-permute-start.7 = (bf16[160,256]{1,0:T(8,128)(2,1)S(1)}, bf16[160,256]{1,0:T(8,128)(2,1)S(1)}, u32[]{:S(2)}, u32[]{:S(2)}) collective-permute-start(bf16[160,256]{1,0:T(8,128)(2,1)S(1)} %get-tuple-element.43), channel_id=1, source_target_pairs={{0,8},{4,12},{8,0},{12,4},{1,9},{5,13},{9,1},{13,5},{2,10},{6,14},... | collective-permute-start | bytes 245768 | tf_op jit(solution)/shard_map/ppermute | solution.py:130
  20.8 4.4 %collective-permute-start.3 = (bf16[160,256]{1,0:T(8,128)(2,1)S(1)}, bf16[160,256]{1,0:T(8,128)(2,1)S(1)}, u32[]{:S(2)}, u32[]{:S(2)}) collective-permute-start(bf16[160,256]{1,0:T(8,128)(2,1)S(1)} %get-tuple-element.44), channel_id=1, source_target_pairs={{0,3},{1,0},{2,1},{3,2},{4,7},{5,4},{6,5},{7,6},{8,11},{9,8},{10,9... | collective-permute-start | bytes 245768 | tf_op jit(solution)/shard_map/ppermute | solution.py:129
  23.5 5.1 %collective-permute-start.4 = (bf16[160,256]{1,0:T(8,128)(2,1)S(1)}, bf16[160,256]{1,0:T(8,128)(2,1)S(1)}, u32[]{:S(2)}, u32[]{:S(2)}) collective-permute-start(bf16[160,256]{1,0:T(8,128)(2,1)S(1)} %get-tuple-element.44), channel_id=1, source_target_pairs={{0,2},{1,3},{2,0},{3,1},{4,6},{5,7},{6,4},{7,5},{8,10},{9,11},{10,... | collective-permute-start | bytes 245768 | tf_op jit(solution)/shard_map/ppermute | solution.py:129
  24.3 5.2 %collective-permute-start.2 = (bf16[160,256]{1,0:T(8,128)(2,1)S(1)}, bf16[160,256]{1,0:T(8,128)(2,1)S(1)}, u32[]{:S(2)}, u32[]{:S(2)}) collective-permute-start(bf16[160,256]{1,0:T(8,128)(2,1)S(1)} %get-tuple-element.44), channel_id=1, source_target_pairs={{0,1},{1,2},{2,3},{3,0},{4,5},{5,6},{6,7},{7,4},{8,9},{9,10},{10,1... | collective-permute-start | bytes 245768 | tf_op jit(solution)/shard_map/ppermute | solution.py:129
  29.6 7.8 %collective-permute-start.10 = (bf16[4,160,256]{2,1,0:T(8,128)(2,1)S(1)}, bf16[4,160,256]{2,1,0:T(8,128)(2,1)S(1)}, u32[]{:S(2)}, u32[]{:S(2)}) collective-permute-start(bf16[4,160,256]{2,1,0:T(8,128)(2,1)S(1)} %pad_maximum_fusion.refs_0_), channel_id=1, source_target_pairs={{0,8},{4,12},{8,0},{12,4},{1,9},{5,13},{9,1},{13,5},{2,10},{6,14},... | collective-permute-start | bytes 983048 | tf_op jit(solution)/shard_map/ppermute | solution.py:132
  31.1 11.1 %collective-permute-start.11 = (bf16[4,160,256]{2,1,0:T(8,128)(2,1)S(1)}, bf16[4,160,256]{2,1,0:T(8,128)(2,1)S(1)}, u32[]{:S(2)}, u32[]{:S(2)}) collective-permute-start(bf16[4,160,256]{2,1,0:T(8,128)(2,1)S(1)} %pad_maximum_fusion.1.refs_4_), channel_id=1, source_target_pairs={{0,1},{1,2},{2,3},{3,0},{4,5},{5,6},{6,7},{7,4},{8,9},{9,10},{10,1... | collective-permute-start | bytes 983048 | tf_op jit(solution)/shard_map/ppermute | solution.py:133
  31.1 18.4 %collective-permute-start.12 = (bf16[4,160,256]{2,1,0:T(8,128)(2,1)S(1)}, bf16[4,160,256]{2,1,0:T(8,128)(2,1)S(1)}, u32[]{:S(2)}, u32[]{:S(2)}) collective-permute-start(bf16[4,160,256]{2,1,0:T(8,128)(2,1)S(1)} %pad_maximum_fusion.1.refs_4_), channel_id=1, source_target_pairs={{0,3},{1,0},{2,1},{3,2},{4,7},{5,4},{6,5},{7,6},{8,11},{9,8},{10,9... | collective-permute-start | bytes 983048 | tf_op jit(solution)/shard_map/ppermute | solution.py:133
  33.8 15.8 %collective-permute-start.13 = (bf16[4,160,256]{2,1,0:T(8,128)(2,1)S(1)}, bf16[4,160,256]{2,1,0:T(8,128)(2,1)S(1)}, u32[]{:S(2)}, u32[]{:S(2)}) collective-permute-start(bf16[4,160,256]{2,1,0:T(8,128)(2,1)S(1)} %pad_maximum_fusion.1.refs_4_), channel_id=1, source_target_pairs={{0,2},{1,3},{2,0},{3,1},{4,6},{5,7},{6,4},{7,5},{8,10},{9,11},{10,... | collective-permute-start | bytes 983048 | tf_op jit(solution)/shard_map/ppermute | solution.py:133
  37.4 12.7 %collective-permute-start.8 = (bf16[4,160,256]{2,1,0:T(8,128)(2,1)S(1)}, bf16[4,160,256]{2,1,0:T(8,128)(2,1)S(1)}, u32[]{:S(2)}, u32[]{:S(2)}) collective-permute-start(bf16[4,160,256]{2,1,0:T(8,128)(2,1)S(1)} %pad_maximum_fusion.refs_0_), channel_id=1, source_target_pairs={{0,4},{4,8},{8,12},{12,0},{1,5},{5,9},{9,13},{13,1},{2,6},{6,10},{... | collective-permute-start | bytes 983048 | tf_op jit(solution)/shard_map/ppermute | solution.py:132
  38.7 11.9 %collective-permute-start.9 = (bf16[4,160,256]{2,1,0:T(8,128)(2,1)S(1)}, bf16[4,160,256]{2,1,0:T(8,128)(2,1)}, u32[]{:S(2)}, u32[]{:S(2)}) collective-permute-start(bf16[4,160,256]{2,1,0:T(8,128)(2,1)S(1)} %pad_maximum_fusion.refs_0_), channel_id=1, source_target_pairs={{0,12},{4,0},{8,4},{12,8},{1,13},{5,1},{9,5},{13,9},{2,14},{6,2},{... | collective-permute-start | bytes 983048 | tf_op jit(solution)/shard_map/ppermute | solution.py:132
  42.2 8.8 %collective-permute-start.15 = (bf16[256,512]{1,0:T(8,128)(2,1)}, bf16[256,512]{1,0:T(8,128)(2,1)}, u32[]{:S(2)}, u32[]{:S(2)}) collective-permute-start(bf16[256,512]{1,0:T(8,128)(2,1)} %get-tuple-element.40), channel_id=1, source_target_pairs={{0,32},{32,0},{1,33},{33,1},{2,34},{34,2},{3,35},{35,3},{4,36},{36... | collective-permute-start | bytes 786440 | tf_op jit(solution)/shard_map/ppermute | solution.py:417
  49.5 1.9 %collective-permute-start.16 = (bf16[256,512]{1,0:T(8,128)(2,1)}, bf16[256,512]{1,0:T(8,128)(2,1)}, u32[]{:S(2)}, u32[]{:S(2)}) collective-permute-start(bf16[256,512]{1,0:T(8,128)(2,1)} %get-tuple-element.39), channel_id=1, source_target_pairs={{0,32},{32,0},{1,33},{33,1},{2,34},{34,2},{3,35},{35,3},{4,36},{36... | collective-permute-start | bytes 786440 | tf_op jit(solution)/shard_map/ppermute | solution.py:417
  49.5 2.2 %collective-permute-start.17 = (bf16[256,512]{1,0:T(8,128)(2,1)}, bf16[256,512]{1,0:T(8,128)(2,1)}, u32[]{:S(2)}, u32[]{:S(2)}) collective-permute-start(bf16[256,512]{1,0:T(8,128)(2,1)} %get-tuple-element.38), channel_id=1, source_target_pairs={{0,32},{32,0},{1,33},{33,1},{2,34},{34,2},{3,35},{35,3},{4,36},{36... | collective-permute-start | bytes 786440 | tf_op jit(solution)/shard_map/ppermute | solution.py:417
  50.0 2.1 %collective-permute-start.18 = (bf16[256,512]{1,0:T(8,128)(2,1)}, bf16[256,512]{1,0:T(8,128)(2,1)}, u32[]{:S(2)}, u32[]{:S(2)}) collective-permute-start(bf16[256,512]{1,0:T(8,128)(2,1)} %get-tuple-element.37), channel_id=1, source_target_pairs={{0,32},{32,0},{1,33},{33,1},{2,34},{34,2},{3,35},{35,3},{4,36},{36... | collective-permute-start | bytes 786440 | tf_op jit(solution)/shard_map/ppermute | solution.py:417
  50.5 4.9 %copy-start.1 = (bf16[256,8192]{1,0:T(8,128)(2,1)S(1)}, bf16[256,8192]{1,0:T(8,128)(2,1)}, u32[]{:S(2)}) copy-start(bf16[256,8192]{1,0:T(8,128)(2,1)} %refs_8_.1) | copy-start | bytes 12582916
  50.5 4.9 %copy-start.7 = (f32[256,128]{1,0:T(8,128)S(1)}, f32[256,128]{1,0:T(8,128)}, u32[]{:S(2)}) copy-start(f32[256,128]{1,0:T(8,128)} %copy-done.6) | copy-start | bytes 393220
  55.2 7.7 %collective-permute-start.19 = (bf16[384,256]{1,0:T(8,128)(2,1)S(1)}, bf16[384,256]{1,0:T(8,128)(2,1)S(1)}, u32[]{:S(2)}, u32[]{:S(2)}) collective-permute-start(bf16[384,256]{1,0:T(8,128)(2,1)S(1)} %theirs.1), channel_id=1, source_target_pairs={{0,16},{16,0},{1,17},{17,1},{2,18},{18,2},{3,19},{19,3},{4,20},{20... | collective-permute-start | bytes 589832 | tf_op jit(solution)/shard_map/ppermute | solution.py:432
  58.2 0.7 copy-start.3
  64.1 25.4 %all-to-all-start = ((bf16[128,32,128]{2,1,0:T(8,128)(2,1)}), bf16[128,32,128]{2,1,0:T(8,128)(2,1)S(1)}, u32[]{:S(2)}, u32[]{:S(2)}) async-start(bf16[128,32,128]{2,1,0:T(8,128)(2,1)} %bitcast.16), calls=%async_computation | async-start | bytes 2097152 | tf_op jit(solution)/shard_map/all_to_all | solution.py:438
  71.1 1.0 copy-start.4
  72.4 15.4 %collective-permute-start.21 = (bf16[2,128,256]{2,1,0:T(8,128)(2,1)S(1)}, bf16[2,128,256]{2,1,0:T(8,128)(2,1)S(1)}, u32[]{:S(2)}, u32[]{:S(2)}) collective-permute-start(bf16[2,128,256]{2,1,0:T(8,128)(2,1)S(1)} %q_finish.1.refs_0_), channel_id=1, source_target_pairs={{0,64},{64,0},{1,65},{65,1},{2,66},{66,2},{3,67},{67,3},{4,68},{68... | collective-permute-start | bytes 393224 | tf_op jit(solution)/shard_map/ppermute | solution.py:391
  74.0 14.4 %collective-permute-start.20 = (bf16[2,128,256]{2,1,0:T(8,128)(2,1)S(1)}, bf16[2,128,256]{2,1,0:T(8,128)(2,1)S(1)}, u32[]{:S(2)}, u32[]{:S(2)}) collective-permute-start(bf16[2,128,256]{2,1,0:T(8,128)(2,1)S(1)} %q_finish.1.refs_0_), channel_id=1, source_target_pairs={{0,32},{32,0},{1,33},{33,1},{2,34},{34,2},{3,35},{35,3},{4,36},{36... | collective-permute-start | bytes 393224 | tf_op jit(solution)/shard_map/ppermute | solution.py:389
  87.8 1.6 %collective-permute-start.22 = (bf16[2,128,256]{2,1,0:T(8,128)(2,1)S(1)}, bf16[2,128,256]{2,1,0:T(8,128)(2,1)S(1)}, u32[]{:S(2)}, u32[]{:S(2)}) collective-permute-start(bf16[2,128,256]{2,1,0:T(8,128)(2,1)S(1)} %collective-permute-done.21.refs_2_), channel_id=1, source_target_pairs={{0,32},{32,0},{1,33},{33,1},{2,34},{34,2},{3,35},{35,3},{4,36},{36... | collective-permute-start | bytes 393224 | tf_op jit(solution)/shard_map/ppermute | solution.py:389
  95.7 2.1 %collective-permute-start.23 = (bf16[288,256]{1,0:T(8,128)(2,1)S(1)}, bf16[288,256]{1,0:T(8,128)(2,1)S(1)}, u32[]{:S(2)}, u32[]{:S(2)}) collective-permute-start(bf16[288,256]{1,0:T(8,128)(2,1)S(1)} %get-tuple-element.33), channel_id=1, source_target_pairs={{0,32},{32,0},{1,33},{33,1},{2,34},{34,2},{3,35},{35,3},{4,36},{36... | collective-permute-start | bytes 442376 | tf_op jit(solution)/shard_map/ppermute | solution.py:389
  96.8 1.4 %collective-permute-start.24 = (bf16[288,256]{1,0:T(8,128)(2,1)S(1)}, bf16[288,256]{1,0:T(8,128)(2,1)S(1)}, u32[]{:S(2)}, u32[]{:S(2)}) collective-permute-start(bf16[288,256]{1,0:T(8,128)(2,1)S(1)} %get-tuple-element.34), channel_id=1, source_target_pairs={{0,32},{32,0},{1,33},{33,1},{2,34},{34,2},{3,35},{35,3},{4,36},{36... | collective-permute-start | bytes 442376 | tf_op jit(solution)/shard_map/ppermute | solution.py:389
  98.3 5.3 %collective-permute-start.25 = (bf16[288,256]{1,0:T(8,128)(2,1)S(1)}, bf16[288,256]{1,0:T(8,128)(2,1)S(1)}, u32[]{:S(2)}, u32[]{:S(2)}) collective-permute-start(bf16[288,256]{1,0:T(8,128)(2,1)S(1)} %get-tuple-element.36.a1), channel_id=1, source_target_pairs={{0,64},{64,0},{1,65},{65,1},{2,66},{66,2},{3,67},{67,3},{4,68},{68... | collective-permute-start | bytes 442376 | tf_op jit(solution)/shard_map/ppermute | solution.py:391
  98.9 7.9 %collective-permute-start.26 = (bf16[288,256]{1,0:T(8,128)(2,1)S(1)}, bf16[288,256]{1,0:T(8,128)(2,1)S(1)}, u32[]{:S(2)}, u32[]{:S(2)}) collective-permute-start(bf16[288,256]{1,0:T(8,128)(2,1)S(1)} %get-tuple-element.35.a0), channel_id=1, source_target_pairs={{0,64},{64,0},{1,65},{65,1},{2,66},{66,2},{3,67},{67,3},{4,68},{68... | collective-permute-start | bytes 442376 | tf_op jit(solution)/shard_map/ppermute | solution.py:391
  107.0 2.3 %collective-permute-start.27 = (bf16[256,512]{1,0:T(8,128)(2,1)S(1)}, bf16[256,512]{1,0:T(8,128)(2,1)S(1)}, u32[]{:S(2)}, u32[]{:S(2)}) collective-permute-start(bf16[256,512]{1,0:T(8,128)(2,1)S(1)} %last.1.mine_ref), channel_id=1, source_target_pairs={{0,32},{32,0},{1,33},{33,1},{2,34},{34,2},{3,35},{35,3},{4,36},{36... | collective-permute-start | bytes 786440 | tf_op jit(solution)/shard_map/ppermute | solution.py:389

commit v4 on v3

--- a/solution.py
+++ b/solution.py
@@ -182,10 +182,8 @@
         return jnp.where(at // 8 == idx[1], xa_ref[:, cols], xb_ref[:, cols])
 
     q, pair = accumulate(idx, w_refs, block)
-    high = pair.astype(BF16)
     out_ref[0:256] = q.astype(BF16)
-    out_ref[256:320] = high
-    out_ref[320:384] = (pair - high.astype(F32)).astype(BF16)
+    out_ref[256:320] = pair.astype(BF16)
 
 
 def project(kernel, args, outs, name, scratch=()):
@@ -202,7 +200,7 @@
 
 
 def pair_finish_kernel(own_ref, got_ref, cos_ref, sin_ref, out_ref):
-    t = own_ref[...] + (got_ref[256:320].astype(F32) + got_ref[320:384].astype(F32))
+    t = own_ref[...] + got_ref[256:320].astype(F32)
     u, w = t[0:16], t[16:32]
     cos, sin = cos_ref[...], sin_ref[...]
     key = jnp.concatenate([u * cos - w * sin, w * cos + u * sin], axis=0)
@@ -244,8 +242,8 @@
 
 def attend_kernel(idx, *refs):
     q_refs, kv_ref = refs[0:4], refs[4]
-    o_refs = refs[5:9]
-    k_s, v_s, qx, s0, s1 = refs[9:]
+    o_refs = refs[5:7]
+    k_s, v_s, qx, s0, s1 = refs[7:]
     scores = (s0, s1)
     f, r = idx[2], idx[3]
     lane = lax.broadcasted_iota(jnp.int32, (32, 128), 1)
@@ -299,18 +297,18 @@
             acc = mix if acc is None else acc + mix
             total = part if total is None else total + part
         total = jnp.sum(total, axis=0, keepdims=True)
-        o_ref, at = o_refs[h // 2], (h % 2) * STAT
+        o_ref, at = o_refs[h // 2 % 2], (h // 4 * 2 + h % 2) * STAT
         o_ref[at:at + 128] = (acc / total).astype(BF16)
         put_log(o_ref, at, top * EXP_SCALE + jnp.log2(total))
 
 
 def attend(idx, qs, kv):
-    shape = jax.ShapeDtypeStruct((2 * STAT, 256), BF16)
+    shape = jax.ShapeDtypeStruct((4 * STAT, 256), BF16)
     return pl.pallas_call(
         attend_kernel,
         in_specs=[sspec()] + [vspec()] * 5,
-        out_specs=[vspec()] * 4,
-        out_shape=[shape] * 4,
+        out_specs=[vspec()] * 2,
+        out_shape=[shape] * 2,
         scratch_shapes=[
             VMEM((KEYS, 256), BF16), VMEM((128, KEYS), BF16), VMEM((128, 256), BF16),
             VMEM((KEYS, 256), F32), VMEM((KEYS, 256), F32),
@@ -334,31 +332,28 @@
     ref[at + 128:at + STAT] = terms.astype(BF16)
 
 
-def merged(a_ref, b_ref, at):
-    a, b = log_sum(a_ref, at), log_sum(b_ref, at)
+def merged(a_ref, b_ref, i, j):
+    a, b = log_sum(a_ref, i), log_sum(b_ref, j)
     top = jnp.maximum(a, b)
     fa, fb = jnp.exp2(a - top), jnp.exp2(b - top)
     total = fa + fb
-    mixed = a_ref[at:at + 128].astype(F32) * (fa / total)
-    mixed = mixed + b_ref[at:at + 128].astype(F32) * (fb / total)
+    mixed = a_ref[i:i + 128].astype(F32) * (fa / total)
+    mixed = mixed + b_ref[j:j + 128].astype(F32) * (fb / total)
     return mixed, top + jnp.log2(total)
 
 
-def merge_kernel(a0, a1, b0, b1, o0, o1):
-    for a_ref, b_ref, o_ref in ((a0, b0, o0), (a1, b1, o1)):
-        for h in range(2):
-            at = h * STAT
-            mixed, log = merged(a_ref, b_ref, at)
-            o_ref[at:at + 128] = mixed.astype(BF16)
-            put_log(o_ref, at, log)
-
-
-def last_kernel(a0, a1, b0, b1, out_ref):
-    for i, (a_ref, b_ref) in enumerate(((a0, b0), (a1, b1))):
-        for h in range(2):
-            mixed, _ = merged(a_ref, b_ref, h * STAT)
-            col = (i * 2 + h) * 128
-            out_ref[:, col:col + 128] = mixed.T.astype(BF16)
+def merge_kernel(a_ref, b_ref, o_ref):
+    for h in range(4):
+        at = h * STAT
+        mixed, log = merged(a_ref, b_ref, at, at)
+        o_ref[at:at + 128] = mixed.astype(BF16)
+        put_log(o_ref, at, log)
+
+
+def last_kernel(a_ref, b_ref, out_ref):
+    for h in range(4):
+        mixed, _ = merged(a_ref, b_ref, h * STAT, (h + 2) % 4 * STAT)
+        out_ref[:, h * 128:(h + 1) * 128] = mixed.T.astype(BF16)
 
 
 def place_kernel(idx, mine_ref, other_ref, out_ref):
@@ -427,7 +422,7 @@
     cos_t, sin_t = jnp.cos(angles_t), jnp.sin(angles_t)
 
     (theirs,) = project(
-        theirs_kernel, (idx, *w_all, got, *other), [jax.ShapeDtypeStruct((384, 256), BF16)],
+        theirs_kernel, (idx, *w_all, got, *other), [jax.ShapeDtypeStruct((320, 256), BF16)],
         "theirs", [VMEM((256, 2048), BF16)])
     back = lax.ppermute(theirs, "zh", SWAP)
     q_own, pair_own = project(
@@ -441,12 +436,9 @@
     q1, q2 = to_rep(q0, 1), to_rep(q0, 2)
     qs = [q0, q1, q2, to_rep(q2, 1)]
 
-    parts = attend(idx, qs, pair_all.reshape(32, 4, 32, 128))
-    stat = (2 * STAT, 256)
-    b0, b1 = to_rep(parts[1], 1), to_rep(parts[3], 1)
-    a0, a1 = small(merge_kernel, (parts[0], parts[2], b0, b1), [stat, stat], "merge")
-    c0, c1 = to_rep(a1, 2), to_rep(a0, 2)
-    (mine,) = small(last_kernel, (a0, a1, c0, c1), [(256, 512)], "last")
+    kept, sent = attend(idx, qs, pair_all.reshape(32, 4, 32, 128))
+    (part,) = small(merge_kernel, (kept, to_rep(sent, 1)), [(4 * STAT, 256)], "merge")
+    (mine,) = small(last_kernel, (part, to_rep(part, 2)), [(256, 512)], "last")
     (out,) = small(place_kernel, (idx, mine, to_rep(mine, 1)), [(256, 1024)], "place", 1)
     return out
 

time: 111 us -> 111 us (level)
    ppermute x3 -> x2, starting transfers between devices: 3.13 us -> 2.14 us  [to_rep(): return lax.ppermute(x, 'zl', SWAP)]
    ppermute x3 -> x2, waiting for transfers between devices: 20.1 us -> 20.9 us  [to_rep(): return lax.ppermute(x, 'zl', SWAP)]
    ppermute x5 -> x4, starting transfers between devices: 3.55 us -> 3.64 us  [to_rep(): return lax.ppermute(x, 'c', SWAP)]
    ppermute x5 -> x4, waiting for transfers between devices: 3.43 us -> 3.36 us  [to_rep(): return lax.ppermute(x, 'c', SWAP)]
  transfers between devices with their start and end apart: 29 -> 27, of which waited for: 19 -> 17; matrix products, arithmetic and copies ran while one was open for 2% -> 2% of each run, Pallas kernels for 4% -> 4%
where the time goes in v4:
time: 111 us; the launch traced here: 110 us
  starting transfers between devices  42.6 us (38%)
  waiting for transfers between devices  40.5 us (36%)
  Pallas kernels  18.1 us (16%)
  local copies, waits for them, and re-layouts  7.84 us (7%)
    ppermute x2, waiting for transfers between devices, to_rep(): return lax.ppermute(x, 'zl', SWAP)  20.9 us
    ppermute x4, starting transfers between devices, local(): lax.ppermute(got[:, i * width:(i + 1) * width], 'c', SWAP)  8.33 us
    all_to_all x1, starting transfers between devices, local(): lax.all_to_all(pair.reshape(128, 32, 128), ('zh', 'x', 'y', 'zl', 'c'), 0...  6.78 us
    unnamed x18, local copies, waits for them, and re-layouts  6.67 us
    pallas_call x1, Pallas kernels, attend(): pl.pallas_call(attend_kernel, in_specs=[sspec()] + [vspec()] * 5, out_spe...  6.21 us
    pallas_call x2, Pallas kernels, project(): pl.pallas_call(kernel, scratch_shapes=scratch, in_specs=[sspec()] + [vspe...  5.76 us
    ppermute x3, starting transfers between devices, gather_plane(): lowers = [lower] + [lax.ppermute(lower, 'x', ring(d)) for d in (1, 3, 2)]  4.31 us
    ppermute x3, starting transfers between devices, gather_plane(): lax.ppermute(upper, 'x', ring(d))  4.28 us
  transfers between devices with their start and end apart: 27, of which 17 were waited for; matrix products, arithmetic and copies ran while one was open for 2% of the time, Pallas kernels for 4%

profile of v4, /device:TPU:1, one launch (start us, length us, event | category | flops | bytes accessed | tf_op | source)
XLA Modules:
  0.0 110.2 jit_solution(12417051254090778191)
XLA Ops:
  0.0 0.1 stack.57.idx
  0.1 1.2 %copy-done.2 = f32[1,256,1024]{2,1,0:T(8,128)S(1)} copy-done((f32[1,256,1024]{2,1,0:T(8,128)S(1)}, f32[1,256,1024]{2,1,0:T(8,128)}, u32[]{:S(2)}) %copy-start.2) | copy-done | bytes 1048600
  1.3 0.9 copy-done.5
  2.3 0.7 copy-done.8
  2.9 1.0 prepare.1
  3.9 1.5 %collective-permute-start = (f32[2,320,256]{2,1,0:T(8,128)S(1)}, f32[2,320,256]{2,1,0:T(8,128)S(1)}, u32[]{:S(2)}, u32[]{:S(2)}) collective-permute-start(f32[2,320,256]{2,1,0:T(8,128)S(1)} %get-tuple-element.18), channel_id=1, source_target_pairs={{0,32},{32,0},{1,33},{33,1},{2,34},{34,2},{3,35},{35,3},{4,36},{36... | collective-permute-start | bytes 1966088 | tf_op jit(solution)/shard_map/ppermute | solution.py:391
  5.4 1.7 %collective-permute-done = f32[2,320,256]{2,1,0:T(8,128)S(1)} collective-permute-done((f32[2,320,256]{2,1,0:T(8,128)S(1)}, f32[2,320,256]{2,1,0:T(8,128)S(1)}, u32[]{:S(2)}, u32[]{:S(2)}) %collective-permute-start) | collective-permute-done | bytes 655392 | tf_op jit(solution)/shard_map/ppermute | solution.py:391
  7.1 0.1 add.35
  7.3 1.8 %collective-permute-start.1 = (bf16[320,256]{1,0:T(8,128)(2,1)S(1)}, bf16[320,256]{1,0:T(8,128)(2,1)S(1)}, u32[]{:S(2)}, u32[]{:S(2)}) collective-permute-start(bf16[320,256]{1,0:T(8,128)(2,1)S(1)} %fusion.1), channel_id=1, source_target_pairs={{0,64},{64,0},{1,65},{65,1},{2,66},{66,2},{3,67},{67,3},{4,68},{68... | collective-permute-start | bytes 491528 | tf_op jit(solution)/shard_map/ppermute | solution.py:394
  9.1 2.2 %copy-done = bf16[256,8192]{1,0:T(8,128)(2,1)S(1)} copy-done((bf16[256,8192]{1,0:T(8,128)(2,1)S(1)}, bf16[256,8192]{1,0:T(8,128)(2,1)}, u32[]{:S(2)}) %copy-start) | copy-done | bytes 4194328
  11.3 1.8 %normalise.1 = (f32[256,128]{1,0:T(8,128)S(1)}, bf16[256,2048]{1,0:T(8,128)(2,1)S(1)}) custom-call(s32[6]{0:T(128)S(1)} %stack.57.idx, bf16[256,8192]{1,0:T(8,128)(2,1)S(1)} %copy-done), custom_call_target="tpu_custom_call" | custom-call | flops 8388608 | bytes 6291456 | tf_op jit(solution)/shard_map/normalise/pallas_call | solution.py:64
  13.0 0.3 collective-permute-done.1
  13.3 3.1 %collective-permute-start.14 = (bf16[256,2048]{1,0:T(8,128)(2,1)S(1)}, bf16[256,2048]{1,0:T(8,128)(2,1)S(1)}, u32[]{:S(2)}, u32[]{:S(2)}) collective-permute-start(bf16[256,2048]{1,0:T(8,128)(2,1)S(1)} %get-tuple-element.25), channel_id=1, source_target_pairs={{0,16},{16,0},{1,17},{17,1},{2,18},{18,2},{3,19},{19,3},{4,20},{20... | collective-permute-start | bytes 3145736 | tf_op jit(solution)/shard_map/ppermute | solution.py:410
  16.4 0.1 fusion
  16.5 1.3 %collective-permute-start.5 = (bf16[160,256]{1,0:T(8,128)(2,1)S(1)}, bf16[160,256]{1,0:T(8,128)(2,1)S(1)}, u32[]{:S(2)}, u32[]{:S(2)}) collective-permute-start(bf16[160,256]{1,0:T(8,128)(2,1)S(1)} %get-tuple-element.35), channel_id=1, source_target_pairs={{0,4},{4,8},{8,12},{12,0},{1,5},{5,9},{9,13},{13,1},{2,6},{6,10},{... | collective-permute-start | bytes 245768 | tf_op jit(solution)/shard_map/ppermute | solution.py:130
  17.8 1.5 %collective-permute-start.6 = (bf16[160,256]{1,0:T(8,128)(2,1)S(1)}, bf16[160,256]{1,0:T(8,128)(2,1)S(1)}, u32[]{:S(2)}, u32[]{:S(2)}) collective-permute-start(bf16[160,256]{1,0:T(8,128)(2,1)S(1)} %get-tuple-element.35), channel_id=1, source_target_pairs={{0,12},{4,0},{8,4},{12,8},{1,13},{5,1},{9,5},{13,9},{2,14},{6,2},{... | collective-permute-start | bytes 245768 | tf_op jit(solution)/shard_map/ppermute | solution.py:130
  19.3 1.5 %collective-permute-start.7 = (bf16[160,256]{1,0:T(8,128)(2,1)S(1)}, bf16[160,256]{1,0:T(8,128)(2,1)S(1)}, u32[]{:S(2)}, u32[]{:S(2)}) collective-permute-start(bf16[160,256]{1,0:T(8,128)(2,1)S(1)} %get-tuple-element.35), channel_id=1, source_target_pairs={{0,8},{4,12},{8,0},{12,4},{1,9},{5,13},{9,1},{13,5},{2,10},{6,14},... | collective-permute-start | bytes 245768 | tf_op jit(solution)/shard_map/ppermute | solution.py:130
  20.8 2.7 %collective-permute-start.3 = (bf16[160,256]{1,0:T(8,128)(2,1)S(1)}, bf16[160,256]{1,0:T(8,128)(2,1)S(1)}, u32[]{:S(2)}, u32[]{:S(2)}) collective-permute-start(bf16[160,256]{1,0:T(8,128)(2,1)S(1)} %get-tuple-element.36), channel_id=1, source_target_pairs={{0,3},{1,0},{2,1},{3,2},{4,7},{5,4},{6,5},{7,6},{8,11},{9,8},{10,9... | collective-permute-start | bytes 245768 | tf_op jit(solution)/shard_map/ppermute | solution.py:129
  23.5 0.8 collective-permute-start.4
  24.3 0.4 collective-permute-start.2
  24.7 0.5 collective-permute-done.7
  25.3 3.4 %collective-permute-done.4 = bf16[160,256]{1,0:T(8,128)(2,1)S(1)} collective-permute-done((bf16[160,256]{1,0:T(8,128)(2,1)S(1)}, bf16[160,256]{1,0:T(8,128)(2,1)S(1)}, u32[]{:S(2)}, u32[]{:S(2)}) %collective-permute-start.4) | collective-permute-done | bytes 81952 | tf_op jit(solution)/shard_map/ppermute | solution.py:129
  28.6 0.9 collective-permute-done.2
  29.6 1.5 %collective-permute-start.10 = (bf16[4,160,256]{2,1,0:T(8,128)(2,1)S(1)}, bf16[4,160,256]{2,1,0:T(8,128)(2,1)S(1)}, u32[]{:S(2)}, u32[]{:S(2)}) collective-permute-start(bf16[4,160,256]{2,1,0:T(8,128)(2,1)S(1)} %pad_maximum_fusion.refs_0_), channel_id=1, source_target_pairs={{0,8},{4,12},{8,0},{12,4},{1,9},{5,13},{9,1},{13,5},{2,10},{6,14},... | collective-permute-start | bytes 983048 | tf_op jit(solution)/shard_map/ppermute | solution.py:132
  31.1 2.7 %collective-permute-start.12 = (bf16[4,160,256]{2,1,0:T(8,128)(2,1)S(1)}, bf16[4,160,256]{2,1,0:T(8,128)(2,1)S(1)}, u32[]{:S(2)}, u32[]{:S(2)}) collective-permute-start(bf16[4,160,256]{2,1,0:T(8,128)(2,1)S(1)} %pad_maximum_fusion.1.refs_4_), channel_id=1, source_target_pairs={{0,3},{1,0},{2,1},{3,2},{4,7},{5,4},{6,5},{7,6},{8,11},{9,8},{10,9... | collective-permute-start | bytes 983048 | tf_op jit(solution)/shard_map/ppermute | solution.py:133
  33.8 3.6 %collective-permute-done.10.refs_3_ = bf16[4,160,256]{2,1,0:T(8,128)(2,1)S(1)} collective-permute-done((bf16[4,160,256]{2,1,0:T(8,128)(2,1)S(1)}, bf16[4,160,256]{2,1,0:T(8,128)(2,1)S(1)}, u32[]{:S(2)}, u32[]{:S(2)}) %collective-permute-start.10) | collective-permute-done | bytes 327712 | tf_op jit(solution)/shard_map/ppermute | solution.py:132
  37.4 0.3 collective-permute-start.8
  37.7 1.0 collective-permute-done.14.refs_8_
  38.7 2.5 %collective-permute-start.9 = (bf16[4,160,256]{2,1,0:T(8,128)(2,1)S(1)}, bf16[4,160,256]{2,1,0:T(8,128)(2,1)}, u32[]{:S(2)}, u32[]{:S(2)}) collective-permute-start(bf16[4,160,256]{2,1,0:T(8,128)(2,1)S(1)} %pad_maximum_fusion.refs_0_), channel_id=1, source_target_pairs={{0,12},{4,0},{8,4},{12,8},{1,13},{5,1},{9,5},{13,9},{2,14},{6,2},{... | collective-permute-start | bytes 983048 | tf_op jit(solution)/shard_map/ppermute | solution.py:132
  41.2 1.0 fusion.2
  42.2 7.3 %collective-permute-start.15 = (bf16[256,512]{1,0:T(8,128)(2,1)}, bf16[256,512]{1,0:T(8,128)(2,1)}, u32[]{:S(2)}, u32[]{:S(2)}) collective-permute-start(bf16[256,512]{1,0:T(8,128)(2,1)} %get-tuple-element.32), channel_id=1, source_target_pairs={{0,32},{32,0},{1,33},{33,1},{2,34},{34,2},{3,35},{35,3},{4,36},{36... | collective-permute-start | bytes 786440 | tf_op jit(solution)/shard_map/ppermute | solution.py:412
  49.5 0.5 collective-permute-start.17
  50.0 0.5 collective-permute-start.18
  50.5 0.1 dynamic_slice.3
  50.6 0.4 collective-permute-done.15.refs_9_
  51.0 0.4 collective-permute-done.16.refs_10_
  51.4 0.4 collective-permute-done.17.refs_11_
  51.8 0.4 collective-permute-done.18.refs_12_
  52.1 3.1 %theirs.1 = bf16[320,256]{1,0:T(8,128)(2,1)S(1)} custom-call(s32[6]{0:T(128)S(1)} %stack.57.idx, bf16[4,160,256]{2,1,0:T(8,128)(2,1)S(1)} %pad_maximum_fusion.refs_0_, bf16[4,160,256]{2,1,0:T(8,128)(2,1)S(1)} %collective-permute-done.8.refs_1_, bf16[4,160,256]{2,1,0:T(8,128)(2,1)} %collective-permute-done.9.refs_2_, ...), custom_call_target="tpu_custom_call" | custom-call | flops 671088640 | bytes 5242880 | tf_op jit(solution)/shard_map/theirs/pallas_call | solution.py:190
  55.2 0.1 collective-permute-start.19
  55.3 0.1 multiply_sine_fusion.1
  55.5 2.7 %own.1 = (f32[256,256]{1,0:T(8,128)S(1)}, f32[64,256]{1,0:T(8,128)S(1)}) custom-call(s32[6]{0:T(128)S(1)} %stack.57.idx, bf16[4,160,256]{2,1,0:T(8,128)(2,1)S(1)} %pad_maximum_fusion.refs_0_, bf16[4,160,256]{2,1,0:T(8,128)(2,1)S(1)} %collective-permute-done.8.refs_1_, bf16[4,160,256]{2,1,0:T(8,128)(2,1)} %collective-permute-done.9.refs_2_, ...), custom_call_target="tpu_custom_call" | custom-call | flops 671088640 | bytes 5242880 | tf_op jit(solution)/shard_map/own/pallas_call | solution.py:190
  58.2 0.7 copy-done.3
  58.9 3.3 %collective-permute-done.19.got_ref = bf16[320,256]{1,0:T(8,128)(2,1)S(1)} collective-permute-done((bf16[320,256]{1,0:T(8,128)(2,1)S(1)}, bf16[320,256]{1,0:T(8,128)(2,1)S(1)}, u32[]{:S(2)}, u32[]{:S(2)}) %collective-permute-start.19) | collective-permute-done | bytes 163872 | tf_op jit(solution)/shard_map/ppermute | solution.py:427
  62.2 1.2 %pair_finish.1 = bf16[32,4,32,128]{3,2,1,0:T(8,128)(2,1)} custom-call(f32[64,256]{1,0:T(8,128)S(1)} %get-tuple-element.26.own_ref, bf16[320,256]{1,0:T(8,128)(2,1)S(1)} %collective-permute-done.19.got_ref, f32[16,256]{1,0:T(8,128)S(1)} %get-tuple-element.38.cos_ref, f32[16,256]{1,0:T(8,128)S(1)} %get-tuple-element.37.sin_ref), custom_call_target="tpu_custom_call" | custom-call | flops 262144 | bytes 1048576 | tf_op jit(solution)/shard_map/pair_finish/pallas_call | solution.py:226
  63.4 6.8 %all-to-all-start = ((bf16[128,32,128]{2,1,0:T(8,128)(2,1)}), bf16[128,32,128]{2,1,0:T(8,128)(2,1)S(1)}, u32[]{:S(2)}, u32[]{:S(2)}) async-start(bf16[128,32,128]{2,1,0:T(8,128)(2,1)} %bitcast.16), calls=%async_computation | async-start | bytes 2097152 | tf_op jit(solution)/shard_map/all_to_all | solution.py:433
  70.2 0.5 multiply_sine_fusion
  70.7 0.9 copy-done.4
  71.7 0.4 q_finish.1.refs_0_
  72.1 1.6 %collective-permute-start.21 = (bf16[2,128,256]{2,1,0:T(8,128)(2,1)S(1)}, bf16[2,128,256]{2,1,0:T(8,128)(2,1)S(1)}, u32[]{:S(2)}, u32[]{:S(2)}) collective-permute-start(bf16[2,128,256]{2,1,0:T(8,128)(2,1)S(1)} %q_finish.1.refs_0_), channel_id=1, source_target_pairs={{0,64},{64,0},{1,65},{65,1},{2,66},{66,2},{3,67},{67,3},{4,68},{68... | collective-permute-start | bytes 393224 | tf_op jit(solution)/shard_map/ppermute | solution.py:386
  73.7 0.6 collective-permute-start.20
  74.3 13.2 %collective-permute-done.21.refs_2_ = bf16[2,128,256]{2,1,0:T(8,128)(2,1)S(1)} collective-permute-done((bf16[2,128,256]{2,1,0:T(8,128)(2,1)S(1)}, bf16[2,128,256]{2,1,0:T(8,128)(2,1)S(1)}, u32[]{:S(2)}, u32[]{:S(2)}) %collective-permute-start.21) | collective-permute-done | bytes 131104 | tf_op jit(solution)/shard_map/ppermute | solution.py:386
  87.5 0.6 collective-permute-start.22
  88.1 1.0 collective-permute-done.22.refs_3_
  89.1 6.2 %attend.1 = (bf16[576,256]{1,0:T(8,128)(2,1)S(1)}, bf16[576,256]{1,0:T(8,128)(2,1)S(1)}) custom-call(s32[6]{0:T(128)S(1)} %stack.57.idx, bf16[2,128,256]{2,1,0:T(8,128)(2,1)S(1)} %q_finish.1.refs_0_, bf16[2,128,256]{2,1,0:T(8,128)(2,1)S(1)} %collective-permute-done.20.refs_1_, bf16[2,128,256]{2,1,0:T(8,128)(2,1)S(1)} %collective-permute-done.21.refs_2_, ...), custom_call_target="tpu_custom_call" | custom-call | flops 2147483648 | bytes 4194304 | tf_op jit(solution)/shard_map/attend/pallas_call | solution.py:307
  95.3 1.1 collective-permute-start.23
  96.4 1.2 %collective-permute-done.23.b_ref = bf16[576,256]{1,0:T(8,128)(2,1)S(1)} collective-permute-done((bf16[576,256]{1,0:T(8,128)(2,1)S(1)}, bf16[576,256]{1,0:T(8,128)(2,1)S(1)}, u32[]{:S(2)}, u32[]{:S(2)}) %collective-permute-start.23) | collective-permute-done | bytes 294944 | tf_op jit(solution)/shard_map/ppermute | solution.py:384
  97.6 0.2 merge.1.a_ref
  97.8 0.6 collective-permute-start.24
  98.3 7.7 %collective-permute-done.24.b_ref = bf16[576,256]{1,0:T(8,128)(2,1)S(1)} collective-permute-done((bf16[576,256]{1,0:T(8,128)(2,1)S(1)}, bf16[576,256]{1,0:T(8,128)(2,1)S(1)}, u32[]{:S(2)}, u32[]{:S(2)}) %collective-permute-start.24) | collective-permute-done | bytes 294944 | tf_op jit(solution)/shard_map/ppermute | solution.py:386
  106.1 0.2 last.1.mine_ref
  106.3 1.3 %collective-permute-start.25 = (bf16[256,512]{1,0:T(8,128)(2,1)S(1)}, bf16[256,512]{1,0:T(8,128)(2,1)S(1)}, u32[]{:S(2)}, u32[]{:S(2)}) collective-permute-start(bf16[256,512]{1,0:T(8,128)(2,1)S(1)} %last.1.mine_ref), channel_id=1, source_target_pairs={{0,32},{32,0},{1,33},{33,1},{2,34},{34,2},{3,35},{35,3},{4,36},{36... | collective-permute-start | bytes 786440 | tf_op jit(solution)/shard_map/ppermute | solution.py:384
  107.6 1.2 %collective-permute-done.25.other_ref = bf16[256,512]{1,0:T(8,128)(2,1)S(1)} collective-permute-done((bf16[256,512]{1,0:T(8,128)(2,1)S(1)}, bf16[256,512]{1,0:T(8,128)(2,1)S(1)}, u32[]{:S(2)}, u32[]{:S(2)}) %collective-permute-start.25) | collective-permute-done | bytes 262176 | tf_op jit(solution)/shard_map/ppermute | solution.py:384
  108.8 1.4 %place.1 = bf16[256,1024]{1,0:T(8,128)(2,1)} custom-call(s32[6]{0:T(128)S(1)} %stack.57.idx, bf16[256,512]{1,0:T(8,128)(2,1)S(1)} %last.1.mine_ref, bf16[256,512]{1,0:T(8,128)(2,1)S(1)} %collective-permute-done.25.other_ref), custom_call_target="tpu_custom_call" | custom-call | flops 524288 | bytes 1048576 | tf_op jit(solution)/shard_map/place/pallas_call | solution.py:368
  (31 shorter events, 0.2 us)
Async XLA Ops:
  0.1 1.2 %copy-start.2 = (f32[1,256,1024]{2,1,0:T(8,128)S(1)}, f32[1,256,1024]{2,1,0:T(8,128)}, u32[]{:S(2)}) copy-start(f32[1,256,1024]{2,1,0:T(8,128)} %q_ref.1) | copy-start | bytes 3145732
  1.3 0.9 copy-start.5
  2.3 0.7 copy-start.8
  3.9 3.2 %collective-permute-start = (f32[2,320,256]{2,1,0:T(8,128)S(1)}, f32[2,320,256]{2,1,0:T(8,128)S(1)}, u32[]{:S(2)}, u32[]{:S(2)}) collective-permute-start(f32[2,320,256]{2,1,0:T(8,128)S(1)} %get-tuple-element.18), channel_id=1, source_target_pairs={{0,32},{32,0},{1,33},{33,1},{2,34},{34,2},{3,35},{35,3},{4,36},{36... | collective-permute-start | bytes 1966088 | tf_op jit(solution)/shard_map/ppermute | solution.py:391
  7.3 6.0 %collective-permute-start.1 = (bf16[320,256]{1,0:T(8,128)(2,1)S(1)}, bf16[320,256]{1,0:T(8,128)(2,1)S(1)}, u32[]{:S(2)}, u32[]{:S(2)}) collective-permute-start(bf16[320,256]{1,0:T(8,128)(2,1)S(1)} %fusion.1), channel_id=1, source_target_pairs={{0,64},{64,0},{1,65},{65,1},{2,66},{66,2},{3,67},{67,3},{4,68},{68... | collective-permute-start | bytes 491528 | tf_op jit(solution)/shard_map/ppermute | solution.py:394
  9.1 2.2 %copy-start = (bf16[256,8192]{1,0:T(8,128)(2,1)S(1)}, bf16[256,8192]{1,0:T(8,128)(2,1)}, u32[]{:S(2)}) copy-start(bf16[256,8192]{1,0:T(8,128)(2,1)} %refs_8_.1) | copy-start | bytes 12582916
  13.0 37.0 %copy-start.6 = (f32[256,128]{1,0:T(8,128)}, f32[256,128]{1,0:T(8,128)S(1)}, u32[]{:S(2)}) copy-start(f32[256,128]{1,0:T(8,128)S(1)} %get-tuple-element.23.refs_9_) | copy-start | bytes 393220
  13.3 25.4 %collective-permute-start.14 = (bf16[256,2048]{1,0:T(8,128)(2,1)S(1)}, bf16[256,2048]{1,0:T(8,128)(2,1)S(1)}, u32[]{:S(2)}, u32[]{:S(2)}) collective-permute-start(bf16[256,2048]{1,0:T(8,128)(2,1)S(1)} %get-tuple-element.25), channel_id=1, source_target_pairs={{0,16},{16,0},{1,17},{17,1},{2,18},{18,2},{3,19},{19,3},{4,20},{20... | collective-permute-start | bytes 3145736 | tf_op jit(solution)/shard_map/ppermute | solution.py:410
  16.5 7.0 %collective-permute-start.5 = (bf16[160,256]{1,0:T(8,128)(2,1)S(1)}, bf16[160,256]{1,0:T(8,128)(2,1)S(1)}, u32[]{:S(2)}, u32[]{:S(2)}) collective-permute-start(bf16[160,256]{1,0:T(8,128)(2,1)S(1)} %get-tuple-element.35), channel_id=1, source_target_pairs={{0,4},{4,8},{8,12},{12,0},{1,5},{5,9},{9,13},{13,1},{2,6},{6,10},{... | collective-permute-start | bytes 245768 | tf_op jit(solution)/shard_map/ppermute | solution.py:130
  17.8 6.5 %collective-permute-start.6 = (bf16[160,256]{1,0:T(8,128)(2,1)S(1)}, bf16[160,256]{1,0:T(8,128)(2,1)S(1)}, u32[]{:S(2)}, u32[]{:S(2)}) collective-permute-start(bf16[160,256]{1,0:T(8,128)(2,1)S(1)} %get-tuple-element.35), channel_id=1, source_target_pairs={{0,12},{4,0},{8,4},{12,8},{1,13},{5,1},{9,5},{13,9},{2,14},{6,2},{... | collective-permute-start | bytes 245768 | tf_op jit(solution)/shard_map/ppermute | solution.py:130
  19.3 5.9 %collective-permute-start.7 = (bf16[160,256]{1,0:T(8,128)(2,1)S(1)}, bf16[160,256]{1,0:T(8,128)(2,1)S(1)}, u32[]{:S(2)}, u32[]{:S(2)}) collective-permute-start(bf16[160,256]{1,0:T(8,128)(2,1)S(1)} %get-tuple-element.35), channel_id=1, source_target_pairs={{0,8},{4,12},{8,0},{12,4},{1,9},{5,13},{9,1},{13,5},{2,10},{6,14},... | collective-permute-start | bytes 245768 | tf_op jit(solution)/shard_map/ppermute | solution.py:130
  20.8 4.4 %collective-permute-start.3 = (bf16[160,256]{1,0:T(8,128)(2,1)S(1)}, bf16[160,256]{1,0:T(8,128)(2,1)S(1)}, u32[]{:S(2)}, u32[]{:S(2)}) collective-permute-start(bf16[160,256]{1,0:T(8,128)(2,1)S(1)} %get-tuple-element.36), channel_id=1, source_target_pairs={{0,3},{1,0},{2,1},{3,2},{4,7},{5,4},{6,5},{7,6},{8,11},{9,8},{10,9... | collective-permute-start | bytes 245768 | tf_op jit(solution)/shard_map/ppermute | solution.py:129
  23.5 5.1 %collective-permute-start.4 = (bf16[160,256]{1,0:T(8,128)(2,1)S(1)}, bf16[160,256]{1,0:T(8,128)(2,1)S(1)}, u32[]{:S(2)}, u32[]{:S(2)}) collective-permute-start(bf16[160,256]{1,0:T(8,128)(2,1)S(1)} %get-tuple-element.36), channel_id=1, source_target_pairs={{0,2},{1,3},{2,0},{3,1},{4,6},{5,7},{6,4},{7,5},{8,10},{9,11},{10,... | collective-permute-start | bytes 245768 | tf_op jit(solution)/shard_map/ppermute | solution.py:129
  24.3 5.2 %collective-permute-start.2 = (bf16[160,256]{1,0:T(8,128)(2,1)S(1)}, bf16[160,256]{1,0:T(8,128)(2,1)S(1)}, u32[]{:S(2)}, u32[]{:S(2)}) collective-permute-start(bf16[160,256]{1,0:T(8,128)(2,1)S(1)} %get-tuple-element.36), channel_id=1, source_target_pairs={{0,1},{1,2},{2,3},{3,0},{4,5},{5,6},{6,7},{7,4},{8,9},{9,10},{10,1... | collective-permute-start | bytes 245768 | tf_op jit(solution)/shard_map/ppermute | solution.py:129
  29.6 7.8 %collective-permute-start.10 = (bf16[4,160,256]{2,1,0:T(8,128)(2,1)S(1)}, bf16[4,160,256]{2,1,0:T(8,128)(2,1)S(1)}, u32[]{:S(2)}, u32[]{:S(2)}) collective-permute-start(bf16[4,160,256]{2,1,0:T(8,128)(2,1)S(1)} %pad_maximum_fusion.refs_0_), channel_id=1, source_target_pairs={{0,8},{4,12},{8,0},{12,4},{1,9},{5,13},{9,1},{13,5},{2,10},{6,14},... | collective-permute-start | bytes 983048 | tf_op jit(solution)/shard_map/ppermute | solution.py:132
  31.1 11.1 %collective-permute-start.11 = (bf16[4,160,256]{2,1,0:T(8,128)(2,1)S(1)}, bf16[4,160,256]{2,1,0:T(8,128)(2,1)S(1)}, u32[]{:S(2)}, u32[]{:S(2)}) collective-permute-start(bf16[4,160,256]{2,1,0:T(8,128)(2,1)S(1)} %pad_maximum_fusion.1.refs_4_), channel_id=1, source_target_pairs={{0,1},{1,2},{2,3},{3,0},{4,5},{5,6},{6,7},{7,4},{8,9},{9,10},{10,1... | collective-permute-start | bytes 983048 | tf_op jit(solution)/shard_map/ppermute | solution.py:133
  31.1 18.4 %collective-permute-start.12 = (bf16[4,160,256]{2,1,0:T(8,128)(2,1)S(1)}, bf16[4,160,256]{2,1,0:T(8,128)(2,1)S(1)}, u32[]{:S(2)}, u32[]{:S(2)}) collective-permute-start(bf16[4,160,256]{2,1,0:T(8,128)(2,1)S(1)} %pad_maximum_fusion.1.refs_4_), channel_id=1, source_target_pairs={{0,3},{1,0},{2,1},{3,2},{4,7},{5,4},{6,5},{7,6},{8,11},{9,8},{10,9... | collective-permute-start | bytes 983048 | tf_op jit(solution)/shard_map/ppermute | solution.py:133
  33.8 15.8 %collective-permute-start.13 = (bf16[4,160,256]{2,1,0:T(8,128)(2,1)S(1)}, bf16[4,160,256]{2,1,0:T(8,128)(2,1)S(1)}, u32[]{:S(2)}, u32[]{:S(2)}) collective-permute-start(bf16[4,160,256]{2,1,0:T(8,128)(2,1)S(1)} %pad_maximum_fusion.1.refs_4_), channel_id=1, source_target_pairs={{0,2},{1,3},{2,0},{3,1},{4,6},{5,7},{6,4},{7,5},{8,10},{9,11},{10,... | collective-permute-start | bytes 983048 | tf_op jit(solution)/shard_map/ppermute | solution.py:133
  37.4 12.7 %collective-permute-start.8 = (bf16[4,160,256]{2,1,0:T(8,128)(2,1)S(1)}, bf16[4,160,256]{2,1,0:T(8,128)(2,1)S(1)}, u32[]{:S(2)}, u32[]{:S(2)}) collective-permute-start(bf16[4,160,256]{2,1,0:T(8,128)(2,1)S(1)} %pad_maximum_fusion.refs_0_), channel_id=1, source_target_pairs={{0,4},{4,8},{8,12},{12,0},{1,5},{5,9},{9,13},{13,1},{2,6},{6,10},{... | collective-permute-start | bytes 983048 | tf_op jit(solution)/shard_map/ppermute | solution.py:132
  38.7 11.9 %collective-permute-start.9 = (bf16[4,160,256]{2,1,0:T(8,128)(2,1)S(1)}, bf16[4,160,256]{2,1,0:T(8,128)(2,1)}, u32[]{:S(2)}, u32[]{:S(2)}) collective-permute-start(bf16[4,160,256]{2,1,0:T(8,128)(2,1)S(1)} %pad_maximum_fusion.refs_0_), channel_id=1, source_target_pairs={{0,12},{4,0},{8,4},{12,8},{1,13},{5,1},{9,5},{13,9},{2,14},{6,2},{... | collective-permute-start | bytes 983048 | tf_op jit(solution)/shard_map/ppermute | solution.py:132
  42.2 8.8 %collective-permute-start.15 = (bf16[256,512]{1,0:T(8,128)(2,1)}, bf16[256,512]{1,0:T(8,128)(2,1)}, u32[]{:S(2)}, u32[]{:S(2)}) collective-permute-start(bf16[256,512]{1,0:T(8,128)(2,1)} %get-tuple-element.32), channel_id=1, source_target_pairs={{0,32},{32,0},{1,33},{33,1},{2,34},{34,2},{3,35},{35,3},{4,36},{36... | collective-permute-start | bytes 786440 | tf_op jit(solution)/shard_map/ppermute | solution.py:412
  49.5 1.9 %collective-permute-start.16 = (bf16[256,512]{1,0:T(8,128)(2,1)}, bf16[256,512]{1,0:T(8,128)(2,1)}, u32[]{:S(2)}, u32[]{:S(2)}) collective-permute-start(bf16[256,512]{1,0:T(8,128)(2,1)} %get-tuple-element.31), channel_id=1, source_target_pairs={{0,32},{32,0},{1,33},{33,1},{2,34},{34,2},{3,35},{35,3},{4,36},{36... | collective-permute-start | bytes 786440 | tf_op jit(solution)/shard_map/ppermute | solution.py:412
  49.5 2.2 %collective-permute-start.17 = (bf16[256,512]{1,0:T(8,128)(2,1)}, bf16[256,512]{1,0:T(8,128)(2,1)}, u32[]{:S(2)}, u32[]{:S(2)}) collective-permute-start(bf16[256,512]{1,0:T(8,128)(2,1)} %get-tuple-element.30), channel_id=1, source_target_pairs={{0,32},{32,0},{1,33},{33,1},{2,34},{34,2},{3,35},{35,3},{4,36},{36... | collective-permute-start | bytes 786440 | tf_op jit(solution)/shard_map/ppermute | solution.py:412
  50.0 2.1 %collective-permute-start.18 = (bf16[256,512]{1,0:T(8,128)(2,1)}, bf16[256,512]{1,0:T(8,128)(2,1)}, u32[]{:S(2)}, u32[]{:S(2)}) collective-permute-start(bf16[256,512]{1,0:T(8,128)(2,1)} %get-tuple-element.29), channel_id=1, source_target_pairs={{0,32},{32,0},{1,33},{33,1},{2,34},{34,2},{3,35},{35,3},{4,36},{36... | collective-permute-start | bytes 786440 | tf_op jit(solution)/shard_map/ppermute | solution.py:412
  50.5 4.9 %copy-start.1 = (bf16[256,8192]{1,0:T(8,128)(2,1)S(1)}, bf16[256,8192]{1,0:T(8,128)(2,1)}, u32[]{:S(2)}) copy-start(bf16[256,8192]{1,0:T(8,128)(2,1)} %refs_8_.1) | copy-start | bytes 12582916
  50.5 4.9 %copy-start.7 = (f32[256,128]{1,0:T(8,128)S(1)}, f32[256,128]{1,0:T(8,128)}, u32[]{:S(2)}) copy-start(f32[256,128]{1,0:T(8,128)} %copy-done.6) | copy-start | bytes 393220
  55.2 7.0 %collective-permute-start.19 = (bf16[320,256]{1,0:T(8,128)(2,1)S(1)}, bf16[320,256]{1,0:T(8,128)(2,1)S(1)}, u32[]{:S(2)}, u32[]{:S(2)}) collective-permute-start(bf16[320,256]{1,0:T(8,128)(2,1)S(1)} %theirs.1), channel_id=1, source_target_pairs={{0,16},{16,0},{1,17},{17,1},{2,18},{18,2},{3,19},{19,3},{4,20},{20... | collective-permute-start | bytes 491528 | tf_op jit(solution)/shard_map/ppermute | solution.py:427
  58.2 0.7 copy-start.3
  63.4 25.7 %all-to-all-start = ((bf16[128,32,128]{2,1,0:T(8,128)(2,1)}), bf16[128,32,128]{2,1,0:T(8,128)(2,1)S(1)}, u32[]{:S(2)}, u32[]{:S(2)}) async-start(bf16[128,32,128]{2,1,0:T(8,128)(2,1)} %bitcast.16), calls=%async_computation | async-start | bytes 2097152 | tf_op jit(solution)/shard_map/all_to_all | solution.py:433
  70.7 1.0 copy-start.4
  72.1 15.4 %collective-permute-start.21 = (bf16[2,128,256]{2,1,0:T(8,128)(2,1)S(1)}, bf16[2,128,256]{2,1,0:T(8,128)(2,1)S(1)}, u32[]{:S(2)}, u32[]{:S(2)}) collective-permute-start(bf16[2,128,256]{2,1,0:T(8,128)(2,1)S(1)} %q_finish.1.refs_0_), channel_id=1, source_target_pairs={{0,64},{64,0},{1,65},{65,1},{2,66},{66,2},{3,67},{67,3},{4,68},{68... | collective-permute-start | bytes 393224 | tf_op jit(solution)/shard_map/ppermute | solution.py:386
  73.7 14.4 %collective-permute-start.20 = (bf16[2,128,256]{2,1,0:T(8,128)(2,1)S(1)}, bf16[2,128,256]{2,1,0:T(8,128)(2,1)S(1)}, u32[]{:S(2)}, u32[]{:S(2)}) collective-permute-start(bf16[2,128,256]{2,1,0:T(8,128)(2,1)S(1)} %q_finish.1.refs_0_), channel_id=1, source_target_pairs={{0,32},{32,0},{1,33},{33,1},{2,34},{34,2},{3,35},{35,3},{4,36},{36... | collective-permute-start | bytes 393224 | tf_op jit(solution)/shard_map/ppermute | solution.py:384
  87.5 1.6 %collective-permute-start.22 = (bf16[2,128,256]{2,1,0:T(8,128)(2,1)S(1)}, bf16[2,128,256]{2,1,0:T(8,128)(2,1)S(1)}, u32[]{:S(2)}, u32[]{:S(2)}) collective-permute-start(bf16[2,128,256]{2,1,0:T(8,128)(2,1)S(1)} %collective-permute-done.21.refs_2_), channel_id=1, source_target_pairs={{0,32},{32,0},{1,33},{33,1},{2,34},{34,2},{3,35},{35,3},{4,36},{36... | collective-permute-start | bytes 393224 | tf_op jit(solution)/shard_map/ppermute | solution.py:384
  95.3 2.3 %collective-permute-start.23 = (bf16[576,256]{1,0:T(8,128)(2,1)S(1)}, bf16[576,256]{1,0:T(8,128)(2,1)S(1)}, u32[]{:S(2)}, u32[]{:S(2)}) collective-permute-start(bf16[576,256]{1,0:T(8,128)(2,1)S(1)} %get-tuple-element.28), channel_id=1, source_target_pairs={{0,32},{32,0},{1,33},{33,1},{2,34},{34,2},{3,35},{35,3},{4,36},{36... | collective-permute-start | bytes 884744 | tf_op jit(solution)/shard_map/ppermute | solution.py:384
  97.8 8.3 %collective-permute-start.24 = (bf16[576,256]{1,0:T(8,128)(2,1)S(1)}, bf16[576,256]{1,0:T(8,128)(2,1)S(1)}, u32[]{:S(2)}, u32[]{:S(2)}) collective-permute-start(bf16[576,256]{1,0:T(8,128)(2,1)S(1)} %merge.1.a_ref), channel_id=1, source_target_pairs={{0,64},{64,0},{1,65},{65,1},{2,66},{66,2},{3,67},{67,3},{4,68},{68... | collective-permute-start | bytes 884744 | tf_op jit(solution)/shard_map/ppermute | solution.py:386
  106.3 2.4 %collective-permute-start.25 = (bf16[256,512]{1,0:T(8,128)(2,1)S(1)}, bf16[256,512]{1,0:T(8,128)(2,1)S(1)}, u32[]{:S(2)}, u32[]{:S(2)}) collective-permute-start(bf16[256,512]{1,0:T(8,128)(2,1)S(1)} %last.1.mine_ref), channel_id=1, source_target_pairs={{0,32},{32,0},{1,33},{33,1},{2,34},{34,2},{3,35},{35,3},{4,36},{36... | collective-permute-start | bytes 786440 | tf_op jit(solution)/shard_map/ppermute | solution.py:384

commit v5 on v4

--- a/solution.py
+++ b/solution.py
@@ -182,8 +182,10 @@
         return jnp.where(at // 8 == idx[1], xa_ref[:, cols], xb_ref[:, cols])
 
     q, pair = accumulate(idx, w_refs, block)
+    high = pair.astype(BF16)
     out_ref[0:256] = q.astype(BF16)
-    out_ref[256:320] = pair.astype(BF16)
+    out_ref[256:320] = high
+    out_ref[320:384] = (pair - high.astype(F32)).astype(BF16)
 
 
 def project(kernel, args, outs, name, scratch=()):
@@ -200,7 +202,7 @@
 
 
 def pair_finish_kernel(own_ref, got_ref, cos_ref, sin_ref, out_ref):
-    t = own_ref[...] + got_ref[256:320].astype(F32)
+    t = own_ref[...] + (got_ref[256:320].astype(F32) + got_ref[320:384].astype(F32))
     u, w = t[0:16], t[16:32]
     cos, sin = cos_ref[...], sin_ref[...]
     key = jnp.concatenate([u * cos - w * sin, w * cos + u * sin], axis=0)
@@ -422,7 +424,7 @@
     cos_t, sin_t = jnp.cos(angles_t), jnp.sin(angles_t)
 
     (theirs,) = project(
-        theirs_kernel, (idx, *w_all, got, *other), [jax.ShapeDtypeStruct((320, 256), BF16)],
+        theirs_kernel, (idx, *w_all, got, *other), [jax.ShapeDtypeStruct((384, 256), BF16)],
         "theirs", [VMEM((256, 2048), BF16)])
     back = lax.ppermute(theirs, "zh", SWAP)
     q_own, pair_own = project(

time: 111 us -> 111 us (level)
  no operation moved by 1% of the time
where the time goes in v5:
time: 111 us
  starting transfers between devices  42.2 us (38%)
  waiting for transfers between devices  41.2 us (37%)
  Pallas kernels  18.1 us (16%)
  local copies, waits for them, and re-layouts  7.84 us (7%)
    ppermute x2, waiting for transfers between devices, to_rep(): return lax.ppermute(x, 'zl', SWAP)  20.9 us
    ppermute x4, starting transfers between devices, local(): lax.ppermute(got[:, i * width:(i + 1) * width], 'c', SWAP)  8.33 us
    unnamed x18, local copies, waits for them, and re-layouts  6.67 us
    all_to_all x1, starting transfers between devices, local(): lax.all_to_all(pair.reshape(128, 32, 128), ('zh', 'x', 'y', 'zl', 'c'), 0...  6.43 us
    pallas_call x1, Pallas kernels, attend(): pl.pallas_call(attend_kernel, in_specs=[sspec()] + [vspec()] * 5, out_spe...  6.21 us
    pallas_call x2, Pallas kernels, project(): pl.pallas_call(kernel, scratch_shapes=scratch, in_specs=[sspec()] + [vspe...  5.77 us
    ppermute x3, starting transfers between devices, gather_plane(): lowers = [lower] + [lax.ppermute(lower, 'x', ring(d)) for d in (1, 3, 2)]  4.31 us
    ppermute x3, starting transfers between devices, gather_plane(): lax.ppermute(upper, 'x', ring(d))  4.28 us
  transfers between devices with their start and end apart: 27, of which 17 were waited for; matrix products, arithmetic and copies ran while one was open for 2% of the time, Pallas kernels for 4%

profile of v5, /device:TPU:1, one launch (start us, length us, event | category | flops | bytes accessed | tf_op | source)
XLA Modules:
  0.0 110.5 jit_solution(16362276106213957220)
XLA Ops:
  0.0 0.1 stack.57.idx
  0.1 1.2 %copy-done.2 = f32[1,256,1024]{2,1,0:T(8,128)S(1)} copy-done((f32[1,256,1024]{2,1,0:T(8,128)S(1)}, f32[1,256,1024]{2,1,0:T(8,128)}, u32[]{:S(2)}) %copy-start.2) | copy-done | bytes 1048600
  1.3 0.9 copy-done.5
  2.3 0.7 copy-done.8
  2.9 1.0 prepare.1
  3.9 1.5 %collective-permute-start = (f32[2,320,256]{2,1,0:T(8,128)S(1)}, f32[2,320,256]{2,1,0:T(8,128)S(1)}, u32[]{:S(2)}, u32[]{:S(2)}) collective-permute-start(f32[2,320,256]{2,1,0:T(8,128)S(1)} %get-tuple-element.18), channel_id=1, source_target_pairs={{0,32},{32,0},{1,33},{33,1},{2,34},{34,2},{3,35},{35,3},{4,36},{36... | collective-permute-start | bytes 1966088 | tf_op jit(solution)/shard_map/ppermute | solution.py:393
  5.4 1.7 %collective-permute-done = f32[2,320,256]{2,1,0:T(8,128)S(1)} collective-permute-done((f32[2,320,256]{2,1,0:T(8,128)S(1)}, f32[2,320,256]{2,1,0:T(8,128)S(1)}, u32[]{:S(2)}, u32[]{:S(2)}) %collective-permute-start) | collective-permute-done | bytes 655392 | tf_op jit(solution)/shard_map/ppermute | solution.py:393
  7.1 0.1 add.35
  7.3 1.8 %collective-permute-start.1 = (bf16[320,256]{1,0:T(8,128)(2,1)S(1)}, bf16[320,256]{1,0:T(8,128)(2,1)S(1)}, u32[]{:S(2)}, u32[]{:S(2)}) collective-permute-start(bf16[320,256]{1,0:T(8,128)(2,1)S(1)} %fusion.1), channel_id=1, source_target_pairs={{0,64},{64,0},{1,65},{65,1},{2,66},{66,2},{3,67},{67,3},{4,68},{68... | collective-permute-start | bytes 491528 | tf_op jit(solution)/shard_map/ppermute | solution.py:396
  9.1 2.2 %copy-done = bf16[256,8192]{1,0:T(8,128)(2,1)S(1)} copy-done((bf16[256,8192]{1,0:T(8,128)(2,1)S(1)}, bf16[256,8192]{1,0:T(8,128)(2,1)}, u32[]{:S(2)}) %copy-start) | copy-done | bytes 4194328
  11.3 1.8 %normalise.1 = (f32[256,128]{1,0:T(8,128)S(1)}, bf16[256,2048]{1,0:T(8,128)(2,1)S(1)}) custom-call(s32[6]{0:T(128)S(1)} %stack.57.idx, bf16[256,8192]{1,0:T(8,128)(2,1)S(1)} %copy-done), custom_call_target="tpu_custom_call" | custom-call | flops 8388608 | bytes 6291456 | tf_op jit(solution)/shard_map/normalise/pallas_call | solution.py:64
  13.0 0.3 collective-permute-done.1
  13.3 3.1 %collective-permute-start.14 = (bf16[256,2048]{1,0:T(8,128)(2,1)S(1)}, bf16[256,2048]{1,0:T(8,128)(2,1)S(1)}, u32[]{:S(2)}, u32[]{:S(2)}) collective-permute-start(bf16[256,2048]{1,0:T(8,128)(2,1)S(1)} %get-tuple-element.25), channel_id=1, source_target_pairs={{0,16},{16,0},{1,17},{17,1},{2,18},{18,2},{3,19},{19,3},{4,20},{20... | collective-permute-start | bytes 3145736 | tf_op jit(solution)/shard_map/ppermute | solution.py:412
  16.4 0.1 fusion
  16.5 1.3 %collective-permute-start.5 = (bf16[160,256]{1,0:T(8,128)(2,1)S(1)}, bf16[160,256]{1,0:T(8,128)(2,1)S(1)}, u32[]{:S(2)}, u32[]{:S(2)}) collective-permute-start(bf16[160,256]{1,0:T(8,128)(2,1)S(1)} %get-tuple-element.35), channel_id=1, source_target_pairs={{0,4},{4,8},{8,12},{12,0},{1,5},{5,9},{9,13},{13,1},{2,6},{6,10},{... | collective-permute-start | bytes 245768 | tf_op jit(solution)/shard_map/ppermute | solution.py:130
  17.8 1.5 %collective-permute-start.6 = (bf16[160,256]{1,0:T(8,128)(2,1)S(1)}, bf16[160,256]{1,0:T(8,128)(2,1)S(1)}, u32[]{:S(2)}, u32[]{:S(2)}) collective-permute-start(bf16[160,256]{1,0:T(8,128)(2,1)S(1)} %get-tuple-element.35), channel_id=1, source_target_pairs={{0,12},{4,0},{8,4},{12,8},{1,13},{5,1},{9,5},{13,9},{2,14},{6,2},{... | collective-permute-start | bytes 245768 | tf_op jit(solution)/shard_map/ppermute | solution.py:130
  19.3 1.5 %collective-permute-start.7 = (bf16[160,256]{1,0:T(8,128)(2,1)S(1)}, bf16[160,256]{1,0:T(8,128)(2,1)S(1)}, u32[]{:S(2)}, u32[]{:S(2)}) collective-permute-start(bf16[160,256]{1,0:T(8,128)(2,1)S(1)} %get-tuple-element.35), channel_id=1, source_target_pairs={{0,8},{4,12},{8,0},{12,4},{1,9},{5,13},{9,1},{13,5},{2,10},{6,14},... | collective-permute-start | bytes 245768 | tf_op jit(solution)/shard_map/ppermute | solution.py:130
  20.8 2.7 %collective-permute-start.3 = (bf16[160,256]{1,0:T(8,128)(2,1)S(1)}, bf16[160,256]{1,0:T(8,128)(2,1)S(1)}, u32[]{:S(2)}, u32[]{:S(2)}) collective-permute-start(bf16[160,256]{1,0:T(8,128)(2,1)S(1)} %get-tuple-element.36), channel_id=1, source_target_pairs={{0,3},{1,0},{2,1},{3,2},{4,7},{5,4},{6,5},{7,6},{8,11},{9,8},{10,9... | collective-permute-start | bytes 245768 | tf_op jit(solution)/shard_map/ppermute | solution.py:129
  23.5 0.8 collective-permute-start.4
  24.3 0.4 collective-permute-start.2
  24.7 0.5 collective-permute-done.7
  25.3 3.4 %collective-permute-done.4 = bf16[160,256]{1,0:T(8,128)(2,1)S(1)} collective-permute-done((bf16[160,256]{1,0:T(8,128)(2,1)S(1)}, bf16[160,256]{1,0:T(8,128)(2,1)S(1)}, u32[]{:S(2)}, u32[]{:S(2)}) %collective-permute-start.4) | collective-permute-done | bytes 81952 | tf_op jit(solution)/shard_map/ppermute | solution.py:129
  28.6 0.9 collective-permute-done.2
  29.6 1.5 %collective-permute-start.10 = (bf16[4,160,256]{2,1,0:T(8,128)(2,1)S(1)}, bf16[4,160,256]{2,1,0:T(8,128)(2,1)S(1)}, u32[]{:S(2)}, u32[]{:S(2)}) collective-permute-start(bf16[4,160,256]{2,1,0:T(8,128)(2,1)S(1)} %pad_maximum_fusion.refs_0_), channel_id=1, source_target_pairs={{0,8},{4,12},{8,0},{12,4},{1,9},{5,13},{9,1},{13,5},{2,10},{6,14},... | collective-permute-start | bytes 983048 | tf_op jit(solution)/shard_map/ppermute | solution.py:132
  31.1 2.7 %collective-permute-start.12 = (bf16[4,160,256]{2,1,0:T(8,128)(2,1)S(1)}, bf16[4,160,256]{2,1,0:T(8,128)(2,1)S(1)}, u32[]{:S(2)}, u32[]{:S(2)}) collective-permute-start(bf16[4,160,256]{2,1,0:T(8,128)(2,1)S(1)} %pad_maximum_fusion.1.refs_4_), channel_id=1, source_target_pairs={{0,3},{1,0},{2,1},{3,2},{4,7},{5,4},{6,5},{7,6},{8,11},{9,8},{10,9... | collective-permute-start | bytes 983048 | tf_op jit(solution)/shard_map/ppermute | solution.py:133
  33.8 3.6 %collective-permute-done.10.refs_3_ = bf16[4,160,256]{2,1,0:T(8,128)(2,1)S(1)} collective-permute-done((bf16[4,160,256]{2,1,0:T(8,128)(2,1)S(1)}, bf16[4,160,256]{2,1,0:T(8,128)(2,1)S(1)}, u32[]{:S(2)}, u32[]{:S(2)}) %collective-permute-start.10) | collective-permute-done | bytes 327712 | tf_op jit(solution)/shard_map/ppermute | solution.py:132
  37.4 0.3 collective-permute-start.8
  37.7 1.0 collective-permute-done.14.refs_8_
  38.7 2.5 %collective-permute-start.9 = (bf16[4,160,256]{2,1,0:T(8,128)(2,1)S(1)}, bf16[4,160,256]{2,1,0:T(8,128)(2,1)}, u32[]{:S(2)}, u32[]{:S(2)}) collective-permute-start(bf16[4,160,256]{2,1,0:T(8,128)(2,1)S(1)} %pad_maximum_fusion.refs_0_), channel_id=1, source_target_pairs={{0,12},{4,0},{8,4},{12,8},{1,13},{5,1},{9,5},{13,9},{2,14},{6,2},{... | collective-permute-start | bytes 983048 | tf_op jit(solution)/shard_map/ppermute | solution.py:132
  41.2 1.0 fusion.2
  42.2 7.3 %collective-permute-start.15 = (bf16[256,512]{1,0:T(8,128)(2,1)}, bf16[256,512]{1,0:T(8,128)(2,1)}, u32[]{:S(2)}, u32[]{:S(2)}) collective-permute-start(bf16[256,512]{1,0:T(8,128)(2,1)} %get-tuple-element.32), channel_id=1, source_target_pairs={{0,32},{32,0},{1,33},{33,1},{2,34},{34,2},{3,35},{35,3},{4,36},{36... | collective-permute-start | bytes 786440 | tf_op jit(solution)/shard_map/ppermute | solution.py:414
  49.5 0.5 collective-permute-start.17
  50.0 0.5 collective-permute-start.18
  50.5 0.1 dynamic_slice.3
  50.6 0.4 collective-permute-done.15.refs_9_
  51.0 0.4 collective-permute-done.16.refs_10_
  51.4 0.4 collective-permute-done.17.refs_11_
  51.8 0.4 collective-permute-done.18.refs_12_
  52.1 3.1 %theirs.1 = bf16[384,256]{1,0:T(8,128)(2,1)S(1)} custom-call(s32[6]{0:T(128)S(1)} %stack.57.idx, bf16[4,160,256]{2,1,0:T(8,128)(2,1)S(1)} %pad_maximum_fusion.refs_0_, bf16[4,160,256]{2,1,0:T(8,128)(2,1)S(1)} %collective-permute-done.8.refs_1_, bf16[4,160,256]{2,1,0:T(8,128)(2,1)} %collective-permute-done.9.refs_2_, ...), custom_call_target="tpu_custom_call" | custom-call | flops 671088640 | bytes 5242880 | tf_op jit(solution)/shard_map/theirs/pallas_call | solution.py:192
  55.2 0.1 collective-permute-start.19
  55.3 0.1 multiply_sine_fusion.1
  55.5 2.7 %own.1 = (f32[256,256]{1,0:T(8,128)S(1)}, f32[64,256]{1,0:T(8,128)S(1)}) custom-call(s32[6]{0:T(128)S(1)} %stack.57.idx, bf16[4,160,256]{2,1,0:T(8,128)(2,1)S(1)} %pad_maximum_fusion.refs_0_, bf16[4,160,256]{2,1,0:T(8,128)(2,1)S(1)} %collective-permute-done.8.refs_1_, bf16[4,160,256]{2,1,0:T(8,128)(2,1)} %collective-permute-done.9.refs_2_, ...), custom_call_target="tpu_custom_call" | custom-call | flops 671088640 | bytes 5242880 | tf_op jit(solution)/shard_map/own/pallas_call | solution.py:192
  58.2 0.7 copy-done.3
  58.9 4.0 %collective-permute-done.19.got_ref = bf16[384,256]{1,0:T(8,128)(2,1)S(1)} collective-permute-done((bf16[384,256]{1,0:T(8,128)(2,1)S(1)}, bf16[384,256]{1,0:T(8,128)(2,1)S(1)}, u32[]{:S(2)}, u32[]{:S(2)}) %collective-permute-start.19) | collective-permute-done | bytes 196640 | tf_op jit(solution)/shard_map/ppermute | solution.py:429
  62.9 1.2 %pair_finish.1 = bf16[32,4,32,128]{3,2,1,0:T(8,128)(2,1)} custom-call(f32[64,256]{1,0:T(8,128)S(1)} %get-tuple-element.26.own_ref, bf16[384,256]{1,0:T(8,128)(2,1)S(1)} %collective-permute-done.19.got_ref, f32[16,256]{1,0:T(8,128)S(1)} %get-tuple-element.38.cos_ref, f32[16,256]{1,0:T(8,128)S(1)} %get-tuple-element.37.sin_ref), custom_call_target="tpu_custom_call" | custom-call | flops 262144 | bytes 1048576 | tf_op jit(solution)/shard_map/pair_finish/pallas_call | solution.py:228
  64.1 6.4 %all-to-all-start = ((bf16[128,32,128]{2,1,0:T(8,128)(2,1)}), bf16[128,32,128]{2,1,0:T(8,128)(2,1)S(1)}, u32[]{:S(2)}, u32[]{:S(2)}) async-start(bf16[128,32,128]{2,1,0:T(8,128)(2,1)} %bitcast.16), calls=%async_computation | async-start | bytes 2097152 | tf_op jit(solution)/shard_map/all_to_all | solution.py:435
  70.5 0.5 multiply_sine_fusion
  71.1 0.9 copy-done.4
  72.0 0.4 q_finish.1.refs_0_
  72.4 1.6 %collective-permute-start.21 = (bf16[2,128,256]{2,1,0:T(8,128)(2,1)S(1)}, bf16[2,128,256]{2,1,0:T(8,128)(2,1)S(1)}, u32[]{:S(2)}, u32[]{:S(2)}) collective-permute-start(bf16[2,128,256]{2,1,0:T(8,128)(2,1)S(1)} %q_finish.1.refs_0_), channel_id=1, source_target_pairs={{0,64},{64,0},{1,65},{65,1},{2,66},{66,2},{3,67},{67,3},{4,68},{68... | collective-permute-start | bytes 393224 | tf_op jit(solution)/shard_map/ppermute | solution.py:388
  74.0 0.6 collective-permute-start.20
  74.6 13.2 %collective-permute-done.21.refs_2_ = bf16[2,128,256]{2,1,0:T(8,128)(2,1)S(1)} collective-permute-done((bf16[2,128,256]{2,1,0:T(8,128)(2,1)S(1)}, bf16[2,128,256]{2,1,0:T(8,128)(2,1)S(1)}, u32[]{:S(2)}, u32[]{:S(2)}) %collective-permute-start.21) | collective-permute-done | bytes 131104 | tf_op jit(solution)/shard_map/ppermute | solution.py:388
  87.8 0.6 collective-permute-start.22
  88.5 1.0 collective-permute-done.22.refs_3_
  89.5 6.2 %attend.1 = (bf16[576,256]{1,0:T(8,128)(2,1)S(1)}, bf16[576,256]{1,0:T(8,128)(2,1)S(1)}) custom-call(s32[6]{0:T(128)S(1)} %stack.57.idx, bf16[2,128,256]{2,1,0:T(8,128)(2,1)S(1)} %q_finish.1.refs_0_, bf16[2,128,256]{2,1,0:T(8,128)(2,1)S(1)} %collective-permute-done.20.refs_1_, bf16[2,128,256]{2,1,0:T(8,128)(2,1)S(1)} %collective-permute-done.21.refs_2_, ...), custom_call_target="tpu_custom_call" | custom-call | flops 2147483648 | bytes 4194304 | tf_op jit(solution)/shard_map/attend/pallas_call | solution.py:309
  95.7 1.1 collective-permute-start.23
  96.8 1.2 %collective-permute-done.23.b_ref = bf16[576,256]{1,0:T(8,128)(2,1)S(1)} collective-permute-done((bf16[576,256]{1,0:T(8,128)(2,1)S(1)}, bf16[576,256]{1,0:T(8,128)(2,1)S(1)}, u32[]{:S(2)}, u32[]{:S(2)}) %collective-permute-start.23) | collective-permute-done | bytes 294944 | tf_op jit(solution)/shard_map/ppermute | solution.py:386
  98.0 0.2 merge.1.a_ref
  98.1 0.6 collective-permute-start.24
  98.7 7.7 %collective-permute-done.24.b_ref = bf16[576,256]{1,0:T(8,128)(2,1)S(1)} collective-permute-done((bf16[576,256]{1,0:T(8,128)(2,1)S(1)}, bf16[576,256]{1,0:T(8,128)(2,1)S(1)}, u32[]{:S(2)}, u32[]{:S(2)}) %collective-permute-start.24) | collective-permute-done | bytes 294944 | tf_op jit(solution)/shard_map/ppermute | solution.py:388
  106.4 0.2 last.1.mine_ref
  106.7 1.3 %collective-permute-start.25 = (bf16[256,512]{1,0:T(8,128)(2,1)S(1)}, bf16[256,512]{1,0:T(8,128)(2,1)S(1)}, u32[]{:S(2)}, u32[]{:S(2)}) collective-permute-start(bf16[256,512]{1,0:T(8,128)(2,1)S(1)} %last.1.mine_ref), channel_id=1, source_target_pairs={{0,32},{32,0},{1,33},{33,1},{2,34},{34,2},{3,35},{35,3},{4,36},{36... | collective-permute-start | bytes 786440 | tf_op jit(solution)/shard_map/ppermute | solution.py:386
  107.9 1.2 %collective-permute-done.25.other_ref = bf16[256,512]{1,0:T(8,128)(2,1)S(1)} collective-permute-done((bf16[256,512]{1,0:T(8,128)(2,1)S(1)}, bf16[256,512]{1,0:T(8,128)(2,1)S(1)}, u32[]{:S(2)}, u32[]{:S(2)}) %collective-permute-start.25) | collective-permute-done | bytes 262176 | tf_op jit(solution)/shard_map/ppermute | solution.py:386
  109.1 1.4 %place.1 = bf16[256,1024]{1,0:T(8,128)(2,1)} custom-call(s32[6]{0:T(128)S(1)} %stack.57.idx, bf16[256,512]{1,0:T(8,128)(2,1)S(1)} %last.1.mine_ref, bf16[256,512]{1,0:T(8,128)(2,1)S(1)} %collective-permute-done.25.other_ref), custom_call_target="tpu_custom_call" | custom-call | flops 524288 | bytes 1048576 | tf_op jit(solution)/shard_map/place/pallas_call | solution.py:370
  (31 shorter events, 0.2 us)
Async XLA Ops:
  0.1 1.2 %copy-start.2 = (f32[1,256,1024]{2,1,0:T(8,128)S(1)}, f32[1,256,1024]{2,1,0:T(8,128)}, u32[]{:S(2)}) copy-start(f32[1,256,1024]{2,1,0:T(8,128)} %q_ref.1) | copy-start | bytes 3145732
  1.3 0.9 copy-start.5
  2.3 0.7 copy-start.8
  3.9 3.2 %collective-permute-start = (f32[2,320,256]{2,1,0:T(8,128)S(1)}, f32[2,320,256]{2,1,0:T(8,128)S(1)}, u32[]{:S(2)}, u32[]{:S(2)}) collective-permute-start(f32[2,320,256]{2,1,0:T(8,128)S(1)} %get-tuple-element.18), channel_id=1, source_target_pairs={{0,32},{32,0},{1,33},{33,1},{2,34},{34,2},{3,35},{35,3},{4,36},{36... | collective-permute-start | bytes 1966088 | tf_op jit(solution)/shard_map/ppermute | solution.py:393
  7.3 6.0 %collective-permute-start.1 = (bf16[320,256]{1,0:T(8,128)(2,1)S(1)}, bf16[320,256]{1,0:T(8,128)(2,1)S(1)}, u32[]{:S(2)}, u32[]{:S(2)}) collective-permute-start(bf16[320,256]{1,0:T(8,128)(2,1)S(1)} %fusion.1), channel_id=1, source_target_pairs={{0,64},{64,0},{1,65},{65,1},{2,66},{66,2},{3,67},{67,3},{4,68},{68... | collective-permute-start | bytes 491528 | tf_op jit(solution)/shard_map/ppermute | solution.py:396
  9.1 2.2 %copy-start = (bf16[256,8192]{1,0:T(8,128)(2,1)S(1)}, bf16[256,8192]{1,0:T(8,128)(2,1)}, u32[]{:S(2)}) copy-start(bf16[256,8192]{1,0:T(8,128)(2,1)} %refs_8_.1) | copy-start | bytes 12582916
  13.0 37.0 %copy-start.6 = (f32[256,128]{1,0:T(8,128)}, f32[256,128]{1,0:T(8,128)S(1)}, u32[]{:S(2)}) copy-start(f32[256,128]{1,0:T(8,128)S(1)} %get-tuple-element.23.refs_9_) | copy-start | bytes 393220
  13.3 25.4 %collective-permute-start.14 = (bf16[256,2048]{1,0:T(8,128)(2,1)S(1)}, bf16[256,2048]{1,0:T(8,128)(2,1)S(1)}, u32[]{:S(2)}, u32[]{:S(2)}) collective-permute-start(bf16[256,2048]{1,0:T(8,128)(2,1)S(1)} %get-tuple-element.25), channel_id=1, source_target_pairs={{0,16},{16,0},{1,17},{17,1},{2,18},{18,2},{3,19},{19,3},{4,20},{20... | collective-permute-start | bytes 3145736 | tf_op jit(solution)/shard_map/ppermute | solution.py:412
  16.5 7.0 %collective-permute-start.5 = (bf16[160,256]{1,0:T(8,128)(2,1)S(1)}, bf16[160,256]{1,0:T(8,128)(2,1)S(1)}, u32[]{:S(2)}, u32[]{:S(2)}) collective-permute-start(bf16[160,256]{1,0:T(8,128)(2,1)S(1)} %get-tuple-element.35), channel_id=1, source_target_pairs={{0,4},{4,8},{8,12},{12,0},{1,5},{5,9},{9,13},{13,1},{2,6},{6,10},{... | collective-permute-start | bytes 245768 | tf_op jit(solution)/shard_map/ppermute | solution.py:130
  17.8 6.5 %collective-permute-start.6 = (bf16[160,256]{1,0:T(8,128)(2,1)S(1)}, bf16[160,256]{1,0:T(8,128)(2,1)S(1)}, u32[]{:S(2)}, u32[]{:S(2)}) collective-permute-start(bf16[160,256]{1,0:T(8,128)(2,1)S(1)} %get-tuple-element.35), channel_id=1, source_target_pairs={{0,12},{4,0},{8,4},{12,8},{1,13},{5,1},{9,5},{13,9},{2,14},{6,2},{... | collective-permute-start | bytes 245768 | tf_op jit(solution)/shard_map/ppermute | solution.py:130
  19.3 5.9 %collective-permute-start.7 = (bf16[160,256]{1,0:T(8,128)(2,1)S(1)}, bf16[160,256]{1,0:T(8,128)(2,1)S(1)}, u32[]{:S(2)}, u32[]{:S(2)}) collective-permute-start(bf16[160,256]{1,0:T(8,128)(2,1)S(1)} %get-tuple-element.35), channel_id=1, source_target_pairs={{0,8},{4,12},{8,0},{12,4},{1,9},{5,13},{9,1},{13,5},{2,10},{6,14},... | collective-permute-start | bytes 245768 | tf_op jit(solution)/shard_map/ppermute | solution.py:130
  20.8 4.4 %collective-permute-start.3 = (bf16[160,256]{1,0:T(8,128)(2,1)S(1)}, bf16[160,256]{1,0:T(8,128)(2,1)S(1)}, u32[]{:S(2)}, u32[]{:S(2)}) collective-permute-start(bf16[160,256]{1,0:T(8,128)(2,1)S(1)} %get-tuple-element.36), channel_id=1, source_target_pairs={{0,3},{1,0},{2,1},{3,2},{4,7},{5,4},{6,5},{7,6},{8,11},{9,8},{10,9... | collective-permute-start | bytes 245768 | tf_op jit(solution)/shard_map/ppermute | solution.py:129
  23.5 5.1 %collective-permute-start.4 = (bf16[160,256]{1,0:T(8,128)(2,1)S(1)}, bf16[160,256]{1,0:T(8,128)(2,1)S(1)}, u32[]{:S(2)}, u32[]{:S(2)}) collective-permute-start(bf16[160,256]{1,0:T(8,128)(2,1)S(1)} %get-tuple-element.36), channel_id=1, source_target_pairs={{0,2},{1,3},{2,0},{3,1},{4,6},{5,7},{6,4},{7,5},{8,10},{9,11},{10,... | collective-permute-start | bytes 245768 | tf_op jit(solution)/shard_map/ppermute | solution.py:129
  24.3 5.2 %collective-permute-start.2 = (bf16[160,256]{1,0:T(8,128)(2,1)S(1)}, bf16[160,256]{1,0:T(8,128)(2,1)S(1)}, u32[]{:S(2)}, u32[]{:S(2)}) collective-permute-start(bf16[160,256]{1,0:T(8,128)(2,1)S(1)} %get-tuple-element.36), channel_id=1, source_target_pairs={{0,1},{1,2},{2,3},{3,0},{4,5},{5,6},{6,7},{7,4},{8,9},{9,10},{10,1... | collective-permute-start | bytes 245768 | tf_op jit(solution)/shard_map/ppermute | solution.py:129
  29.6 7.8 %collective-permute-start.10 = (bf16[4,160,256]{2,1,0:T(8,128)(2,1)S(1)}, bf16[4,160,256]{2,1,0:T(8,128)(2,1)S(1)}, u32[]{:S(2)}, u32[]{:S(2)}) collective-permute-start(bf16[4,160,256]{2,1,0:T(8,128)(2,1)S(1)} %pad_maximum_fusion.refs_0_), channel_id=1, source_target_pairs={{0,8},{4,12},{8,0},{12,4},{1,9},{5,13},{9,1},{13,5},{2,10},{6,14},... | collective-permute-start | bytes 983048 | tf_op jit(solution)/shard_map/ppermute | solution.py:132
  31.1 11.1 %collective-permute-start.11 = (bf16[4,160,256]{2,1,0:T(8,128)(2,1)S(1)}, bf16[4,160,256]{2,1,0:T(8,128)(2,1)S(1)}, u32[]{:S(2)}, u32[]{:S(2)}) collective-permute-start(bf16[4,160,256]{2,1,0:T(8,128)(2,1)S(1)} %pad_maximum_fusion.1.refs_4_), channel_id=1, source_target_pairs={{0,1},{1,2},{2,3},{3,0},{4,5},{5,6},{6,7},{7,4},{8,9},{9,10},{10,1... | collective-permute-start | bytes 983048 | tf_op jit(solution)/shard_map/ppermute | solution.py:133
  31.1 18.4 %collective-permute-start.12 = (bf16[4,160,256]{2,1,0:T(8,128)(2,1)S(1)}, bf16[4,160,256]{2,1,0:T(8,128)(2,1)S(1)}, u32[]{:S(2)}, u32[]{:S(2)}) collective-permute-start(bf16[4,160,256]{2,1,0:T(8,128)(2,1)S(1)} %pad_maximum_fusion.1.refs_4_), channel_id=1, source_target_pairs={{0,3},{1,0},{2,1},{3,2},{4,7},{5,4},{6,5},{7,6},{8,11},{9,8},{10,9... | collective-permute-start | bytes 983048 | tf_op jit(solution)/shard_map/ppermute | solution.py:133
  33.8 15.8 %collective-permute-start.13 = (bf16[4,160,256]{2,1,0:T(8,128)(2,1)S(1)}, bf16[4,160,256]{2,1,0:T(8,128)(2,1)S(1)}, u32[]{:S(2)}, u32[]{:S(2)}) collective-permute-start(bf16[4,160,256]{2,1,0:T(8,128)(2,1)S(1)} %pad_maximum_fusion.1.refs_4_), channel_id=1, source_target_pairs={{0,2},{1,3},{2,0},{3,1},{4,6},{5,7},{6,4},{7,5},{8,10},{9,11},{10,... | collective-permute-start | bytes 983048 | tf_op jit(solution)/shard_map/ppermute | solution.py:133
  37.4 12.7 %collective-permute-start.8 = (bf16[4,160,256]{2,1,0:T(8,128)(2,1)S(1)}, bf16[4,160,256]{2,1,0:T(8,128)(2,1)S(1)}, u32[]{:S(2)}, u32[]{:S(2)}) collective-permute-start(bf16[4,160,256]{2,1,0:T(8,128)(2,1)S(1)} %pad_maximum_fusion.refs_0_), channel_id=1, source_target_pairs={{0,4},{4,8},{8,12},{12,0},{1,5},{5,9},{9,13},{13,1},{2,6},{6,10},{... | collective-permute-start | bytes 983048 | tf_op jit(solution)/shard_map/ppermute | solution.py:132
  38.7 11.9 %collective-permute-start.9 = (bf16[4,160,256]{2,1,0:T(8,128)(2,1)S(1)}, bf16[4,160,256]{2,1,0:T(8,128)(2,1)}, u32[]{:S(2)}, u32[]{:S(2)}) collective-permute-start(bf16[4,160,256]{2,1,0:T(8,128)(2,1)S(1)} %pad_maximum_fusion.refs_0_), channel_id=1, source_target_pairs={{0,12},{4,0},{8,4},{12,8},{1,13},{5,1},{9,5},{13,9},{2,14},{6,2},{... | collective-permute-start | bytes 983048 | tf_op jit(solution)/shard_map/ppermute | solution.py:132
  42.2 8.8 %collective-permute-start.15 = (bf16[256,512]{1,0:T(8,128)(2,1)}, bf16[256,512]{1,0:T(8,128)(2,1)}, u32[]{:S(2)}, u32[]{:S(2)}) collective-permute-start(bf16[256,512]{1,0:T(8,128)(2,1)} %get-tuple-element.32), channel_id=1, source_target_pairs={{0,32},{32,0},{1,33},{33,1},{2,34},{34,2},{3,35},{35,3},{4,36},{36... | collective-permute-start | bytes 786440 | tf_op jit(solution)/shard_map/ppermute | solution.py:414
  49.5 1.9 %collective-permute-start.16 = (bf16[256,512]{1,0:T(8,128)(2,1)}, bf16[256,512]{1,0:T(8,128)(2,1)}, u32[]{:S(2)}, u32[]{:S(2)}) collective-permute-start(bf16[256,512]{1,0:T(8,128)(2,1)} %get-tuple-element.31), channel_id=1, source_target_pairs={{0,32},{32,0},{1,33},{33,1},{2,34},{34,2},{3,35},{35,3},{4,36},{36... | collective-permute-start | bytes 786440 | tf_op jit(solution)/shard_map/ppermute | solution.py:414
  49.5 2.2 %collective-permute-start.17 = (bf16[256,512]{1,0:T(8,128)(2,1)}, bf16[256,512]{1,0:T(8,128)(2,1)}, u32[]{:S(2)}, u32[]{:S(2)}) collective-permute-start(bf16[256,512]{1,0:T(8,128)(2,1)} %get-tuple-element.30), channel_id=1, source_target_pairs={{0,32},{32,0},{1,33},{33,1},{2,34},{34,2},{3,35},{35,3},{4,36},{36... | collective-permute-start | bytes 786440 | tf_op jit(solution)/shard_map/ppermute | solution.py:414
  50.0 2.1 %collective-permute-start.18 = (bf16[256,512]{1,0:T(8,128)(2,1)}, bf16[256,512]{1,0:T(8,128)(2,1)}, u32[]{:S(2)}, u32[]{:S(2)}) collective-permute-start(bf16[256,512]{1,0:T(8,128)(2,1)} %get-tuple-element.29), channel_id=1, source_target_pairs={{0,32},{32,0},{1,33},{33,1},{2,34},{34,2},{3,35},{35,3},{4,36},{36... | collective-permute-start | bytes 786440 | tf_op jit(solution)/shard_map/ppermute | solution.py:414
  50.5 4.9 %copy-start.1 = (bf16[256,8192]{1,0:T(8,128)(2,1)S(1)}, bf16[256,8192]{1,0:T(8,128)(2,1)}, u32[]{:S(2)}) copy-start(bf16[256,8192]{1,0:T(8,128)(2,1)} %refs_8_.1) | copy-start | bytes 12582916
  50.5 4.9 %copy-start.7 = (f32[256,128]{1,0:T(8,128)S(1)}, f32[256,128]{1,0:T(8,128)}, u32[]{:S(2)}) copy-start(f32[256,128]{1,0:T(8,128)} %copy-done.6) | copy-start | bytes 393220
  55.2 7.7 %collective-permute-start.19 = (bf16[384,256]{1,0:T(8,128)(2,1)S(1)}, bf16[384,256]{1,0:T(8,128)(2,1)S(1)}, u32[]{:S(2)}, u32[]{:S(2)}) collective-permute-start(bf16[384,256]{1,0:T(8,128)(2,1)S(1)} %theirs.1), channel_id=1, source_target_pairs={{0,16},{16,0},{1,17},{17,1},{2,18},{18,2},{3,19},{19,3},{4,20},{20... | collective-permute-start | bytes 589832 | tf_op jit(solution)/shard_map/ppermute | solution.py:429
  58.2 0.7 copy-start.3
  64.1 25.4 %all-to-all-start = ((bf16[128,32,128]{2,1,0:T(8,128)(2,1)}), bf16[128,32,128]{2,1,0:T(8,128)(2,1)S(1)}, u32[]{:S(2)}, u32[]{:S(2)}) async-start(bf16[128,32,128]{2,1,0:T(8,128)(2,1)} %bitcast.16), calls=%async_computation | async-start | bytes 2097152 | tf_op jit(solution)/shard_map/all_to_all | solution.py:435
  71.1 1.0 copy-start.4
  72.4 15.4 %collective-permute-start.21 = (bf16[2,128,256]{2,1,0:T(8,128)(2,1)S(1)}, bf16[2,128,256]{2,1,0:T(8,128)(2,1)S(1)}, u32[]{:S(2)}, u32[]{:S(2)}) collective-permute-start(bf16[2,128,256]{2,1,0:T(8,128)(2,1)S(1)} %q_finish.1.refs_0_), channel_id=1, source_target_pairs={{0,64},{64,0},{1,65},{65,1},{2,66},{66,2},{3,67},{67,3},{4,68},{68... | collective-permute-start | bytes 393224 | tf_op jit(solution)/shard_map/ppermute | solution.py:388
  74.0 14.4 %collective-permute-start.20 = (bf16[2,128,256]{2,1,0:T(8,128)(2,1)S(1)}, bf16[2,128,256]{2,1,0:T(8,128)(2,1)S(1)}, u32[]{:S(2)}, u32[]{:S(2)}) collective-permute-start(bf16[2,128,256]{2,1,0:T(8,128)(2,1)S(1)} %q_finish.1.refs_0_), channel_id=1, source_target_pairs={{0,32},{32,0},{1,33},{33,1},{2,34},{34,2},{3,35},{35,3},{4,36},{36... | collective-permute-start | bytes 393224 | tf_op jit(solution)/shard_map/ppermute | solution.py:386
  87.8 1.6 %collective-permute-start.22 = (bf16[2,128,256]{2,1,0:T(8,128)(2,1)S(1)}, bf16[2,128,256]{2,1,0:T(8,128)(2,1)S(1)}, u32[]{:S(2)}, u32[]{:S(2)}) collective-permute-start(bf16[2,128,256]{2,1,0:T(8,128)(2,1)S(1)} %collective-permute-done.21.refs_2_), channel_id=1, source_target_pairs={{0,32},{32,0},{1,33},{33,1},{2,34},{34,2},{3,35},{35,3},{4,36},{36... | collective-permute-start | bytes 393224 | tf_op jit(solution)/shard_map/ppermute | solution.py:386
  95.7 2.3 %collective-permute-start.23 = (bf16[576,256]{1,0:T(8,128)(2,1)S(1)}, bf16[576,256]{1,0:T(8,128)(2,1)S(1)}, u32[]{:S(2)}, u32[]{:S(2)}) collective-permute-start(bf16[576,256]{1,0:T(8,128)(2,1)S(1)} %get-tuple-element.28), channel_id=1, source_target_pairs={{0,32},{32,0},{1,33},{33,1},{2,34},{34,2},{3,35},{35,3},{4,36},{36... | collective-permute-start | bytes 884744 | tf_op jit(solution)/shard_map/ppermute | solution.py:386
  98.1 8.3 %collective-permute-start.24 = (bf16[576,256]{1,0:T(8,128)(2,1)S(1)}, bf16[576,256]{1,0:T(8,128)(2,1)S(1)}, u32[]{:S(2)}, u32[]{:S(2)}) collective-permute-start(bf16[576,256]{1,0:T(8,128)(2,1)S(1)} %merge.1.a_ref), channel_id=1, source_target_pairs={{0,64},{64,0},{1,65},{65,1},{2,66},{66,2},{3,67},{67,3},{4,68},{68... | collective-permute-start | bytes 884744 | tf_op jit(solution)/shard_map/ppermute | solution.py:388
  106.7 2.4 %collective-permute-start.25 = (bf16[256,512]{1,0:T(8,128)(2,1)S(1)}, bf16[256,512]{1,0:T(8,128)(2,1)S(1)}, u32[]{:S(2)}, u32[]{:S(2)}) collective-permute-start(bf16[256,512]{1,0:T(8,128)(2,1)S(1)} %last.1.mine_ref), channel_id=1, source_target_pairs={{0,32},{32,0},{1,33},{33,1},{2,34},{34,2},{3,35},{35,3},{4,36},{36... | collective-permute-start | bytes 786440 | tf_op jit(solution)/shard_map/ppermute | solution.py:386

commit v6 on v4

--- a/solution.py
+++ b/solution.py
@@ -237,7 +237,7 @@
 CHUNK = 512
 KEYS = 2048
 EXP_SCALE = math.log2(math.e) / math.sqrt(HEAD)
-STAT = 144
+STATS, ROWS = 512, 528
 
 
 def attend_kernel(idx, *refs):
@@ -281,6 +281,7 @@
     tops, q = None, queries(0)
     for j in range(chunks):
         tops = score(0, j, q, tops)
+    logs = ([], [])
     for h in range(8):
         top = jnp.max(tops, axis=0, keepdims=True)
         tops, acc, total = None, None, None
@@ -297,13 +298,15 @@
             acc = mix if acc is None else acc + mix
             total = part if total is None else total + part
         total = jnp.sum(total, axis=0, keepdims=True)
-        o_ref, at = o_refs[h // 2 % 2], (h // 4 * 2 + h % 2) * STAT
-        o_ref[at:at + 128] = (acc / total).astype(BF16)
-        put_log(o_ref, at, top * EXP_SCALE + jnp.log2(total))
+        to, at = h // 2 % 2, (h // 4 * 2 + h % 2) * 128
+        o_refs[to][at:at + 128] = (acc / total).astype(BF16)
+        logs[to].append(top * EXP_SCALE + jnp.log2(total))
+    for o_ref, log in zip(o_refs, logs):
+        put_logs(o_ref, log)
 
 
 def attend(idx, qs, kv):
-    shape = jax.ShapeDtypeStruct((4 * STAT, 256), BF16)
+    shape = jax.ShapeDtypeStruct((ROWS, 256), BF16)
     return pl.pallas_call(
         attend_kernel,
         in_specs=[sspec()] + [vspec()] * 5,
@@ -319,17 +322,20 @@
     )(idx, *qs, kv)
 
 
-def log_sum(ref, at):
-    t = ref[at + 128:at + STAT].astype(F32)
-    return t[0:1] + t[1:2] + t[2:3]
-
-
-def put_log(ref, at, log):
-    w = lax.broadcasted_iota(jnp.int32, (16, 256), 0)
-    hi = log.astype(BF16).astype(F32)
-    mid = (log - hi).astype(BF16).astype(F32)
-    terms = jnp.where(w == 0, hi, jnp.where(w == 1, mid, jnp.where(w == 2, log - hi - mid, 0.0)))
-    ref[at + 128:at + STAT] = terms.astype(BF16)
+def log_sum(ref, h):
+    t = ref[STATS:ROWS].astype(F32)
+    return t[3 * h:3 * h + 1] + t[3 * h + 1:3 * h + 2] + t[3 * h + 2:3 * h + 3]
+
+
+def put_logs(ref, logs):
+    w = lax.broadcasted_iota(jnp.int32, (ROWS - STATS, 256), 0)
+    terms = jnp.zeros(w.shape, F32)
+    for h, log in enumerate(logs):
+        hi = log.astype(BF16).astype(F32)
+        mid = (log - hi).astype(BF16).astype(F32)
+        for k, term in enumerate((hi, mid, log - hi - mid)):
+            terms = jnp.where(w == 3 * h + k, term, terms)
+    ref[STATS:ROWS] = terms.astype(BF16)
 
 
 def merged(a_ref, b_ref, i, j):
@@ -337,22 +343,23 @@
     top = jnp.maximum(a, b)
     fa, fb = jnp.exp2(a - top), jnp.exp2(b - top)
     total = fa + fb
-    mixed = a_ref[i:i + 128].astype(F32) * (fa / total)
-    mixed = mixed + b_ref[j:j + 128].astype(F32) * (fb / total)
+    mixed = a_ref[i * 128:i * 128 + 128].astype(F32) * (fa / total)
+    mixed = mixed + b_ref[j * 128:j * 128 + 128].astype(F32) * (fb / total)
     return mixed, top + jnp.log2(total)
 
 
 def merge_kernel(a_ref, b_ref, o_ref):
+    logs = []
     for h in range(4):
-        at = h * STAT
-        mixed, log = merged(a_ref, b_ref, at, at)
-        o_ref[at:at + 128] = mixed.astype(BF16)
-        put_log(o_ref, at, log)
+        mixed, log = merged(a_ref, b_ref, h, h)
+        o_ref[h * 128:h * 128 + 128] = mixed.astype(BF16)
+        logs.append(log)
+    put_logs(o_ref, logs)
 
 
 def last_kernel(a_ref, b_ref, out_ref):
     for h in range(4):
-        mixed, _ = merged(a_ref, b_ref, h * STAT, (h + 2) % 4 * STAT)
+        mixed, _ = merged(a_ref, b_ref, h, (h + 2) % 4)
         out_ref[:, h * 128:(h + 1) * 128] = mixed.T.astype(BF16)
 
 
@@ -437,7 +444,7 @@
     qs = [q0, q1, q2, to_rep(q2, 1)]
 
     kept, sent = attend(idx, qs, pair_all.reshape(32, 4, 32, 128))
-    (part,) = small(merge_kernel, (kept, to_rep(sent, 1)), [(4 * STAT, 256)], "merge")
+    (part,) = small(merge_kernel, (kept, to_rep(sent, 1)), [(ROWS, 256)], "merge")
     (mine,) = small(last_kernel, (part, to_rep(part, 2)), [(256, 512)], "last")
     (out,) = small(place_kernel, (idx, mine, to_rep(mine, 1)), [(256, 1024)], "place", 1)
     return out

time: 111 us -> 110 us (level)
  no operation moved by 1% of the time
where the time goes in v6:
time: 110 us
  starting transfers between devices  42.6 us (39%)
  waiting for transfers between devices  40 us (36%)
  Pallas kernels  18.1 us (16%)
  local copies, waits for them, and re-layouts  7.84 us (7%)
    ppermute x2, waiting for transfers between devices, to_rep(): return lax.ppermute(x, 'zl', SWAP)  20.4 us
    ppermute x4, starting transfers between devices, local(): lax.ppermute(got[:, i * width:(i + 1) * width], 'c', SWAP)  8.33 us
    all_to_all x1, starting transfers between devices, local(): lax.all_to_all(pair.reshape(128, 32, 128), ('zh', 'x', 'y', 'zl', 'c'), 0...  6.78 us
    unnamed x18, local copies, waits for them, and re-layouts  6.67 us
    pallas_call x1, Pallas kernels, attend(): pl.pallas_call(attend_kernel, in_specs=[sspec()] + [vspec()] * 5, out_spe...  6.24 us
    pallas_call x2, Pallas kernels, project(): pl.pallas_call(kernel, scratch_shapes=scratch, in_specs=[sspec()] + [vspe...  5.76 us
    ppermute x3, starting transfers between devices, gather_plane(): lowers = [lower] + [lax.ppermute(lower, 'x', ring(d)) for d in (1, 3, 2)]  4.31 us
    ppermute x3, starting transfers between devices, gather_plane(): lax.ppermute(upper, 'x', ring(d))  4.28 us
  transfers between devices with their start and end apart: 27, of which 17 were waited for; matrix products, arithmetic and copies ran while one was open for 2% of the time, Pallas kernels for 4%

profile of v6, /device:TPU:1, one launch (start us, length us, event | category | flops | bytes accessed | tf_op | source)
XLA Modules:
  0.0 109.6 jit_solution(8697295622109971765)
XLA Ops:
  0.0 0.1 stack.57.idx
  0.1 1.2 %copy-done.2 = f32[1,256,1024]{2,1,0:T(8,128)S(1)} copy-done((f32[1,256,1024]{2,1,0:T(8,128)S(1)}, f32[1,256,1024]{2,1,0:T(8,128)}, u32[]{:S(2)}) %copy-start.2) | copy-done | bytes 1048600
  1.3 0.9 copy-done.5
  2.3 0.7 copy-done.8
  2.9 1.0 prepare.1
  3.9 1.5 %collective-permute-start = (f32[2,320,256]{2,1,0:T(8,128)S(1)}, f32[2,320,256]{2,1,0:T(8,128)S(1)}, u32[]{:S(2)}, u32[]{:S(2)}) collective-permute-start(f32[2,320,256]{2,1,0:T(8,128)S(1)} %get-tuple-element.18), channel_id=1, source_target_pairs={{0,32},{32,0},{1,33},{33,1},{2,34},{34,2},{3,35},{35,3},{4,36},{36... | collective-permute-start | bytes 1966088 | tf_op jit(solution)/shard_map/ppermute | solution.py:398
  5.4 1.7 %collective-permute-done = f32[2,320,256]{2,1,0:T(8,128)S(1)} collective-permute-done((f32[2,320,256]{2,1,0:T(8,128)S(1)}, f32[2,320,256]{2,1,0:T(8,128)S(1)}, u32[]{:S(2)}, u32[]{:S(2)}) %collective-permute-start) | collective-permute-done | bytes 655392 | tf_op jit(solution)/shard_map/ppermute | solution.py:398
  7.1 0.1 add.35
  7.3 1.8 %collective-permute-start.1 = (bf16[320,256]{1,0:T(8,128)(2,1)S(1)}, bf16[320,256]{1,0:T(8,128)(2,1)S(1)}, u32[]{:S(2)}, u32[]{:S(2)}) collective-permute-start(bf16[320,256]{1,0:T(8,128)(2,1)S(1)} %fusion.1), channel_id=1, source_target_pairs={{0,64},{64,0},{1,65},{65,1},{2,66},{66,2},{3,67},{67,3},{4,68},{68... | collective-permute-start | bytes 491528 | tf_op jit(solution)/shard_map/ppermute | solution.py:401
  9.1 2.2 %copy-done = bf16[256,8192]{1,0:T(8,128)(2,1)S(1)} copy-done((bf16[256,8192]{1,0:T(8,128)(2,1)S(1)}, bf16[256,8192]{1,0:T(8,128)(2,1)}, u32[]{:S(2)}) %copy-start) | copy-done | bytes 4194328
  11.3 1.8 %normalise.1 = (f32[256,128]{1,0:T(8,128)S(1)}, bf16[256,2048]{1,0:T(8,128)(2,1)S(1)}) custom-call(s32[6]{0:T(128)S(1)} %stack.57.idx, bf16[256,8192]{1,0:T(8,128)(2,1)S(1)} %copy-done), custom_call_target="tpu_custom_call" | custom-call | flops 8388608 | bytes 6291456 | tf_op jit(solution)/shard_map/normalise/pallas_call | solution.py:64
  13.0 0.3 collective-permute-done.1
  13.3 3.1 %collective-permute-start.14 = (bf16[256,2048]{1,0:T(8,128)(2,1)S(1)}, bf16[256,2048]{1,0:T(8,128)(2,1)S(1)}, u32[]{:S(2)}, u32[]{:S(2)}) collective-permute-start(bf16[256,2048]{1,0:T(8,128)(2,1)S(1)} %get-tuple-element.25), channel_id=1, source_target_pairs={{0,16},{16,0},{1,17},{17,1},{2,18},{18,2},{3,19},{19,3},{4,20},{20... | collective-permute-start | bytes 3145736 | tf_op jit(solution)/shard_map/ppermute | solution.py:417
  16.4 0.1 fusion
  16.5 1.3 %collective-permute-start.5 = (bf16[160,256]{1,0:T(8,128)(2,1)S(1)}, bf16[160,256]{1,0:T(8,128)(2,1)S(1)}, u32[]{:S(2)}, u32[]{:S(2)}) collective-permute-start(bf16[160,256]{1,0:T(8,128)(2,1)S(1)} %get-tuple-element.35), channel_id=1, source_target_pairs={{0,4},{4,8},{8,12},{12,0},{1,5},{5,9},{9,13},{13,1},{2,6},{6,10},{... | collective-permute-start | bytes 245768 | tf_op jit(solution)/shard_map/ppermute | solution.py:130
  17.8 1.5 %collective-permute-start.6 = (bf16[160,256]{1,0:T(8,128)(2,1)S(1)}, bf16[160,256]{1,0:T(8,128)(2,1)S(1)}, u32[]{:S(2)}, u32[]{:S(2)}) collective-permute-start(bf16[160,256]{1,0:T(8,128)(2,1)S(1)} %get-tuple-element.35), channel_id=1, source_target_pairs={{0,12},{4,0},{8,4},{12,8},{1,13},{5,1},{9,5},{13,9},{2,14},{6,2},{... | collective-permute-start | bytes 245768 | tf_op jit(solution)/shard_map/ppermute | solution.py:130
  19.3 1.5 %collective-permute-start.7 = (bf16[160,256]{1,0:T(8,128)(2,1)S(1)}, bf16[160,256]{1,0:T(8,128)(2,1)S(1)}, u32[]{:S(2)}, u32[]{:S(2)}) collective-permute-start(bf16[160,256]{1,0:T(8,128)(2,1)S(1)} %get-tuple-element.35), channel_id=1, source_target_pairs={{0,8},{4,12},{8,0},{12,4},{1,9},{5,13},{9,1},{13,5},{2,10},{6,14},... | collective-permute-start | bytes 245768 | tf_op jit(solution)/shard_map/ppermute | solution.py:130
  20.8 2.7 %collective-permute-start.3 = (bf16[160,256]{1,0:T(8,128)(2,1)S(1)}, bf16[160,256]{1,0:T(8,128)(2,1)S(1)}, u32[]{:S(2)}, u32[]{:S(2)}) collective-permute-start(bf16[160,256]{1,0:T(8,128)(2,1)S(1)} %get-tuple-element.36), channel_id=1, source_target_pairs={{0,3},{1,0},{2,1},{3,2},{4,7},{5,4},{6,5},{7,6},{8,11},{9,8},{10,9... | collective-permute-start | bytes 245768 | tf_op jit(solution)/shard_map/ppermute | solution.py:129
  23.5 0.8 collective-permute-start.4
  24.3 0.4 collective-permute-start.2
  24.7 0.5 collective-permute-done.7
  25.3 3.4 %collective-permute-done.4 = bf16[160,256]{1,0:T(8,128)(2,1)S(1)} collective-permute-done((bf16[160,256]{1,0:T(8,128)(2,1)S(1)}, bf16[160,256]{1,0:T(8,128)(2,1)S(1)}, u32[]{:S(2)}, u32[]{:S(2)}) %collective-permute-start.4) | collective-permute-done | bytes 81952 | tf_op jit(solution)/shard_map/ppermute | solution.py:129
  28.6 0.9 collective-permute-done.2
  29.6 1.5 %collective-permute-start.10 = (bf16[4,160,256]{2,1,0:T(8,128)(2,1)S(1)}, bf16[4,160,256]{2,1,0:T(8,128)(2,1)S(1)}, u32[]{:S(2)}, u32[]{:S(2)}) collective-permute-start(bf16[4,160,256]{2,1,0:T(8,128)(2,1)S(1)} %pad_maximum_fusion.refs_0_), channel_id=1, source_target_pairs={{0,8},{4,12},{8,0},{12,4},{1,9},{5,13},{9,1},{13,5},{2,10},{6,14},... | collective-permute-start | bytes 983048 | tf_op jit(solution)/shard_map/ppermute | solution.py:132
  31.1 2.7 %collective-permute-start.12 = (bf16[4,160,256]{2,1,0:T(8,128)(2,1)S(1)}, bf16[4,160,256]{2,1,0:T(8,128)(2,1)S(1)}, u32[]{:S(2)}, u32[]{:S(2)}) collective-permute-start(bf16[4,160,256]{2,1,0:T(8,128)(2,1)S(1)} %pad_maximum_fusion.1.refs_4_), channel_id=1, source_target_pairs={{0,3},{1,0},{2,1},{3,2},{4,7},{5,4},{6,5},{7,6},{8,11},{9,8},{10,9... | collective-permute-start | bytes 983048 | tf_op jit(solution)/shard_map/ppermute | solution.py:133
  33.8 3.6 %collective-permute-done.10.refs_3_ = bf16[4,160,256]{2,1,0:T(8,128)(2,1)S(1)} collective-permute-done((bf16[4,160,256]{2,1,0:T(8,128)(2,1)S(1)}, bf16[4,160,256]{2,1,0:T(8,128)(2,1)S(1)}, u32[]{:S(2)}, u32[]{:S(2)}) %collective-permute-start.10) | collective-permute-done | bytes 327712 | tf_op jit(solution)/shard_map/ppermute | solution.py:132
  37.4 0.3 collective-permute-start.8
  37.7 1.0 collective-permute-done.14.refs_8_
  38.7 2.5 %collective-permute-start.9 = (bf16[4,160,256]{2,1,0:T(8,128)(2,1)S(1)}, bf16[4,160,256]{2,1,0:T(8,128)(2,1)}, u32[]{:S(2)}, u32[]{:S(2)}) collective-permute-start(bf16[4,160,256]{2,1,0:T(8,128)(2,1)S(1)} %pad_maximum_fusion.refs_0_), channel_id=1, source_target_pairs={{0,12},{4,0},{8,4},{12,8},{1,13},{5,1},{9,5},{13,9},{2,14},{6,2},{... | collective-permute-start | bytes 983048 | tf_op jit(solution)/shard_map/ppermute | solution.py:132
  41.2 1.0 fusion.2
  42.2 7.3 %collective-permute-start.15 = (bf16[256,512]{1,0:T(8,128)(2,1)}, bf16[256,512]{1,0:T(8,128)(2,1)}, u32[]{:S(2)}, u32[]{:S(2)}) collective-permute-start(bf16[256,512]{1,0:T(8,128)(2,1)} %get-tuple-element.32), channel_id=1, source_target_pairs={{0,32},{32,0},{1,33},{33,1},{2,34},{34,2},{3,35},{35,3},{4,36},{36... | collective-permute-start | bytes 786440 | tf_op jit(solution)/shard_map/ppermute | solution.py:419
  49.5 0.5 collective-permute-start.17
  50.0 0.5 collective-permute-start.18
  50.5 0.1 dynamic_slice.3
  50.6 0.4 collective-permute-done.15.refs_9_
  51.0 0.4 collective-permute-done.16.refs_10_
  51.4 0.4 collective-permute-done.17.refs_11_
  51.8 0.4 collective-permute-done.18.refs_12_
  52.1 3.1 %theirs.1 = bf16[320,256]{1,0:T(8,128)(2,1)S(1)} custom-call(s32[6]{0:T(128)S(1)} %stack.57.idx, bf16[4,160,256]{2,1,0:T(8,128)(2,1)S(1)} %pad_maximum_fusion.refs_0_, bf16[4,160,256]{2,1,0:T(8,128)(2,1)S(1)} %collective-permute-done.8.refs_1_, bf16[4,160,256]{2,1,0:T(8,128)(2,1)} %collective-permute-done.9.refs_2_, ...), custom_call_target="tpu_custom_call" | custom-call | flops 671088640 | bytes 5242880 | tf_op jit(solution)/shard_map/theirs/pallas_call | solution.py:190
  55.2 0.1 collective-permute-start.19
  55.3 0.1 multiply_sine_fusion.1
  55.5 2.7 %own.1 = (f32[256,256]{1,0:T(8,128)S(1)}, f32[64,256]{1,0:T(8,128)S(1)}) custom-call(s32[6]{0:T(128)S(1)} %stack.57.idx, bf16[4,160,256]{2,1,0:T(8,128)(2,1)S(1)} %pad_maximum_fusion.refs_0_, bf16[4,160,256]{2,1,0:T(8,128)(2,1)S(1)} %collective-permute-done.8.refs_1_, bf16[4,160,256]{2,1,0:T(8,128)(2,1)} %collective-permute-done.9.refs_2_, ...), custom_call_target="tpu_custom_call" | custom-call | flops 671088640 | bytes 5242880 | tf_op jit(solution)/shard_map/own/pallas_call | solution.py:190
  58.2 0.7 copy-done.3
  58.9 3.3 %collective-permute-done.19.got_ref = bf16[320,256]{1,0:T(8,128)(2,1)S(1)} collective-permute-done((bf16[320,256]{1,0:T(8,128)(2,1)S(1)}, bf16[320,256]{1,0:T(8,128)(2,1)S(1)}, u32[]{:S(2)}, u32[]{:S(2)}) %collective-permute-start.19) | collective-permute-done | bytes 163872 | tf_op jit(solution)/shard_map/ppermute | solution.py:434
  62.2 1.2 %pair_finish.1 = bf16[32,4,32,128]{3,2,1,0:T(8,128)(2,1)} custom-call(f32[64,256]{1,0:T(8,128)S(1)} %get-tuple-element.26.own_ref, bf16[320,256]{1,0:T(8,128)(2,1)S(1)} %collective-permute-done.19.got_ref, f32[16,256]{1,0:T(8,128)S(1)} %get-tuple-element.38.cos_ref, f32[16,256]{1,0:T(8,128)S(1)} %get-tuple-element.37.sin_ref), custom_call_target="tpu_custom_call" | custom-call | flops 262144 | bytes 1048576 | tf_op jit(solution)/shard_map/pair_finish/pallas_call | solution.py:226
  63.4 6.8 %all-to-all-start = ((bf16[128,32,128]{2,1,0:T(8,128)(2,1)}), bf16[128,32,128]{2,1,0:T(8,128)(2,1)S(1)}, u32[]{:S(2)}, u32[]{:S(2)}) async-start(bf16[128,32,128]{2,1,0:T(8,128)(2,1)} %bitcast.16), calls=%async_computation | async-start | bytes 2097152 | tf_op jit(solution)/shard_map/all_to_all | solution.py:440
  70.2 0.5 multiply_sine_fusion
  70.7 0.9 copy-done.4
  71.7 0.4 q_finish.1.refs_0_
  72.1 1.6 %collective-permute-start.21 = (bf16[2,128,256]{2,1,0:T(8,128)(2,1)S(1)}, bf16[2,128,256]{2,1,0:T(8,128)(2,1)S(1)}, u32[]{:S(2)}, u32[]{:S(2)}) collective-permute-start(bf16[2,128,256]{2,1,0:T(8,128)(2,1)S(1)} %q_finish.1.refs_0_), channel_id=1, source_target_pairs={{0,64},{64,0},{1,65},{65,1},{2,66},{66,2},{3,67},{67,3},{4,68},{68... | collective-permute-start | bytes 393224 | tf_op jit(solution)/shard_map/ppermute | solution.py:393
  73.7 0.6 collective-permute-start.20
  74.3 13.2 %collective-permute-done.21.refs_2_ = bf16[2,128,256]{2,1,0:T(8,128)(2,1)S(1)} collective-permute-done((bf16[2,128,256]{2,1,0:T(8,128)(2,1)S(1)}, bf16[2,128,256]{2,1,0:T(8,128)(2,1)S(1)}, u32[]{:S(2)}, u32[]{:S(2)}) %collective-permute-start.21) | collective-permute-done | bytes 131104 | tf_op jit(solution)/shard_map/ppermute | solution.py:393
  87.5 0.6 collective-permute-start.22
  88.1 1.0 collective-permute-done.22.refs_3_
  89.1 6.2 %attend.1 = (bf16[528,256]{1,0:T(8,128)(2,1)S(1)}, bf16[528,256]{1,0:T(8,128)(2,1)S(1)}) custom-call(s32[6]{0:T(128)S(1)} %stack.57.idx, bf16[2,128,256]{2,1,0:T(8,128)(2,1)S(1)} %q_finish.1.refs_0_, bf16[2,128,256]{2,1,0:T(8,128)(2,1)S(1)} %collective-permute-done.20.refs_1_, bf16[2,128,256]{2,1,0:T(8,128)(2,1)S(1)} %collective-permute-done.21.refs_2_, ...), custom_call_target="tpu_custom_call" | custom-call | flops 2147483648 | bytes 4194304 | tf_op jit(solution)/shard_map/attend/pallas_call | solution.py:310
  95.4 1.1 collective-permute-start.23
  96.4 1.2 %collective-permute-done.23.b_ref = bf16[528,256]{1,0:T(8,128)(2,1)S(1)} collective-permute-done((bf16[528,256]{1,0:T(8,128)(2,1)S(1)}, bf16[528,256]{1,0:T(8,128)(2,1)S(1)}, u32[]{:S(2)}, u32[]{:S(2)}) %collective-permute-start.23) | collective-permute-done | bytes 270368 | tf_op jit(solution)/shard_map/ppermute | solution.py:391
  97.6 0.2 merge.1.a_ref
  97.8 0.6 collective-permute-start.24
  98.3 7.2 %collective-permute-done.24.b_ref = bf16[528,256]{1,0:T(8,128)(2,1)S(1)} collective-permute-done((bf16[528,256]{1,0:T(8,128)(2,1)S(1)}, bf16[528,256]{1,0:T(8,128)(2,1)S(1)}, u32[]{:S(2)}, u32[]{:S(2)}) %collective-permute-start.24) | collective-permute-done | bytes 270368 | tf_op jit(solution)/shard_map/ppermute | solution.py:393
  105.6 0.2 last.1.mine_ref
  105.8 1.3 %collective-permute-start.25 = (bf16[256,512]{1,0:T(8,128)(2,1)S(1)}, bf16[256,512]{1,0:T(8,128)(2,1)S(1)}, u32[]{:S(2)}, u32[]{:S(2)}) collective-permute-start(bf16[256,512]{1,0:T(8,128)(2,1)S(1)} %last.1.mine_ref), channel_id=1, source_target_pairs={{0,32},{32,0},{1,33},{33,1},{2,34},{34,2},{3,35},{35,3},{4,36},{36... | collective-permute-start | bytes 786440 | tf_op jit(solution)/shard_map/ppermute | solution.py:391
  107.1 1.2 %collective-permute-done.25.other_ref = bf16[256,512]{1,0:T(8,128)(2,1)S(1)} collective-permute-done((bf16[256,512]{1,0:T(8,128)(2,1)S(1)}, bf16[256,512]{1,0:T(8,128)(2,1)S(1)}, u32[]{:S(2)}, u32[]{:S(2)}) %collective-permute-start.25) | collective-permute-done | bytes 262176 | tf_op jit(solution)/shard_map/ppermute | solution.py:391
  108.2 1.4 %place.1 = bf16[256,1024]{1,0:T(8,128)(2,1)} custom-call(s32[6]{0:T(128)S(1)} %stack.57.idx, bf16[256,512]{1,0:T(8,128)(2,1)S(1)} %last.1.mine_ref, bf16[256,512]{1,0:T(8,128)(2,1)S(1)} %collective-permute-done.25.other_ref), custom_call_target="tpu_custom_call" | custom-call | flops 524288 | bytes 1048576 | tf_op jit(solution)/shard_map/place/pallas_call | solution.py:375
  (31 shorter events, 0.2 us)
Async XLA Ops:
  0.1 1.2 %copy-start.2 = (f32[1,256,1024]{2,1,0:T(8,128)S(1)}, f32[1,256,1024]{2,1,0:T(8,128)}, u32[]{:S(2)}) copy-start(f32[1,256,1024]{2,1,0:T(8,128)} %q_ref.1) | copy-start | bytes 3145732
  1.3 0.9 copy-start.5
  2.3 0.7 copy-start.8
  3.9 3.2 %collective-permute-start = (f32[2,320,256]{2,1,0:T(8,128)S(1)}, f32[2,320,256]{2,1,0:T(8,128)S(1)}, u32[]{:S(2)}, u32[]{:S(2)}) collective-permute-start(f32[2,320,256]{2,1,0:T(8,128)S(1)} %get-tuple-element.18), channel_id=1, source_target_pairs={{0,32},{32,0},{1,33},{33,1},{2,34},{34,2},{3,35},{35,3},{4,36},{36... | collective-permute-start | bytes 1966088 | tf_op jit(solution)/shard_map/ppermute | solution.py:398
  7.3 6.0 %collective-permute-start.1 = (bf16[320,256]{1,0:T(8,128)(2,1)S(1)}, bf16[320,256]{1,0:T(8,128)(2,1)S(1)}, u32[]{:S(2)}, u32[]{:S(2)}) collective-permute-start(bf16[320,256]{1,0:T(8,128)(2,1)S(1)} %fusion.1), channel_id=1, source_target_pairs={{0,64},{64,0},{1,65},{65,1},{2,66},{66,2},{3,67},{67,3},{4,68},{68... | collective-permute-start | bytes 491528 | tf_op jit(solution)/shard_map/ppermute | solution.py:401
  9.1 2.2 %copy-start = (bf16[256,8192]{1,0:T(8,128)(2,1)S(1)}, bf16[256,8192]{1,0:T(8,128)(2,1)}, u32[]{:S(2)}) copy-start(bf16[256,8192]{1,0:T(8,128)(2,1)} %refs_8_.1) | copy-start | bytes 12582916
  13.0 37.0 %copy-start.6 = (f32[256,128]{1,0:T(8,128)}, f32[256,128]{1,0:T(8,128)S(1)}, u32[]{:S(2)}) copy-start(f32[256,128]{1,0:T(8,128)S(1)} %get-tuple-element.23.refs_9_) | copy-start | bytes 393220
  13.3 25.4 %collective-permute-start.14 = (bf16[256,2048]{1,0:T(8,128)(2,1)S(1)}, bf16[256,2048]{1,0:T(8,128)(2,1)S(1)}, u32[]{:S(2)}, u32[]{:S(2)}) collective-permute-start(bf16[256,2048]{1,0:T(8,128)(2,1)S(1)} %get-tuple-element.25), channel_id=1, source_target_pairs={{0,16},{16,0},{1,17},{17,1},{2,18},{18,2},{3,19},{19,3},{4,20},{20... | collective-permute-start | bytes 3145736 | tf_op jit(solution)/shard_map/ppermute | solution.py:417
  16.5 7.0 %collective-permute-start.5 = (bf16[160,256]{1,0:T(8,128)(2,1)S(1)}, bf16[160,256]{1,0:T(8,128)(2,1)S(1)}, u32[]{:S(2)}, u32[]{:S(2)}) collective-permute-start(bf16[160,256]{1,0:T(8,128)(2,1)S(1)} %get-tuple-element.35), channel_id=1, source_target_pairs={{0,4},{4,8},{8,12},{12,0},{1,5},{5,9},{9,13},{13,1},{2,6},{6,10},{... | collective-permute-start | bytes 245768 | tf_op jit(solution)/shard_map/ppermute | solution.py:130
  17.8 6.5 %collective-permute-start.6 = (bf16[160,256]{1,0:T(8,128)(2,1)S(1)}, bf16[160,256]{1,0:T(8,128)(2,1)S(1)}, u32[]{:S(2)}, u32[]{:S(2)}) collective-permute-start(bf16[160,256]{1,0:T(8,128)(2,1)S(1)} %get-tuple-element.35), channel_id=1, source_target_pairs={{0,12},{4,0},{8,4},{12,8},{1,13},{5,1},{9,5},{13,9},{2,14},{6,2},{... | collective-permute-start | bytes 245768 | tf_op jit(solution)/shard_map/ppermute | solution.py:130
  19.3 5.9 %collective-permute-start.7 = (bf16[160,256]{1,0:T(8,128)(2,1)S(1)}, bf16[160,256]{1,0:T(8,128)(2,1)S(1)}, u32[]{:S(2)}, u32[]{:S(2)}) collective-permute-start(bf16[160,256]{1,0:T(8,128)(2,1)S(1)} %get-tuple-element.35), channel_id=1, source_target_pairs={{0,8},{4,12},{8,0},{12,4},{1,9},{5,13},{9,1},{13,5},{2,10},{6,14},... | collective-permute-start | bytes 245768 | tf_op jit(solution)/shard_map/ppermute | solution.py:130
  20.8 4.4 %collective-permute-start.3 = (bf16[160,256]{1,0:T(8,128)(2,1)S(1)}, bf16[160,256]{1,0:T(8,128)(2,1)S(1)}, u32[]{:S(2)}, u32[]{:S(2)}) collective-permute-start(bf16[160,256]{1,0:T(8,128)(2,1)S(1)} %get-tuple-element.36), channel_id=1, source_target_pairs={{0,3},{1,0},{2,1},{3,2},{4,7},{5,4},{6,5},{7,6},{8,11},{9,8},{10,9... | collective-permute-start | bytes 245768 | tf_op jit(solution)/shard_map/ppermute | solution.py:129
  23.5 5.1 %collective-permute-start.4 = (bf16[160,256]{1,0:T(8,128)(2,1)S(1)}, bf16[160,256]{1,0:T(8,128)(2,1)S(1)}, u32[]{:S(2)}, u32[]{:S(2)}) collective-permute-start(bf16[160,256]{1,0:T(8,128)(2,1)S(1)} %get-tuple-element.36), channel_id=1, source_target_pairs={{0,2},{1,3},{2,0},{3,1},{4,6},{5,7},{6,4},{7,5},{8,10},{9,11},{10,... | collective-permute-start | bytes 245768 | tf_op jit(solution)/shard_map/ppermute | solution.py:129
  24.3 5.2 %collective-permute-start.2 = (bf16[160,256]{1,0:T(8,128)(2,1)S(1)}, bf16[160,256]{1,0:T(8,128)(2,1)S(1)}, u32[]{:S(2)}, u32[]{:S(2)}) collective-permute-start(bf16[160,256]{1,0:T(8,128)(2,1)S(1)} %get-tuple-element.36), channel_id=1, source_target_pairs={{0,1},{1,2},{2,3},{3,0},{4,5},{5,6},{6,7},{7,4},{8,9},{9,10},{10,1... | collective-permute-start | bytes 245768 | tf_op jit(solution)/shard_map/ppermute | solution.py:129
  29.6 7.8 %collective-permute-start.10 = (bf16[4,160,256]{2,1,0:T(8,128)(2,1)S(1)}, bf16[4,160,256]{2,1,0:T(8,128)(2,1)S(1)}, u32[]{:S(2)}, u32[]{:S(2)}) collective-permute-start(bf16[4,160,256]{2,1,0:T(8,128)(2,1)S(1)} %pad_maximum_fusion.refs_0_), channel_id=1, source_target_pairs={{0,8},{4,12},{8,0},{12,4},{1,9},{5,13},{9,1},{13,5},{2,10},{6,14},... | collective-permute-start | bytes 983048 | tf_op jit(solution)/shard_map/ppermute | solution.py:132
  31.1 11.1 %collective-permute-start.11 = (bf16[4,160,256]{2,1,0:T(8,128)(2,1)S(1)}, bf16[4,160,256]{2,1,0:T(8,128)(2,1)S(1)}, u32[]{:S(2)}, u32[]{:S(2)}) collective-permute-start(bf16[4,160,256]{2,1,0:T(8,128)(2,1)S(1)} %pad_maximum_fusion.1.refs_4_), channel_id=1, source_target_pairs={{0,1},{1,2},{2,3},{3,0},{4,5},{5,6},{6,7},{7,4},{8,9},{9,10},{10,1... | collective-permute-start | bytes 983048 | tf_op jit(solution)/shard_map/ppermute | solution.py:133
  31.1 18.4 %collective-permute-start.12 = (bf16[4,160,256]{2,1,0:T(8,128)(2,1)S(1)}, bf16[4,160,256]{2,1,0:T(8,128)(2,1)S(1)}, u32[]{:S(2)}, u32[]{:S(2)}) collective-permute-start(bf16[4,160,256]{2,1,0:T(8,128)(2,1)S(1)} %pad_maximum_fusion.1.refs_4_), channel_id=1, source_target_pairs={{0,3},{1,0},{2,1},{3,2},{4,7},{5,4},{6,5},{7,6},{8,11},{9,8},{10,9... | collective-permute-start | bytes 983048 | tf_op jit(solution)/shard_map/ppermute | solution.py:133
  33.8 15.8 %collective-permute-start.13 = (bf16[4,160,256]{2,1,0:T(8,128)(2,1)S(1)}, bf16[4,160,256]{2,1,0:T(8,128)(2,1)S(1)}, u32[]{:S(2)}, u32[]{:S(2)}) collective-permute-start(bf16[4,160,256]{2,1,0:T(8,128)(2,1)S(1)} %pad_maximum_fusion.1.refs_4_), channel_id=1, source_target_pairs={{0,2},{1,3},{2,0},{3,1},{4,6},{5,7},{6,4},{7,5},{8,10},{9,11},{10,... | collective-permute-start | bytes 983048 | tf_op jit(solution)/shard_map/ppermute | solution.py:133
  37.4 12.7 %collective-permute-start.8 = (bf16[4,160,256]{2,1,0:T(8,128)(2,1)S(1)}, bf16[4,160,256]{2,1,0:T(8,128)(2,1)S(1)}, u32[]{:S(2)}, u32[]{:S(2)}) collective-permute-start(bf16[4,160,256]{2,1,0:T(8,128)(2,1)S(1)} %pad_maximum_fusion.refs_0_), channel_id=1, source_target_pairs={{0,4},{4,8},{8,12},{12,0},{1,5},{5,9},{9,13},{13,1},{2,6},{6,10},{... | collective-permute-start | bytes 983048 | tf_op jit(solution)/shard_map/ppermute | solution.py:132
  38.7 11.9 %collective-permute-start.9 = (bf16[4,160,256]{2,1,0:T(8,128)(2,1)S(1)}, bf16[4,160,256]{2,1,0:T(8,128)(2,1)}, u32[]{:S(2)}, u32[]{:S(2)}) collective-permute-start(bf16[4,160,256]{2,1,0:T(8,128)(2,1)S(1)} %pad_maximum_fusion.refs_0_), channel_id=1, source_target_pairs={{0,12},{4,0},{8,4},{12,8},{1,13},{5,1},{9,5},{13,9},{2,14},{6,2},{... | collective-permute-start | bytes 983048 | tf_op jit(solution)/shard_map/ppermute | solution.py:132
  42.2 8.8 %collective-permute-start.15 = (bf16[256,512]{1,0:T(8,128)(2,1)}, bf16[256,512]{1,0:T(8,128)(2,1)}, u32[]{:S(2)}, u32[]{:S(2)}) collective-permute-start(bf16[256,512]{1,0:T(8,128)(2,1)} %get-tuple-element.32), channel_id=1, source_target_pairs={{0,32},{32,0},{1,33},{33,1},{2,34},{34,2},{3,35},{35,3},{4,36},{36... | collective-permute-start | bytes 786440 | tf_op jit(solution)/shard_map/ppermute | solution.py:419
  49.5 1.9 %collective-permute-start.16 = (bf16[256,512]{1,0:T(8,128)(2,1)}, bf16[256,512]{1,0:T(8,128)(2,1)}, u32[]{:S(2)}, u32[]{:S(2)}) collective-permute-start(bf16[256,512]{1,0:T(8,128)(2,1)} %get-tuple-element.31), channel_id=1, source_target_pairs={{0,32},{32,0},{1,33},{33,1},{2,34},{34,2},{3,35},{35,3},{4,36},{36... | collective-permute-start | bytes 786440 | tf_op jit(solution)/shard_map/ppermute | solution.py:419
  49.5 2.2 %collective-permute-start.17 = (bf16[256,512]{1,0:T(8,128)(2,1)}, bf16[256,512]{1,0:T(8,128)(2,1)}, u32[]{:S(2)}, u32[]{:S(2)}) collective-permute-start(bf16[256,512]{1,0:T(8,128)(2,1)} %get-tuple-element.30), channel_id=1, source_target_pairs={{0,32},{32,0},{1,33},{33,1},{2,34},{34,2},{3,35},{35,3},{4,36},{36... | collective-permute-start | bytes 786440 | tf_op jit(solution)/shard_map/ppermute | solution.py:419
  50.0 2.1 %collective-permute-start.18 = (bf16[256,512]{1,0:T(8,128)(2,1)}, bf16[256,512]{1,0:T(8,128)(2,1)}, u32[]{:S(2)}, u32[]{:S(2)}) collective-permute-start(bf16[256,512]{1,0:T(8,128)(2,1)} %get-tuple-element.29), channel_id=1, source_target_pairs={{0,32},{32,0},{1,33},{33,1},{2,34},{34,2},{3,35},{35,3},{4,36},{36... | collective-permute-start | bytes 786440 | tf_op jit(solution)/shard_map/ppermute | solution.py:419
  50.5 4.9 %copy-start.1 = (bf16[256,8192]{1,0:T(8,128)(2,1)S(1)}, bf16[256,8192]{1,0:T(8,128)(2,1)}, u32[]{:S(2)}) copy-start(bf16[256,8192]{1,0:T(8,128)(2,1)} %refs_8_.1) | copy-start | bytes 12582916
  50.5 4.9 %copy-start.7 = (f32[256,128]{1,0:T(8,128)S(1)}, f32[256,128]{1,0:T(8,128)}, u32[]{:S(2)}) copy-start(f32[256,128]{1,0:T(8,128)} %copy-done.6) | copy-start | bytes 393220
  55.2 7.0 %collective-permute-start.19 = (bf16[320,256]{1,0:T(8,128)(2,1)S(1)}, bf16[320,256]{1,0:T(8,128)(2,1)S(1)}, u32[]{:S(2)}, u32[]{:S(2)}) collective-permute-start(bf16[320,256]{1,0:T(8,128)(2,1)S(1)} %theirs.1), channel_id=1, source_target_pairs={{0,16},{16,0},{1,17},{17,1},{2,18},{18,2},{3,19},{19,3},{4,20},{20... | collective-permute-start | bytes 491528 | tf_op jit(solution)/shard_map/ppermute | solution.py:434
  58.2 0.7 copy-start.3
  63.4 25.7 %all-to-all-start = ((bf16[128,32,128]{2,1,0:T(8,128)(2,1)}), bf16[128,32,128]{2,1,0:T(8,128)(2,1)S(1)}, u32[]{:S(2)}, u32[]{:S(2)}) async-start(bf16[128,32,128]{2,1,0:T(8,128)(2,1)} %bitcast.16), calls=%async_computation | async-start | bytes 2097152 | tf_op jit(solution)/shard_map/all_to_all | solution.py:440
  70.7 1.0 copy-start.4
  72.1 15.4 %collective-permute-start.21 = (bf16[2,128,256]{2,1,0:T(8,128)(2,1)S(1)}, bf16[2,128,256]{2,1,0:T(8,128)(2,1)S(1)}, u32[]{:S(2)}, u32[]{:S(2)}) collective-permute-start(bf16[2,128,256]{2,1,0:T(8,128)(2,1)S(1)} %q_finish.1.refs_0_), channel_id=1, source_target_pairs={{0,64},{64,0},{1,65},{65,1},{2,66},{66,2},{3,67},{67,3},{4,68},{68... | collective-permute-start | bytes 393224 | tf_op jit(solution)/shard_map/ppermute | solution.py:393
  73.7 14.4 %collective-permute-start.20 = (bf16[2,128,256]{2,1,0:T(8,128)(2,1)S(1)}, bf16[2,128,256]{2,1,0:T(8,128)(2,1)S(1)}, u32[]{:S(2)}, u32[]{:S(2)}) collective-permute-start(bf16[2,128,256]{2,1,0:T(8,128)(2,1)S(1)} %q_finish.1.refs_0_), channel_id=1, source_target_pairs={{0,32},{32,0},{1,33},{33,1},{2,34},{34,2},{3,35},{35,3},{4,36},{36... | collective-permute-start | bytes 393224 | tf_op jit(solution)/shard_map/ppermute | solution.py:391
  87.5 1.6 %collective-permute-start.22 = (bf16[2,128,256]{2,1,0:T(8,128)(2,1)S(1)}, bf16[2,128,256]{2,1,0:T(8,128)(2,1)S(1)}, u32[]{:S(2)}, u32[]{:S(2)}) collective-permute-start(bf16[2,128,256]{2,1,0:T(8,128)(2,1)S(1)} %collective-permute-done.21.refs_2_), channel_id=1, source_target_pairs={{0,32},{32,0},{1,33},{33,1},{2,34},{34,2},{3,35},{35,3},{4,36},{36... | collective-permute-start | bytes 393224 | tf_op jit(solution)/shard_map/ppermute | solution.py:391
  95.4 2.3 %collective-permute-start.23 = (bf16[528,256]{1,0:T(8,128)(2,1)S(1)}, bf16[528,256]{1,0:T(8,128)(2,1)S(1)}, u32[]{:S(2)}, u32[]{:S(2)}) collective-permute-start(bf16[528,256]{1,0:T(8,128)(2,1)S(1)} %get-tuple-element.28), channel_id=1, source_target_pairs={{0,32},{32,0},{1,33},{33,1},{2,34},{34,2},{3,35},{35,3},{4,36},{36... | collective-permute-start | bytes 811016 | tf_op jit(solution)/shard_map/ppermute | solution.py:391
  97.8 7.8 %collective-permute-start.24 = (bf16[528,256]{1,0:T(8,128)(2,1)S(1)}, bf16[528,256]{1,0:T(8,128)(2,1)S(1)}, u32[]{:S(2)}, u32[]{:S(2)}) collective-permute-start(bf16[528,256]{1,0:T(8,128)(2,1)S(1)} %merge.1.a_ref), channel_id=1, source_target_pairs={{0,64},{64,0},{1,65},{65,1},{2,66},{66,2},{3,67},{67,3},{4,68},{68... | collective-permute-start | bytes 811016 | tf_op jit(solution)/shard_map/ppermute | solution.py:393
  105.8 2.4 %collective-permute-start.25 = (bf16[256,512]{1,0:T(8,128)(2,1)S(1)}, bf16[256,512]{1,0:T(8,128)(2,1)S(1)}, u32[]{:S(2)}, u32[]{:S(2)}) collective-permute-start(bf16[256,512]{1,0:T(8,128)(2,1)S(1)} %last.1.mine_ref), channel_id=1, source_target_pairs={{0,32},{32,0},{1,33},{33,1},{2,34},{34,2},{3,35},{35,3},{4,36},{36... | collective-permute-start | bytes 786440 | tf_op jit(solution)/shard_map/ppermute | solution.py:391

commit v7 on v6

--- a/solution.py
+++ b/solution.py
@@ -103,8 +103,8 @@
         ):
             for half in range(2):
                 at = half * 160
-                ref[zl, at:at + 128] = q_ref[0, half * 128:half * 128 + 128, pl.ds(col, 256)] * s
-                ref[zl, at + 128:at + 160] = pair[half * 32:half * 32 + 32]
+                ref[zl, at:at + 128] = (q_ref[0, half * 128:half * 128 + 128, pl.ds(col, 256)] * s).astype(ref.dtype)
+                ref[zl, at + 128:at + 160] = pair[half * 32:half * 32 + 32].astype(ref.dtype)
 
 
 def prepare(idx, num, q, kv):
@@ -113,7 +113,7 @@
         prep_kernel,
         in_specs=[sspec(), sspec()] + [vspec()] * 2,
         out_specs=[vspec(), vspec()],
-        out_shape=[shape, shape],
+        out_shape=[jax.ShapeDtypeStruct(shape.shape, BF16), shape],
         compiler_params=params(),
         cost_estimate=cost(1 << 20, 3 << 20),
         name="prepare",
@@ -395,7 +395,7 @@
 
 
 def average(send, keep, zl, dtype):
-    half = keep + lax.ppermute(send, "c", SWAP)
+    half = keep + lax.ppermute(send, "c", SWAP).astype(F32)
     mine = jnp.where(zl == 0, half[0], half[1])
     theirs = jnp.where(zl == 0, half[1], half[0]).astype(dtype)
     return mine, lax.ppermute(theirs, "zl", SWAP)

time: 110 us -> 110 us (level)
  no operation moved by 1% of the time
where the time goes in v7:
time: 110 us; the launch traced here: 109 us
  starting transfers between devices  42.6 us (39%)
  waiting for transfers between devices  39.5 us (36%)
  Pallas kernels  18.1 us (16%)
  local copies, waits for them, and re-layouts  7.84 us (7%)
    ppermute x2, waiting for transfers between devices, to_rep(): return lax.ppermute(x, 'zl', SWAP)  20.4 us
    ppermute x4, starting transfers between devices, local(): lax.ppermute(got[:, i * width:(i + 1) * width], 'c', SWAP)  8.33 us
    all_to_all x1, starting transfers between devices, local(): lax.all_to_all(pair.reshape(128, 32, 128), ('zh', 'x', 'y', 'zl', 'c'), 0...  6.79 us
    unnamed x18, local copies, waits for them, and re-layouts  6.67 us
    pallas_call x1, Pallas kernels, attend(): pl.pallas_call(attend_kernel, in_specs=[sspec()] + [vspec()] * 5, out_spe...  6.24 us
    pallas_call x2, Pallas kernels, project(): pl.pallas_call(kernel, scratch_shapes=scratch, in_specs=[sspec()] + [vspe...  5.76 us
    ppermute x3, starting transfers between devices, gather_plane(): lowers = [lower] + [lax.ppermute(lower, 'x', ring(d)) for d in (1, 3, 2)]  4.31 us
    ppermute x3, starting transfers between devices, gather_plane(): lax.ppermute(upper, 'x', ring(d))  4.28 us
  transfers between devices with their start and end apart: 27, of which 17 were waited for; matrix products, arithmetic and copies ran while one was open for 2% of the time, Pallas kernels for 4%

profile of v7, /device:TPU:1, one launch (start us, length us, event | category | flops | bytes accessed | tf_op | source)
XLA Modules:
  0.0 109.2 jit_solution(880224114460737648)
XLA Ops:
  0.0 0.1 stack.57.idx
  0.1 1.2 %copy-done.2 = f32[1,256,1024]{2,1,0:T(8,128)S(1)} copy-done((f32[1,256,1024]{2,1,0:T(8,128)S(1)}, f32[1,256,1024]{2,1,0:T(8,128)}, u32[]{:S(2)}) %copy-start.2) | copy-done | bytes 1048600
  1.3 0.9 copy-done.5
  2.3 0.7 copy-done.8
  2.9 1.0 prepare.1
  3.9 1.5 %collective-permute-start = (bf16[2,320,256]{2,1,0:T(8,128)(2,1)S(1)}, bf16[2,320,256]{2,1,0:T(8,128)(2,1)S(1)}, u32[]{:S(2)}, u32[]{:S(2)}) collective-permute-start(bf16[2,320,256]{2,1,0:T(8,128)(2,1)S(1)} %get-tuple-element.18), channel_id=1, source_target_pairs={{0,32},{32,0},{1,33},{33,1},{2,34},{34,2},{3,35},{35,3},{4,36},{36... | collective-permute-start | bytes 983048 | tf_op jit(solution)/shard_map/ppermute | solution.py:398
  5.4 1.3 %collective-permute-done = bf16[2,320,256]{2,1,0:T(8,128)(2,1)S(1)} collective-permute-done((bf16[2,320,256]{2,1,0:T(8,128)(2,1)S(1)}, bf16[2,320,256]{2,1,0:T(8,128)(2,1)S(1)}, u32[]{:S(2)}, u32[]{:S(2)}) %collective-permute-start) | collective-permute-done | bytes 327712 | tf_op jit(solution)/shard_map/ppermute | solution.py:398
  6.7 0.1 convert_add_fusion
  6.8 1.8 %collective-permute-start.1 = (bf16[320,256]{1,0:T(8,128)(2,1)S(1)}, bf16[320,256]{1,0:T(8,128)(2,1)S(1)}, u32[]{:S(2)}, u32[]{:S(2)}) collective-permute-start(bf16[320,256]{1,0:T(8,128)(2,1)S(1)} %fusion.1), channel_id=1, source_target_pairs={{0,64},{64,0},{1,65},{65,1},{2,66},{66,2},{3,67},{67,3},{4,68},{68... | collective-permute-start | bytes 491528 | tf_op jit(solution)/shard_map/ppermute | solution.py:401
  8.6 2.2 %copy-done = bf16[256,8192]{1,0:T(8,128)(2,1)S(1)} copy-done((bf16[256,8192]{1,0:T(8,128)(2,1)S(1)}, bf16[256,8192]{1,0:T(8,128)(2,1)}, u32[]{:S(2)}) %copy-start) | copy-done | bytes 4194328
  10.8 1.8 %normalise.1 = (f32[256,128]{1,0:T(8,128)S(1)}, bf16[256,2048]{1,0:T(8,128)(2,1)S(1)}) custom-call(s32[6]{0:T(128)S(1)} %stack.57.idx, bf16[256,8192]{1,0:T(8,128)(2,1)S(1)} %copy-done), custom_call_target="tpu_custom_call" | custom-call | flops 8388608 | bytes 6291456 | tf_op jit(solution)/shard_map/normalise/pallas_call | solution.py:64
  12.6 0.3 collective-permute-done.1
  12.8 3.1 %collective-permute-start.14 = (bf16[256,2048]{1,0:T(8,128)(2,1)S(1)}, bf16[256,2048]{1,0:T(8,128)(2,1)S(1)}, u32[]{:S(2)}, u32[]{:S(2)}) collective-permute-start(bf16[256,2048]{1,0:T(8,128)(2,1)S(1)} %get-tuple-element.25), channel_id=1, source_target_pairs={{0,16},{16,0},{1,17},{17,1},{2,18},{18,2},{3,19},{19,3},{4,20},{20... | collective-permute-start | bytes 3145736 | tf_op jit(solution)/shard_map/ppermute | solution.py:417
  16.0 0.1 fusion
  16.0 1.3 %collective-permute-start.5 = (bf16[160,256]{1,0:T(8,128)(2,1)S(1)}, bf16[160,256]{1,0:T(8,128)(2,1)S(1)}, u32[]{:S(2)}, u32[]{:S(2)}) collective-permute-start(bf16[160,256]{1,0:T(8,128)(2,1)S(1)} %get-tuple-element.35), channel_id=1, source_target_pairs={{0,4},{4,8},{8,12},{12,0},{1,5},{5,9},{9,13},{13,1},{2,6},{6,10},{... | collective-permute-start | bytes 245768 | tf_op jit(solution)/shard_map/ppermute | solution.py:130
  17.3 1.5 %collective-permute-start.6 = (bf16[160,256]{1,0:T(8,128)(2,1)S(1)}, bf16[160,256]{1,0:T(8,128)(2,1)S(1)}, u32[]{:S(2)}, u32[]{:S(2)}) collective-permute-start(bf16[160,256]{1,0:T(8,128)(2,1)S(1)} %get-tuple-element.35), channel_id=1, source_target_pairs={{0,12},{4,0},{8,4},{12,8},{1,13},{5,1},{9,5},{13,9},{2,14},{6,2},{... | collective-permute-start | bytes 245768 | tf_op jit(solution)/shard_map/ppermute | solution.py:130
  18.8 1.5 %collective-permute-start.7 = (bf16[160,256]{1,0:T(8,128)(2,1)S(1)}, bf16[160,256]{1,0:T(8,128)(2,1)S(1)}, u32[]{:S(2)}, u32[]{:S(2)}) collective-permute-start(bf16[160,256]{1,0:T(8,128)(2,1)S(1)} %get-tuple-element.35), channel_id=1, source_target_pairs={{0,8},{4,12},{8,0},{12,4},{1,9},{5,13},{9,1},{13,5},{2,10},{6,14},... | collective-permute-start | bytes 245768 | tf_op jit(solution)/shard_map/ppermute | solution.py:130
  20.3 2.7 %collective-permute-start.3 = (bf16[160,256]{1,0:T(8,128)(2,1)S(1)}, bf16[160,256]{1,0:T(8,128)(2,1)S(1)}, u32[]{:S(2)}, u32[]{:S(2)}) collective-permute-start(bf16[160,256]{1,0:T(8,128)(2,1)S(1)} %get-tuple-element.36), channel_id=1, source_target_pairs={{0,3},{1,0},{2,1},{3,2},{4,7},{5,4},{6,5},{7,6},{8,11},{9,8},{10,9... | collective-permute-start | bytes 245768 | tf_op jit(solution)/shard_map/ppermute | solution.py:129
  23.1 0.8 collective-permute-start.4
  23.8 0.4 collective-permute-start.2
  24.2 0.5 collective-permute-done.7
  24.8 3.4 %collective-permute-done.4 = bf16[160,256]{1,0:T(8,128)(2,1)S(1)} collective-permute-done((bf16[160,256]{1,0:T(8,128)(2,1)S(1)}, bf16[160,256]{1,0:T(8,128)(2,1)S(1)}, u32[]{:S(2)}, u32[]{:S(2)}) %collective-permute-start.4) | collective-permute-done | bytes 81952 | tf_op jit(solution)/shard_map/ppermute | solution.py:129
  28.2 0.9 collective-permute-done.2
  29.1 1.5 %collective-permute-start.10 = (bf16[4,160,256]{2,1,0:T(8,128)(2,1)S(1)}, bf16[4,160,256]{2,1,0:T(8,128)(2,1)S(1)}, u32[]{:S(2)}, u32[]{:S(2)}) collective-permute-start(bf16[4,160,256]{2,1,0:T(8,128)(2,1)S(1)} %pad_maximum_fusion.refs_0_), channel_id=1, source_target_pairs={{0,8},{4,12},{8,0},{12,4},{1,9},{5,13},{9,1},{13,5},{2,10},{6,14},... | collective-permute-start | bytes 983048 | tf_op jit(solution)/shard_map/ppermute | solution.py:132
  30.6 2.7 %collective-permute-start.12 = (bf16[4,160,256]{2,1,0:T(8,128)(2,1)S(1)}, bf16[4,160,256]{2,1,0:T(8,128)(2,1)S(1)}, u32[]{:S(2)}, u32[]{:S(2)}) collective-permute-start(bf16[4,160,256]{2,1,0:T(8,128)(2,1)S(1)} %pad_maximum_fusion.1.refs_4_), channel_id=1, source_target_pairs={{0,3},{1,0},{2,1},{3,2},{4,7},{5,4},{6,5},{7,6},{8,11},{9,8},{10,9... | collective-permute-start | bytes 983048 | tf_op jit(solution)/shard_map/ppermute | solution.py:133
  33.3 3.6 %collective-permute-done.10.refs_3_ = bf16[4,160,256]{2,1,0:T(8,128)(2,1)S(1)} collective-permute-done((bf16[4,160,256]{2,1,0:T(8,128)(2,1)S(1)}, bf16[4,160,256]{2,1,0:T(8,128)(2,1)S(1)}, u32[]{:S(2)}, u32[]{:S(2)}) %collective-permute-start.10) | collective-permute-done | bytes 327712 | tf_op jit(solution)/shard_map/ppermute | solution.py:132
  36.9 0.3 collective-permute-start.8
  37.2 1.0 collective-permute-done.14.refs_8_
  38.2 2.5 %collective-permute-start.9 = (bf16[4,160,256]{2,1,0:T(8,128)(2,1)S(1)}, bf16[4,160,256]{2,1,0:T(8,128)(2,1)}, u32[]{:S(2)}, u32[]{:S(2)}) collective-permute-start(bf16[4,160,256]{2,1,0:T(8,128)(2,1)S(1)} %pad_maximum_fusion.refs_0_), channel_id=1, source_target_pairs={{0,12},{4,0},{8,4},{12,8},{1,13},{5,1},{9,5},{13,9},{2,14},{6,2},{... | collective-permute-start | bytes 983048 | tf_op jit(solution)/shard_map/ppermute | solution.py:132
  40.7 1.0 fusion.2
  41.7 7.3 %collective-permute-start.15 = (bf16[256,512]{1,0:T(8,128)(2,1)}, bf16[256,512]{1,0:T(8,128)(2,1)}, u32[]{:S(2)}, u32[]{:S(2)}) collective-permute-start(bf16[256,512]{1,0:T(8,128)(2,1)} %get-tuple-element.32), channel_id=1, source_target_pairs={{0,32},{32,0},{1,33},{33,1},{2,34},{34,2},{3,35},{35,3},{4,36},{36... | collective-permute-start | bytes 786440 | tf_op jit(solution)/shard_map/ppermute | solution.py:419
  49.0 0.5 collective-permute-start.17
  49.5 0.5 collective-permute-start.18
  50.1 0.1 dynamic_slice.3
  50.2 0.4 collective-permute-done.15.refs_9_
  50.5 0.4 collective-permute-done.16.refs_10_
  50.9 0.4 collective-permute-done.17.refs_11_
  51.3 0.4 collective-permute-done.18.refs_12_
  51.7 3.1 %theirs.1 = bf16[320,256]{1,0:T(8,128)(2,1)S(1)} custom-call(s32[6]{0:T(128)S(1)} %stack.57.idx, bf16[4,160,256]{2,1,0:T(8,128)(2,1)S(1)} %pad_maximum_fusion.refs_0_, bf16[4,160,256]{2,1,0:T(8,128)(2,1)S(1)} %collective-permute-done.8.refs_1_, bf16[4,160,256]{2,1,0:T(8,128)(2,1)} %collective-permute-done.9.refs_2_, ...), custom_call_target="tpu_custom_call" | custom-call | flops 671088640 | bytes 5242880 | tf_op jit(solution)/shard_map/theirs/pallas_call | solution.py:190
  54.7 0.1 collective-permute-start.19
  54.8 0.1 multiply_sine_fusion.1
  55.0 2.7 %own.1 = (f32[256,256]{1,0:T(8,128)S(1)}, f32[64,256]{1,0:T(8,128)S(1)}) custom-call(s32[6]{0:T(128)S(1)} %stack.57.idx, bf16[4,160,256]{2,1,0:T(8,128)(2,1)S(1)} %pad_maximum_fusion.refs_0_, bf16[4,160,256]{2,1,0:T(8,128)(2,1)S(1)} %collective-permute-done.8.refs_1_, bf16[4,160,256]{2,1,0:T(8,128)(2,1)} %collective-permute-done.9.refs_2_, ...), custom_call_target="tpu_custom_call" | custom-call | flops 671088640 | bytes 5242880 | tf_op jit(solution)/shard_map/own/pallas_call | solution.py:190
  57.7 0.7 copy-done.3
  58.4 3.3 %collective-permute-done.19.got_ref = bf16[320,256]{1,0:T(8,128)(2,1)S(1)} collective-permute-done((bf16[320,256]{1,0:T(8,128)(2,1)S(1)}, bf16[320,256]{1,0:T(8,128)(2,1)S(1)}, u32[]{:S(2)}, u32[]{:S(2)}) %collective-permute-start.19) | collective-permute-done | bytes 163872 | tf_op jit(solution)/shard_map/ppermute | solution.py:434
  61.7 1.2 %pair_finish.1 = bf16[32,4,32,128]{3,2,1,0:T(8,128)(2,1)} custom-call(f32[64,256]{1,0:T(8,128)S(1)} %get-tuple-element.26.own_ref, bf16[320,256]{1,0:T(8,128)(2,1)S(1)} %collective-permute-done.19.got_ref, f32[16,256]{1,0:T(8,128)S(1)} %get-tuple-element.38.cos_ref, f32[16,256]{1,0:T(8,128)S(1)} %get-tuple-element.37.sin_ref), custom_call_target="tpu_custom_call" | custom-call | flops 262144 | bytes 1048576 | tf_op jit(solution)/shard_map/pair_finish/pallas_call | solution.py:226
  62.9 6.8 %all-to-all-start = ((bf16[128,32,128]{2,1,0:T(8,128)(2,1)}), bf16[128,32,128]{2,1,0:T(8,128)(2,1)S(1)}, u32[]{:S(2)}, u32[]{:S(2)}) async-start(bf16[128,32,128]{2,1,0:T(8,128)(2,1)} %bitcast.16), calls=%async_computation | async-start | bytes 2097152 | tf_op jit(solution)/shard_map/all_to_all | solution.py:440
  69.7 0.5 multiply_sine_fusion
  70.2 0.9 copy-done.4
  71.2 0.4 q_finish.1.refs_0_
  71.6 1.6 %collective-permute-start.21 = (bf16[2,128,256]{2,1,0:T(8,128)(2,1)S(1)}, bf16[2,128,256]{2,1,0:T(8,128)(2,1)S(1)}, u32[]{:S(2)}, u32[]{:S(2)}) collective-permute-start(bf16[2,128,256]{2,1,0:T(8,128)(2,1)S(1)} %q_finish.1.refs_0_), channel_id=1, source_target_pairs={{0,64},{64,0},{1,65},{65,1},{2,66},{66,2},{3,67},{67,3},{4,68},{68... | collective-permute-start | bytes 393224 | tf_op jit(solution)/shard_map/ppermute | solution.py:393
  73.2 0.6 collective-permute-start.20
  73.8 13.2 %collective-permute-done.21.refs_2_ = bf16[2,128,256]{2,1,0:T(8,128)(2,1)S(1)} collective-permute-done((bf16[2,128,256]{2,1,0:T(8,128)(2,1)S(1)}, bf16[2,128,256]{2,1,0:T(8,128)(2,1)S(1)}, u32[]{:S(2)}, u32[]{:S(2)}) %collective-permute-start.21) | collective-permute-done | bytes 131104 | tf_op jit(solution)/shard_map/ppermute | solution.py:393
  87.0 0.6 collective-permute-start.22
  87.6 1.0 collective-permute-done.22.refs_3_
  88.6 6.2 %attend.1 = (bf16[528,256]{1,0:T(8,128)(2,1)S(1)}, bf16[528,256]{1,0:T(8,128)(2,1)S(1)}) custom-call(s32[6]{0:T(128)S(1)} %stack.57.idx, bf16[2,128,256]{2,1,0:T(8,128)(2,1)S(1)} %q_finish.1.refs_0_, bf16[2,128,256]{2,1,0:T(8,128)(2,1)S(1)} %collective-permute-done.20.refs_1_, bf16[2,128,256]{2,1,0:T(8,128)(2,1)S(1)} %collective-permute-done.21.refs_2_, ...), custom_call_target="tpu_custom_call" | custom-call | flops 2147483648 | bytes 4194304 | tf_op jit(solution)/shard_map/attend/pallas_call | solution.py:310
  94.9 1.1 collective-permute-start.23
  96.0 1.2 %collective-permute-done.23.b_ref = bf16[528,256]{1,0:T(8,128)(2,1)S(1)} collective-permute-done((bf16[528,256]{1,0:T(8,128)(2,1)S(1)}, bf16[528,256]{1,0:T(8,128)(2,1)S(1)}, u32[]{:S(2)}, u32[]{:S(2)}) %collective-permute-start.23) | collective-permute-done | bytes 270368 | tf_op jit(solution)/shard_map/ppermute | solution.py:391
  97.1 0.2 merge.1.a_ref
  97.3 0.6 collective-permute-start.24
  97.9 7.2 %collective-permute-done.24.b_ref = bf16[528,256]{1,0:T(8,128)(2,1)S(1)} collective-permute-done((bf16[528,256]{1,0:T(8,128)(2,1)S(1)}, bf16[528,256]{1,0:T(8,128)(2,1)S(1)}, u32[]{:S(2)}, u32[]{:S(2)}) %collective-permute-start.24) | collective-permute-done | bytes 270368 | tf_op jit(solution)/shard_map/ppermute | solution.py:393
  105.1 0.2 last.1.mine_ref
  105.3 1.3 %collective-permute-start.25 = (bf16[256,512]{1,0:T(8,128)(2,1)S(1)}, bf16[256,512]{1,0:T(8,128)(2,1)S(1)}, u32[]{:S(2)}, u32[]{:S(2)}) collective-permute-start(bf16[256,512]{1,0:T(8,128)(2,1)S(1)} %last.1.mine_ref), channel_id=1, source_target_pairs={{0,32},{32,0},{1,33},{33,1},{2,34},{34,2},{3,35},{35,3},{4,36},{36... | collective-permute-start | bytes 786440 | tf_op jit(solution)/shard_map/ppermute | solution.py:391
  106.6 1.2 %collective-permute-done.25.other_ref = bf16[256,512]{1,0:T(8,128)(2,1)S(1)} collective-permute-done((bf16[256,512]{1,0:T(8,128)(2,1)S(1)}, bf16[256,512]{1,0:T(8,128)(2,1)S(1)}, u32[]{:S(2)}, u32[]{:S(2)}) %collective-permute-start.25) | collective-permute-done | bytes 262176 | tf_op jit(solution)/shard_map/ppermute | solution.py:391
  107.8 1.4 %place.1 = bf16[256,1024]{1,0:T(8,128)(2,1)} custom-call(s32[6]{0:T(128)S(1)} %stack.57.idx, bf16[256,512]{1,0:T(8,128)(2,1)S(1)} %last.1.mine_ref, bf16[256,512]{1,0:T(8,128)(2,1)S(1)} %collective-permute-done.25.other_ref), custom_call_target="tpu_custom_call" | custom-call | flops 524288 | bytes 1048576 | tf_op jit(solution)/shard_map/place/pallas_call | solution.py:375
  (31 shorter events, 0.2 us)
Async XLA Ops:
  0.1 1.2 %copy-start.2 = (f32[1,256,1024]{2,1,0:T(8,128)S(1)}, f32[1,256,1024]{2,1,0:T(8,128)}, u32[]{:S(2)}) copy-start(f32[1,256,1024]{2,1,0:T(8,128)} %q_ref.1) | copy-start | bytes 3145732
  1.3 0.9 copy-start.5
  2.3 0.7 copy-start.8
  3.9 2.8 %collective-permute-start = (bf16[2,320,256]{2,1,0:T(8,128)(2,1)S(1)}, bf16[2,320,256]{2,1,0:T(8,128)(2,1)S(1)}, u32[]{:S(2)}, u32[]{:S(2)}) collective-permute-start(bf16[2,320,256]{2,1,0:T(8,128)(2,1)S(1)} %get-tuple-element.18), channel_id=1, source_target_pairs={{0,32},{32,0},{1,33},{33,1},{2,34},{34,2},{3,35},{35,3},{4,36},{36... | collective-permute-start | bytes 983048 | tf_op jit(solution)/shard_map/ppermute | solution.py:398
  6.8 6.0 %collective-permute-start.1 = (bf16[320,256]{1,0:T(8,128)(2,1)S(1)}, bf16[320,256]{1,0:T(8,128)(2,1)S(1)}, u32[]{:S(2)}, u32[]{:S(2)}) collective-permute-start(bf16[320,256]{1,0:T(8,128)(2,1)S(1)} %fusion.1), channel_id=1, source_target_pairs={{0,64},{64,0},{1,65},{65,1},{2,66},{66,2},{3,67},{67,3},{4,68},{68... | collective-permute-start | bytes 491528 | tf_op jit(solution)/shard_map/ppermute | solution.py:401
  8.6 2.2 %copy-start = (bf16[256,8192]{1,0:T(8,128)(2,1)S(1)}, bf16[256,8192]{1,0:T(8,128)(2,1)}, u32[]{:S(2)}) copy-start(bf16[256,8192]{1,0:T(8,128)(2,1)} %refs_8_.1) | copy-start | bytes 12582916
  12.5 37.0 %copy-start.6 = (f32[256,128]{1,0:T(8,128)}, f32[256,128]{1,0:T(8,128)S(1)}, u32[]{:S(2)}) copy-start(f32[256,128]{1,0:T(8,128)S(1)} %get-tuple-element.23.refs_9_) | copy-start | bytes 393220
  12.8 25.4 %collective-permute-start.14 = (bf16[256,2048]{1,0:T(8,128)(2,1)S(1)}, bf16[256,2048]{1,0:T(8,128)(2,1)S(1)}, u32[]{:S(2)}, u32[]{:S(2)}) collective-permute-start(bf16[256,2048]{1,0:T(8,128)(2,1)S(1)} %get-tuple-element.25), channel_id=1, source_target_pairs={{0,16},{16,0},{1,17},{17,1},{2,18},{18,2},{3,19},{19,3},{4,20},{20... | collective-permute-start | bytes 3145736 | tf_op jit(solution)/shard_map/ppermute | solution.py:417
  16.0 7.0 %collective-permute-start.5 = (bf16[160,256]{1,0:T(8,128)(2,1)S(1)}, bf16[160,256]{1,0:T(8,128)(2,1)S(1)}, u32[]{:S(2)}, u32[]{:S(2)}) collective-permute-start(bf16[160,256]{1,0:T(8,128)(2,1)S(1)} %get-tuple-element.35), channel_id=1, source_target_pairs={{0,4},{4,8},{8,12},{12,0},{1,5},{5,9},{9,13},{13,1},{2,6},{6,10},{... | collective-permute-start | bytes 245768 | tf_op jit(solution)/shard_map/ppermute | solution.py:130
  17.3 6.5 %collective-permute-start.6 = (bf16[160,256]{1,0:T(8,128)(2,1)S(1)}, bf16[160,256]{1,0:T(8,128)(2,1)S(1)}, u32[]{:S(2)}, u32[]{:S(2)}) collective-permute-start(bf16[160,256]{1,0:T(8,128)(2,1)S(1)} %get-tuple-element.35), channel_id=1, source_target_pairs={{0,12},{4,0},{8,4},{12,8},{1,13},{5,1},{9,5},{13,9},{2,14},{6,2},{... | collective-permute-start | bytes 245768 | tf_op jit(solution)/shard_map/ppermute | solution.py:130
  18.8 5.9 %collective-permute-start.7 = (bf16[160,256]{1,0:T(8,128)(2,1)S(1)}, bf16[160,256]{1,0:T(8,128)(2,1)S(1)}, u32[]{:S(2)}, u32[]{:S(2)}) collective-permute-start(bf16[160,256]{1,0:T(8,128)(2,1)S(1)} %get-tuple-element.35), channel_id=1, source_target_pairs={{0,8},{4,12},{8,0},{12,4},{1,9},{5,13},{9,1},{13,5},{2,10},{6,14},... | collective-permute-start | bytes 245768 | tf_op jit(solution)/shard_map/ppermute | solution.py:130
  20.3 4.4 %collective-permute-start.3 = (bf16[160,256]{1,0:T(8,128)(2,1)S(1)}, bf16[160,256]{1,0:T(8,128)(2,1)S(1)}, u32[]{:S(2)}, u32[]{:S(2)}) collective-permute-start(bf16[160,256]{1,0:T(8,128)(2,1)S(1)} %get-tuple-element.36), channel_id=1, source_target_pairs={{0,3},{1,0},{2,1},{3,2},{4,7},{5,4},{6,5},{7,6},{8,11},{9,8},{10,9... | collective-permute-start | bytes 245768 | tf_op jit(solution)/shard_map/ppermute | solution.py:129
  23.1 5.1 %collective-permute-start.4 = (bf16[160,256]{1,0:T(8,128)(2,1)S(1)}, bf16[160,256]{1,0:T(8,128)(2,1)S(1)}, u32[]{:S(2)}, u32[]{:S(2)}) collective-permute-start(bf16[160,256]{1,0:T(8,128)(2,1)S(1)} %get-tuple-element.36), channel_id=1, source_target_pairs={{0,2},{1,3},{2,0},{3,1},{4,6},{5,7},{6,4},{7,5},{8,10},{9,11},{10,... | collective-permute-start | bytes 245768 | tf_op jit(solution)/shard_map/ppermute | solution.py:129
  23.8 5.2 %collective-permute-start.2 = (bf16[160,256]{1,0:T(8,128)(2,1)S(1)}, bf16[160,256]{1,0:T(8,128)(2,1)S(1)}, u32[]{:S(2)}, u32[]{:S(2)}) collective-permute-start(bf16[160,256]{1,0:T(8,128)(2,1)S(1)} %get-tuple-element.36), channel_id=1, source_target_pairs={{0,1},{1,2},{2,3},{3,0},{4,5},{5,6},{6,7},{7,4},{8,9},{9,10},{10,1... | collective-permute-start | bytes 245768 | tf_op jit(solution)/shard_map/ppermute | solution.py:129
  29.1 7.8 %collective-permute-start.10 = (bf16[4,160,256]{2,1,0:T(8,128)(2,1)S(1)}, bf16[4,160,256]{2,1,0:T(8,128)(2,1)S(1)}, u32[]{:S(2)}, u32[]{:S(2)}) collective-permute-start(bf16[4,160,256]{2,1,0:T(8,128)(2,1)S(1)} %pad_maximum_fusion.refs_0_), channel_id=1, source_target_pairs={{0,8},{4,12},{8,0},{12,4},{1,9},{5,13},{9,1},{13,5},{2,10},{6,14},... | collective-permute-start | bytes 983048 | tf_op jit(solution)/shard_map/ppermute | solution.py:132
  30.6 11.1 %collective-permute-start.11 = (bf16[4,160,256]{2,1,0:T(8,128)(2,1)S(1)}, bf16[4,160,256]{2,1,0:T(8,128)(2,1)S(1)}, u32[]{:S(2)}, u32[]{:S(2)}) collective-permute-start(bf16[4,160,256]{2,1,0:T(8,128)(2,1)S(1)} %pad_maximum_fusion.1.refs_4_), channel_id=1, source_target_pairs={{0,1},{1,2},{2,3},{3,0},{4,5},{5,6},{6,7},{7,4},{8,9},{9,10},{10,1... | collective-permute-start | bytes 983048 | tf_op jit(solution)/shard_map/ppermute | solution.py:133
  30.6 18.4 %collective-permute-start.12 = (bf16[4,160,256]{2,1,0:T(8,128)(2,1)S(1)}, bf16[4,160,256]{2,1,0:T(8,128)(2,1)S(1)}, u32[]{:S(2)}, u32[]{:S(2)}) collective-permute-start(bf16[4,160,256]{2,1,0:T(8,128)(2,1)S(1)} %pad_maximum_fusion.1.refs_4_), channel_id=1, source_target_pairs={{0,3},{1,0},{2,1},{3,2},{4,7},{5,4},{6,5},{7,6},{8,11},{9,8},{10,9... | collective-permute-start | bytes 983048 | tf_op jit(solution)/shard_map/ppermute | solution.py:133
  33.3 15.8 %collective-permute-start.13 = (bf16[4,160,256]{2,1,0:T(8,128)(2,1)S(1)}, bf16[4,160,256]{2,1,0:T(8,128)(2,1)S(1)}, u32[]{:S(2)}, u32[]{:S(2)}) collective-permute-start(bf16[4,160,256]{2,1,0:T(8,128)(2,1)S(1)} %pad_maximum_fusion.1.refs_4_), channel_id=1, source_target_pairs={{0,2},{1,3},{2,0},{3,1},{4,6},{5,7},{6,4},{7,5},{8,10},{9,11},{10,... | collective-permute-start | bytes 983048 | tf_op jit(solution)/shard_map/ppermute | solution.py:133
  36.9 12.7 %collective-permute-start.8 = (bf16[4,160,256]{2,1,0:T(8,128)(2,1)S(1)}, bf16[4,160,256]{2,1,0:T(8,128)(2,1)S(1)}, u32[]{:S(2)}, u32[]{:S(2)}) collective-permute-start(bf16[4,160,256]{2,1,0:T(8,128)(2,1)S(1)} %pad_maximum_fusion.refs_0_), channel_id=1, source_target_pairs={{0,4},{4,8},{8,12},{12,0},{1,5},{5,9},{9,13},{13,1},{2,6},{6,10},{... | collective-permute-start | bytes 983048 | tf_op jit(solution)/shard_map/ppermute | solution.py:132
  38.2 11.9 %collective-permute-start.9 = (bf16[4,160,256]{2,1,0:T(8,128)(2,1)S(1)}, bf16[4,160,256]{2,1,0:T(8,128)(2,1)}, u32[]{:S(2)}, u32[]{:S(2)}) collective-permute-start(bf16[4,160,256]{2,1,0:T(8,128)(2,1)S(1)} %pad_maximum_fusion.refs_0_), channel_id=1, source_target_pairs={{0,12},{4,0},{8,4},{12,8},{1,13},{5,1},{9,5},{13,9},{2,14},{6,2},{... | collective-permute-start | bytes 983048 | tf_op jit(solution)/shard_map/ppermute | solution.py:132
  41.7 8.8 %collective-permute-start.15 = (bf16[256,512]{1,0:T(8,128)(2,1)}, bf16[256,512]{1,0:T(8,128)(2,1)}, u32[]{:S(2)}, u32[]{:S(2)}) collective-permute-start(bf16[256,512]{1,0:T(8,128)(2,1)} %get-tuple-element.32), channel_id=1, source_target_pairs={{0,32},{32,0},{1,33},{33,1},{2,34},{34,2},{3,35},{35,3},{4,36},{36... | collective-permute-start | bytes 786440 | tf_op jit(solution)/shard_map/ppermute | solution.py:419
  49.0 1.9 %collective-permute-start.16 = (bf16[256,512]{1,0:T(8,128)(2,1)}, bf16[256,512]{1,0:T(8,128)(2,1)}, u32[]{:S(2)}, u32[]{:S(2)}) collective-permute-start(bf16[256,512]{1,0:T(8,128)(2,1)} %get-tuple-element.31), channel_id=1, source_target_pairs={{0,32},{32,0},{1,33},{33,1},{2,34},{34,2},{3,35},{35,3},{4,36},{36... | collective-permute-start | bytes 786440 | tf_op jit(solution)/shard_map/ppermute | solution.py:419
  49.0 2.2 %collective-permute-start.17 = (bf16[256,512]{1,0:T(8,128)(2,1)}, bf16[256,512]{1,0:T(8,128)(2,1)}, u32[]{:S(2)}, u32[]{:S(2)}) collective-permute-start(bf16[256,512]{1,0:T(8,128)(2,1)} %get-tuple-element.30), channel_id=1, source_target_pairs={{0,32},{32,0},{1,33},{33,1},{2,34},{34,2},{3,35},{35,3},{4,36},{36... | collective-permute-start | bytes 786440 | tf_op jit(solution)/shard_map/ppermute | solution.py:419
  49.5 2.1 %collective-permute-start.18 = (bf16[256,512]{1,0:T(8,128)(2,1)}, bf16[256,512]{1,0:T(8,128)(2,1)}, u32[]{:S(2)}, u32[]{:S(2)}) collective-permute-start(bf16[256,512]{1,0:T(8,128)(2,1)} %get-tuple-element.29), channel_id=1, source_target_pairs={{0,32},{32,0},{1,33},{33,1},{2,34},{34,2},{3,35},{35,3},{4,36},{36... | collective-permute-start | bytes 786440 | tf_op jit(solution)/shard_map/ppermute | solution.py:419
  50.0 4.9 %copy-start.1 = (bf16[256,8192]{1,0:T(8,128)(2,1)S(1)}, bf16[256,8192]{1,0:T(8,128)(2,1)}, u32[]{:S(2)}) copy-start(bf16[256,8192]{1,0:T(8,128)(2,1)} %refs_8_.1) | copy-start | bytes 12582916
  50.1 4.9 %copy-start.7 = (f32[256,128]{1,0:T(8,128)S(1)}, f32[256,128]{1,0:T(8,128)}, u32[]{:S(2)}) copy-start(f32[256,128]{1,0:T(8,128)} %copy-done.6) | copy-start | bytes 393220
  54.7 7.0 %collective-permute-start.19 = (bf16[320,256]{1,0:T(8,128)(2,1)S(1)}, bf16[320,256]{1,0:T(8,128)(2,1)S(1)}, u32[]{:S(2)}, u32[]{:S(2)}) collective-permute-start(bf16[320,256]{1,0:T(8,128)(2,1)S(1)} %theirs.1), channel_id=1, source_target_pairs={{0,16},{16,0},{1,17},{17,1},{2,18},{18,2},{3,19},{19,3},{4,20},{20... | collective-permute-start | bytes 491528 | tf_op jit(solution)/shard_map/ppermute | solution.py:434
  57.7 0.7 copy-start.3
  62.9 25.7 %all-to-all-start = ((bf16[128,32,128]{2,1,0:T(8,128)(2,1)}), bf16[128,32,128]{2,1,0:T(8,128)(2,1)S(1)}, u32[]{:S(2)}, u32[]{:S(2)}) async-start(bf16[128,32,128]{2,1,0:T(8,128)(2,1)} %bitcast.16), calls=%async_computation | async-start | bytes 2097152 | tf_op jit(solution)/shard_map/all_to_all | solution.py:440
  70.2 1.0 copy-start.4
  71.6 15.4 %collective-permute-start.21 = (bf16[2,128,256]{2,1,0:T(8,128)(2,1)S(1)}, bf16[2,128,256]{2,1,0:T(8,128)(2,1)S(1)}, u32[]{:S(2)}, u32[]{:S(2)}) collective-permute-start(bf16[2,128,256]{2,1,0:T(8,128)(2,1)S(1)} %q_finish.1.refs_0_), channel_id=1, source_target_pairs={{0,64},{64,0},{1,65},{65,1},{2,66},{66,2},{3,67},{67,3},{4,68},{68... | collective-permute-start | bytes 393224 | tf_op jit(solution)/shard_map/ppermute | solution.py:393
  73.2 14.4 %collective-permute-start.20 = (bf16[2,128,256]{2,1,0:T(8,128)(2,1)S(1)}, bf16[2,128,256]{2,1,0:T(8,128)(2,1)S(1)}, u32[]{:S(2)}, u32[]{:S(2)}) collective-permute-start(bf16[2,128,256]{2,1,0:T(8,128)(2,1)S(1)} %q_finish.1.refs_0_), channel_id=1, source_target_pairs={{0,32},{32,0},{1,33},{33,1},{2,34},{34,2},{3,35},{35,3},{4,36},{36... | collective-permute-start | bytes 393224 | tf_op jit(solution)/shard_map/ppermute | solution.py:391
  87.0 1.6 %collective-permute-start.22 = (bf16[2,128,256]{2,1,0:T(8,128)(2,1)S(1)}, bf16[2,128,256]{2,1,0:T(8,128)(2,1)S(1)}, u32[]{:S(2)}, u32[]{:S(2)}) collective-permute-start(bf16[2,128,256]{2,1,0:T(8,128)(2,1)S(1)} %collective-permute-done.21.refs_2_), channel_id=1, source_target_pairs={{0,32},{32,0},{1,33},{33,1},{2,34},{34,2},{3,35},{35,3},{4,36},{36... | collective-permute-start | bytes 393224 | tf_op jit(solution)/shard_map/ppermute | solution.py:391
  94.9 2.3 %collective-permute-start.23 = (bf16[528,256]{1,0:T(8,128)(2,1)S(1)}, bf16[528,256]{1,0:T(8,128)(2,1)S(1)}, u32[]{:S(2)}, u32[]{:S(2)}) collective-permute-start(bf16[528,256]{1,0:T(8,128)(2,1)S(1)} %get-tuple-element.28), channel_id=1, source_target_pairs={{0,32},{32,0},{1,33},{33,1},{2,34},{34,2},{3,35},{35,3},{4,36},{36... | collective-permute-start | bytes 811016 | tf_op jit(solution)/shard_map/ppermute | solution.py:391
  97.3 7.8 %collective-permute-start.24 = (bf16[528,256]{1,0:T(8,128)(2,1)S(1)}, bf16[528,256]{1,0:T(8,128)(2,1)S(1)}, u32[]{:S(2)}, u32[]{:S(2)}) collective-permute-start(bf16[528,256]{1,0:T(8,128)(2,1)S(1)} %merge.1.a_ref), channel_id=1, source_target_pairs={{0,64},{64,0},{1,65},{65,1},{2,66},{66,2},{3,67},{67,3},{4,68},{68... | collective-permute-start | bytes 811016 | tf_op jit(solution)/shard_map/ppermute | solution.py:393
  105.3 2.4 %collective-permute-start.25 = (bf16[256,512]{1,0:T(8,128)(2,1)S(1)}, bf16[256,512]{1,0:T(8,128)(2,1)S(1)}, u32[]{:S(2)}, u32[]{:S(2)}) collective-permute-start(bf16[256,512]{1,0:T(8,128)(2,1)S(1)} %last.1.mine_ref), channel_id=1, source_target_pairs={{0,32},{32,0},{1,33},{33,1},{2,34},{34,2},{3,35},{35,3},{4,36},{36... | collective-permute-start | bytes 786440 | tf_op jit(solution)/shard_map/ppermute | solution.py:391
